TPU v7x, 32 devices: a whole 2x2x4 slice. The times are simulated.
32 devices in a mesh: groups: 2 (over x), owner: 16 (over z, y, core).
Axes of the slice: x: 2, y: 2, z: 4, core: 2. Of those that a mesh axis runs over, the one named last changes fastest.
Arguments:
- states: bfloat16 [832, 8192], P(('groups', 'owner')), parts along dimension 0, may hold values from -6 to 6
- row_adapter_index: int32 [832], P('groups'), parts along dimension 0, may hold values from 0 to 63, as said below
- adapter_storage_slot: int32 [128], P('groups'), parts along dimension 0, may hold values from 0 to 63, as said below
- base_weight: bfloat16 [8192, 8192], P(None, 'owner'), may hold values from -0.0625 to 0.0625
- down_weight: bfloat16 [64, 8192, 64], P('owner'), may hold values from -0.0625 to 0.0625
- up_weight: bfloat16 [64, 64, 8192], P('owner'), may hold values from -0.75 to 0.75
Outputs:
- layer_out: bfloat16 [832, 8192], P(('groups', 'owner')), parts along dimension 0
There are 2 independent parts, one for each index of `groups`. A program takes and returns all parts, laid end to end along the dimension named above; an argument that names none is the same for every part. Nothing has to cross between parts.
Inputs may be any that keep to these rules, and one draw needn't show every extreme that they name: `adapter_storage_slot`: a permutation of 0 to 63. With owner(r) = adapter_storage_slot[row_adapter_index[r]] // 4, the 26 rows of one row group (aligned blocks) name at most 2 rows of one owner; in every draw some owner gets exactly 2 rows from every row group.
All inputs are finite; a program needn't handle non-finite values.
Results may differ from a plain program's by a relative error of at most 0.0053.
Values may be sent and summed in bfloat16 or wider, within the bound.
No kernel may reach another device: no remote copies, remote signals or barrier semaphores. Data moves between devices by JAX's collectives and lax.ppermute only.
A program may use at most 192 MiB of HBM per device.

v0:
```python
import jax
import jax.numpy as jnp
from jax import lax
from jax.sharding import PartitionSpec as P

OWNER_ROW_LIMIT = 2


adapter_scale = 0.5


def per_device(
    states, row_adapter_index, adapter_storage_slot, base_weight, down_weight, up_weight
):
    owner_count = lax.axis_size("owner")
    my_index = lax.axis_index("owner")
    rows_dev, input_features = states.shape
    all_rows = row_adapter_index.shape[0]
    adapters_per_owner = down_weight.shape[0]
    adapter_rank_width = down_weight.shape[2]
    full_states = lax.all_gather(states, "owner", axis=0, tiled=True)
    base_cols = jnp.dot(full_states, base_weight, preferred_element_type=jnp.float32).astype(
        jnp.bfloat16
    )
    slot_per_row = jnp.take(adapter_storage_slot, row_adapter_index)
    owners = slot_per_row // adapters_per_owner
    source = jnp.arange(all_rows, dtype=jnp.int32) // rows_dev
    member = (owners[:, None] == jnp.arange(owner_count, dtype=jnp.int32)[None, :]).astype(
        jnp.int32
    )
    running = (
        jnp.cumsum(member.reshape(owner_count, rows_dev, owner_count), axis=1).reshape(
            all_rows, owner_count
        )
        - 1
    )
    position = jnp.sum(running * member, axis=1)
    bucket = source * OWNER_ROW_LIMIT + position
    targets = jnp.arange(owner_count * OWNER_ROW_LIMIT, dtype=jnp.int32)
    matched = ((owners == my_index)[:, None] & (bucket[:, None] == targets[None, :])).astype(
        jnp.int32
    )
    row_index = jnp.sum(matched * jnp.arange(all_rows, dtype=jnp.int32)[:, None], axis=0)
    local_slot = jnp.sum(matched * slot_per_row[:, None], axis=0) - my_index * adapters_per_owner
    filled = jnp.sum(matched, axis=0) > 0
    selected_rows = jnp.take(full_states, row_index, axis=0)
    chosen_masks = []
    rank_projection = jnp.zeros((owner_count * OWNER_ROW_LIMIT, adapter_rank_width), jnp.float32)
    for owner_adapter in range(adapters_per_owner):
        chosen = (filled & (local_slot == owner_adapter))[:, None]
        chosen_masks.append(chosen)
        matrix_product = jnp.dot(
            selected_rows, down_weight[owner_adapter], preferred_element_type=jnp.float32
        )
        rank_projection = rank_projection + jnp.where(chosen, matrix_product, 0.0)
    rank_projection = rank_projection.astype(jnp.bfloat16)
    adapter_delta = jnp.zeros((owner_count * OWNER_ROW_LIMIT, input_features), jnp.float32)
    for owner_adapter in range(adapters_per_owner):
        mask_applied = jnp.where(
            chosen_masks[owner_adapter], rank_projection, jnp.zeros_like(rank_projection)
        )
        adapter_delta = adapter_delta + jnp.dot(
            mask_applied, up_weight[owner_adapter], preferred_element_type=jnp.float32
        )
    returned = lax.all_to_all(
        adapter_delta.astype(jnp.bfloat16).reshape(owner_count, OWNER_ROW_LIMIT, input_features),
        "owner",
        split_axis=0,
        concat_axis=0,
        tiled=True,
    )
    my_buckets = lax.dynamic_slice_in_dim(
        owners * OWNER_ROW_LIMIT + position, my_index * rows_dev, rows_dev
    )
    row_deltas = jnp.take(
        returned.reshape(owner_count * OWNER_ROW_LIMIT, input_features), my_buckets, axis=0
    )
    received_rows = lax.all_to_all(base_cols, "owner", split_axis=0, concat_axis=1, tiled=True)
    return (
        received_rows.astype(jnp.float32) + adapter_scale * row_deltas.astype(jnp.float32)
    ).astype(jnp.bfloat16)


def solution(mesh):
    return jax.shard_map(
        per_device,
        mesh=mesh,
        in_specs=(
            P(("groups", "owner"), None),
            P("groups"),
            P("groups"),
            P(None, "owner"),
            P("owner", None, None),
            P("owner", None, None),
        ),
        out_specs=P(("groups", "owner"), None),
        check_vma=False,
    )
```

profile of v0, /device:TPU:0, one launch (start us, length us, event | category | flops | bytes accessed | tf_op | source)
XLA Modules:
  0.0 150.5 jit_solution(7546591204359563648)
XLA Ops:
  6.5 0.7 all-gather.3.cloned.1.call-update
  7.3 1.6 %fusion.53 = (s32[1]{0:T(128)}, s32[1]{0:T(128)}, s32[1]{0:T(128)}, s32[1]{0:T(128)}, s32[1]{0:T(128)}, /*index=5*/s32[1]{0:T(128)}, s32[1]{0:T(128)}) fusion(s32[64]{0:T(128)} %param.8), kind=kLoop, calls=%fused_computation.98 | loop fusion | bytes 56 | tf_op jit(solution)/shard_map/jit(_take)/gather | solution.py:25
  8.8 2.1 %fusion.52 = (s32[1]{0:T(128)}, s32[1]{0:T(128)}, s32[1]{0:T(128)}, s32[1]{0:T(128)}, s32[1]{0:T(128)}, /*index=5*/s32[1]{0:T(128)}, s32[1]{0:T(128)}, s32[1]{0:...) fusion(s32[64]{0:T(128)} %param.8), kind=kLoop, calls=%fused_computation.97 | loop fusion | bytes 152 | tf_op jit(solution)/shard_map/jit(_take)/gather | solution.py:25
  10.9 2.1 %fusion.51 = (s32[1]{0:T(128)}, s32[1]{0:T(128)}, s32[1]{0:T(128)}, s32[1]{0:T(128)}, s32[1]{0:T(128)}, /*index=5*/s32[1]{0:T(128)}, s32[1]{0:T(128)}, s32[1]{0:...) fusion(s32[64]{0:T(128)} %param.8), kind=kLoop, calls=%fused_computation.96 | loop fusion | bytes 152 | tf_op jit(solution)/shard_map/jit(_take)/gather | solution.py:25
  13.0 2.1 %fusion.50 = (s32[1]{0:T(128)}, s32[1]{0:T(128)}, s32[1]{0:T(128)}, s32[1]{0:T(128)}, s32[1]{0:T(128)}, /*index=5*/s32[1]{0:T(128)}, s32[1]{0:T(128)}, s32[1]{0:...) fusion(s32[64]{0:T(128)} %param.8), kind=kLoop, calls=%fused_computation.95 | loop fusion | bytes 152 | tf_op jit(solution)/shard_map/jit(_take)/gather | solution.py:25
  15.1 40.6 %broadcast_compare_fusion = (pred[416]{0:T(512)(128)(4,1)S(1)}, s32[416]{0:T(512)S(1)}, s32[416]{0:T(512)S(1)}) fusion(s32[]{:T(128)S(6)} %axis_index.12, s32[]{:T(128)} %bitcast.65, s32[]{:T(128)} %bitcast.64, s32[]{:T(128)} %bitcast.63, s32[]{:T(128)} %bitcast.62, s32[]{:T(128)} %bitcast.61, s32[]{:T(128)} %bitcast.60, s32[]{:T(128)} %bitcast.59, ...), kind=kLoop, calls=%fused_computation.87 | loop fusion | flops 61984 | bytes 5668 | tf_op jit(solution)/shard_map/eq | solution.py:40
  55.9 0.6 fusion.54
  57.0 30.2 %all-gather.3.cloned.1.call-done = bf16[16,26,8192]{2,1,0:T(8,128)(2,1)} async-done(((bf16[1,26,8192]{2,1,0:T(8,128)(2,1)}), bf16[16,26,8192]{2,1,0:T(8,128)(2,1)}) %all-gather.3.cloned.1.call-update) | async-done | bytes 6815760 | tf_op jit(solution)/shard_map/all_gather | solution.py:21
  87.2 7.4 %reshape.220 = bf16[416,8192]{1,0:T(8,128)(2,1)} reshape(bf16[16,26,8192]{2,1,0:T(8,128)(2,1)} %all-gather.3.cloned.1.call-done) | data formatting | bytes 13631488
  94.6 9.0 %convolution_convert_fusion = bf16[416,512]{1,0:T(8,128)(2,1)S(1)} fusion(bf16[416,8192]{1,0:T(8,128)(2,1)} %reshape.220, bf16[8192,512]{1,0:T(8,128)(2,1)} %param.9), kind=kOutput, calls=%fused_computation.6 | convolution fusion | flops 3489873920 | bytes 15630336 | tf_op jit(solution)/shard_map/dot_general | solution.py:22
  103.6 0.9 all_to_all.13
  104.5 3.6 %all-to-all-start = ((bf16[16,26,512]{2,1,0:T(8,128)(2,1)}), bf16[16,26,512]{2,1,0:T(8,128)(2,1)S(1)}, u32[]{:S(2)}, u32[]{:S(2)}) async-start(bf16[16,26,512]{2,1,0:T(8,128)(2,1)} %all_to_all.13), calls=%async_computation | async-start | bytes 1048576 | tf_op jit(solution)/shard_map/all_to_all | solution.py:78
  108.1 5.2 %gather_fusion = bf16[32,8192]{1,0:T(8,128)(2,1)S(1)} fusion(bf16[416,8192]{1,0:T(8,128)(2,1)} %reshape.220, s32[1024]{0:T(1024)S(1)} %pad_clamp_fusion.1), kind=kCustom, calls=%fused_computation | custom fusion | bytes 1048704 | tf_op jit(solution)/shard_map/jit(_take)/gather | solution.py:46
  113.3 1.8 %convolution_select_fusion = f32[32,64]{1,0:T(8,128)S(1)} fusion(bf16[4,8192,64]{1,2,0:T(8,128)(2,1)} %param.10, pred[32]{0:T(512)(128)(4,1)S(1)} %get-tuple-element.19, bf16[32,8192]{1,0:T(8,128)(2,1)S(1)} %gather_fusion, pred[32]{0:T(512)(128)(4,1)S(1)} %get-tuple-element.84), kind=kOutput, calls=%fused_computation.9 | convolution fusion | flops 33818624 | bytes 1581120 | tf_op jit(solution)/shard_map/dot_general | solution.py:52
  115.1 2.4 %convolution_select_fusion.1 = f32[32,64]{1,0:T(8,128)S(1)} fusion(bf16[4,8192,64]{1,2,0:T(8,128)(2,1)} %param.10, pred[32]{0:T(512)(128)(4,1)S(1)} %get-tuple-element.18, bf16[32,8192]{1,0:T(8,128)(2,1)S(1)} %gather_fusion, pred[32]{0:T(512)(128)(4,1)S(1)} %get-tuple-element.84), kind=kOutput, calls=%fused_computation.10 | convolution fusion | flops 33818624 | bytes 1581120 | tf_op jit(solution)/shard_map/dot_general | solution.py:52
  118.0 0.5 fusion.5
  120.0 1.1 reshape.127
  121.2 1.3 all-to-all-done
  122.5 4.7 %all-to-all-start.1 = ((bf16[16,2,8192]{2,1,0:T(2,128)(2,1)}), bf16[16,2,8192]{2,1,0:T(2,128)(2,1)S(1)}, u32[]{:S(2)}, u32[]{:S(2)}) async-start(bf16[16,2,8192]{2,1,0:T(2,128)(2,1)} %reshape.127), calls=%async_computation.1 | async-start | bytes 1048576 | tf_op jit(solution)/shard_map/all_to_all | solution.py:65
  127.4 0.5 copy.15
  128.0 0.6 copy.18
  128.6 13.0 %all-to-all-done.1 = bf16[16,2,8192]{2,1,0:T(2,128)(2,1)S(1)} async-done(((bf16[16,2,8192]{2,1,0:T(2,128)(2,1)}), bf16[16,2,8192]{2,1,0:T(2,128)(2,1)S(1)}, u32[]{:S(2)}, u32[]{:S(2)}) %all-to-all-start.1) | async-done | bytes 524320 | tf_op jit(solution)/shard_map/all_to_all | solution.py:65
  141.8 0.8 gather_fusion.1
  142.6 1.0 add_convert_fusion
  (25 shorter events, 3.0 us)
Async XLA Ops:
  6.5 80.6 %all-gather.3.cloned.1.call-start = ((), (), s32[]{:S(2)}) async-start(), calls=%async_computation.2 | async-start | bytes 8912896 | tf_op jit(solution)/shard_map/all_gather | solution.py:21
  104.5 18.0 %all-to-all-start = ((bf16[16,26,512]{2,1,0:T(8,128)(2,1)}), bf16[16,26,512]{2,1,0:T(8,128)(2,1)S(1)}, u32[]{:S(2)}, u32[]{:S(2)}) async-start(bf16[16,26,512]{2,1,0:T(8,128)(2,1)} %all_to_all.13), calls=%async_computation | async-start | bytes 1048576 | tf_op jit(solution)/shard_map/all_to_all | solution.py:78
  113.2 4.3 %copy-start.1 = (bf16[4,8192,64]{1,2,0:T(8,128)(2,1)S(1)}, bf16[4,8192,64]{1,2,0:T(8,128)(2,1)}, u32[]{:S(2)}) copy-start(bf16[4,8192,64]{1,2,0:T(8,128)(2,1)} %param.10) | copy-start | bytes 12582916
  113.2 5.3 %copy-start = (bf16[4,64,8192]{2,1,0:T(8,128)(2,1)S(1)}, bf16[4,64,8192]{2,1,0:T(8,128)(2,1)}, u32[]{:S(2)}) copy-start(bf16[4,64,8192]{2,1,0:T(8,128)(2,1)} %param.11) | copy-start | bytes 12582916
  122.5 19.1 %all-to-all-start.1 = ((bf16[16,2,8192]{2,1,0:T(2,128)(2,1)}), bf16[16,2,8192]{2,1,0:T(2,128)(2,1)S(1)}, u32[]{:S(2)}, u32[]{:S(2)}) async-start(bf16[16,2,8192]{2,1,0:T(2,128)(2,1)} %reshape.127), calls=%async_computation.1 | async-start | bytes 1048576 | tf_op jit(solution)/shard_map/all_to_all | solution.py:65
Sparse Core Ops, SparseCore 0:
  9.5 77.6 all-gather.2
where the time goes:
time: 152 us; the launch traced here: 151 us
  waiting for transfers between devices  45.2 us (30%)
  other arithmetic  42.7 us (28%)
  local copies, waits for them, and re-layouts  25 us (16%)
  matrix products  15.7 us (10%)
  between operations  13.6 us (9%)
  starting transfers between devices  8.23 us (5%)
    eq x1, other arithmetic, per_device(): owners == my_index  40.6 us
    all_gather x1, waiting for transfers between devices, per_device(): full_states = lax.all_gather(states, 'owner', axis=0, tiled=True)  30.2 us
    all_to_all x1, waiting for transfers between devices, per_device(): lax.all_to_all(adapter_delta.astype(jnp.bfloat16).reshape(owner_count, OW...  13 us
    dot_general x1, matrix products, per_device(): jnp.dot(full_states, base_weight, preferred_element_type=jnp.float32)  8.99 us
    unnamed x7, local copies, waits for them, and re-layouts  8.16 us
    gather x4, local copies, waits for them, and re-layouts, per_device(): slot_per_row = jnp.take(adapter_storage_slot, row_adapter_index)  7.82 us
    dot_general x4, matrix products, per_device(): jnp.dot(selected_rows, down_weight[owner_adapter], preferred_element_type...  5.29 us
    gather x1, local copies, waits for them, and re-layouts, per_device(): selected_rows = jnp.take(full_states, row_index, axis=0)  5.16 us
  transfers between devices with their start and end apart: 3, of which 3 were waited for; matrix products, arithmetic and copies ran while one was open for 43% of the time, Pallas kernels for 0%

commit v1 on v0

v1 whole, which is shorter than its diff:
```python
import functools

import jax
import jax.numpy as jnp
import numpy as np
from jax import lax
from jax.experimental import pallas as pl
from jax.experimental.pallas import tpu as pltpu
from jax.sharding import PartitionSpec as P

OWNER_ROW_LIMIT = 2
ROW_PAD = 16
adapter_scale = 0.5

VMEM = pl.BlockSpec(memory_space=pltpu.VMEM)
SMEM = pl.BlockSpec(memory_space=pltpu.SMEM)
ANY = pl.BlockSpec(memory_space=pl.ANY)
MIB = 1 << 20


def ring_order(chips):
    return list(range(0, chips, 2)) + list(range(1, chips, 2))[::-1]


def ring_tables(owner_count):
    chips = owner_count // 2
    order = ring_order(chips)
    place = {chip: at for at, chip in enumerate(order)}

    def beside(chip, core, hops):
        return order[(place[chip] + (-hops if core == 0 else hops)) % chips]

    step = [
        (2 * chip + core, 2 * order[(place[chip] + (1 if core == 0 else -1)) % chips] + core)
        for chip in range(chips)
        for core in range(2)
    ]
    swap = [(device, device ^ 1) for device in range(owner_count)]
    sources = np.zeros((owner_count, owner_count), np.int32)
    for device in range(owner_count):
        chip, core = divmod(device, 2)
        row = [device, device ^ 1]
        for hops in range(1, chips // 2 + 1):
            mine, mates = beside(chip, core, hops), beside(chip, 1 - core, hops)
            row += [2 * mine + core, 2 * mates + 1 - core]
            if 2 * hops < chips:
                row += [2 * mine + 1 - core, 2 * mates + core]
        assert sorted(row) == list(range(owner_count))
        sources[device] = row
    return step, swap, sources


def pair_rows(x):
    rows, width = x.shape

    def kernel(x_ref, o_ref):
        o_ref[...] = x_ref[...].reshape(rows // 2, 2, width)

    return pl.pallas_call(
        kernel,
        out_shape=jax.ShapeDtypeStruct((rows // 2, 2, width), x.dtype),
        in_specs=[VMEM],
        out_specs=VMEM,
        compiler_params=pltpu.CompilerParams(vmem_limit_bytes=4 * MIB),
        name="pair_rows",
    )(x)


def hold(*weights):
    def kernel(*refs):
        n = len(weights)
        sem = refs[2 * n]
        copies = [
            pltpu.make_async_copy(refs[i], refs[n + i], sem.at[i]) for i in range(n)
        ]
        for copy in copies:
            copy.start()
        for copy in copies:
            copy.wait()

    return pl.pallas_call(
        kernel,
        out_shape=[pltpu.VMEM(w.shape, w.dtype) for w in weights],
        in_specs=[ANY] * len(weights),
        out_specs=[VMEM] * len(weights),
        scratch_shapes=[pltpu.SemaphoreType.DMA((len(weights),))],
        compiler_params=pltpu.CompilerParams(vmem_limit_bytes=1 * MIB),
        name="hold",
    )(*weights)


def block_products(sources, code, blocks, base_weight, down, up, rank, owner_count):
    count = len(blocks)
    pairs, _, width = blocks[0].shape
    rows = 2 * pairs
    padded = -(-rows // ROW_PAD) * ROW_PAD
    columns = base_weight.shape[1]
    ranks = down.shape[0]
    depth = min(width, 1024)

    def kernel(src_ref, code_ref, *refs):
        block_refs = refs[:count]
        w_ref, d_ref, u_ref, out_ref, x_ref = refs[count:]
        for b in range(count):
            x_ref[padded * b : padded * b + rows] = block_refs[b][...].reshape(rows, width)
            x_ref[padded * b + rows : padded * (b + 1)] = jnp.zeros(
                (padded - rows, width), x_ref.dtype
            )
        low = jnp.zeros((padded * count, ranks), jnp.float32)
        for at in range(0, width, depth):
            low += lax.dot_general(
                x_ref[:, at : at + depth],
                d_ref[:, at : at + depth],
                (((1,), (1,)), ((), ())),
                preferred_element_type=jnp.float32,
            )
        low = low.astype(jnp.bfloat16).astype(jnp.float32)
        adapter = lax.broadcasted_iota(jnp.int32, (padded, ranks), 1) // rank
        chosen = []
        for b in range(count):
            row_code = code_ref[src_ref[b]]
            for q in range(OWNER_ROW_LIMIT):
                mask = row_code == OWNER_ROW_LIMIT * adapter + q
                chosen.append(
                    jnp.sum(
                        jnp.where(mask, low[padded * b : padded * (b + 1)], 0.0),
                        axis=0,
                        keepdims=True,
                    )
                )
        chosen = jnp.concatenate(chosen, axis=0).astype(jnp.bfloat16)
        base = jnp.zeros((padded * count, columns), jnp.float32)
        for at in range(0, width, depth):
            base += jnp.dot(
                x_ref[:, at : at + depth],
                w_ref[at : at + depth, :],
                preferred_element_type=jnp.float32,
            )
        for b in range(count):
            out_ref[b, :pairs] = (
                base[padded * b : padded * b + rows]
                .astype(jnp.bfloat16)
                .reshape(pairs, 2, columns)
            )
        for k in range(owner_count):
            delta = jnp.dot(
                chosen, u_ref[:, columns * k : columns * (k + 1)], preferred_element_type=jnp.float32
            ).astype(jnp.bfloat16)
            for b in range(count):
                out_ref[b, pairs + k] = delta[OWNER_ROW_LIMIT * b : OWNER_ROW_LIMIT * (b + 1)]

    return pl.pallas_call(
        kernel,
        out_shape=jax.ShapeDtypeStruct((count, pairs + owner_count, 2, columns), jnp.bfloat16),
        in_specs=[SMEM, VMEM] + [VMEM] * (count + 3),
        out_specs=VMEM,
        scratch_shapes=[pltpu.VMEM((padded * count, width), jnp.bfloat16)],
        compiler_params=pltpu.CompilerParams(vmem_limit_bytes=16 * MIB),
        cost_estimate=pl.CostEstimate(
            flops=2 * padded * count * width * (columns + ranks),
            bytes_accessed=width * (columns + 2 * ranks) * 2,
            transcendentals=0,
        ),
        name="block_products",
    )(sources, code, *blocks, base_weight, down, up)


def pack(sources, pieces, owner_count):
    counts = [p.shape[0] for p in pieces]

    def kernel(src_ref, *refs):
        piece_refs, out_ref, sem = refs[: len(pieces)], refs[-2], refs[-1]
        copies = []
        at = 0
        for ref, count in zip(piece_refs, counts):
            for b in range(count):
                copies.append(
                    pltpu.make_async_copy(ref.at[b], out_ref.at[src_ref[at]], sem.at[at])
                )
                at += 1
        for copy in copies:
            copy.start()
        for copy in copies:
            copy.wait()

    return pl.pallas_call(
        kernel,
        out_shape=jax.ShapeDtypeStruct((owner_count,) + pieces[0].shape[1:], pieces[0].dtype),
        in_specs=[SMEM] + [ANY] * len(pieces),
        out_specs=ANY,
        scratch_shapes=[pltpu.SemaphoreType.DMA((owner_count,))],
        compiler_params=pltpu.CompilerParams(vmem_limit_bytes=1 * MIB),
        name="pack",
    )(sources, *pieces)


def assemble(key, received, rows):
    owner_count, _, _, columns = received.shape
    pairs = rows // 2
    slots = OWNER_ROW_LIMIT * owner_count

    def kernel(key_ref, r_ref, o_ref):
        pick = (
            key_ref[...] == lax.broadcasted_iota(jnp.int32, (rows, slots), 1)
        ).astype(jnp.bfloat16)
        for k in range(owner_count):
            delta = jnp.dot(
                pick,
                r_ref[:, pairs + k].reshape(slots, columns),
                preferred_element_type=jnp.float32,
            )
            base = r_ref[k, :pairs].reshape(rows, columns).astype(jnp.float32)
            o_ref[:, columns * k : columns * (k + 1)] = (base + adapter_scale * delta).astype(
                o_ref.dtype
            )

    return pl.pallas_call(
        kernel,
        out_shape=jax.ShapeDtypeStruct((rows, owner_count * columns), jnp.bfloat16),
        in_specs=[VMEM, VMEM],
        out_specs=VMEM,
        compiler_params=pltpu.CompilerParams(vmem_limit_bytes=16 * MIB),
        name="assemble",
    )(key, received)


def per_device(
    states, row_adapter_index, adapter_storage_slot, base_weight, down_weight, up_weight
):
    owner_count = lax.axis_size("owner")
    me = lax.axis_index("owner")
    rows, width = states.shape
    adapters, rank = down_weight.shape[0], down_weight.shape[2]
    padded = -(-rows // ROW_PAD) * ROW_PAD
    step, swap, sources = ring_tables(owner_count)
    send = functools.partial(lax.ppermute, axis_name="owner")

    down = down_weight.transpose(0, 2, 1).reshape(adapters * rank, width)
    up = up_weight.reshape(adapters * rank, width)
    held = hold(base_weight, down, up)

    index = row_adapter_index.reshape(owner_count, rows)
    total = adapter_storage_slot.shape[0]
    slot = jnp.sum(
        jnp.where(
            index[:, :, None] == jnp.arange(total, dtype=jnp.int32),
            adapter_storage_slot,
            0,
        ),
        axis=2,
    )
    owner = slot // adapters
    earlier = jnp.arange(rows)[None, :] < jnp.arange(rows)[:, None]
    position = jnp.sum(
        ((owner[:, :, None] == owner[:, None, :]) & earlier).astype(jnp.int32), axis=2
    )
    code = jnp.where(owner == me, (slot - owner * adapters) * OWNER_ROW_LIMIT + position, -1)
    code = jnp.pad(code, ((0, 0), (0, padded - rows)), constant_values=-1)[:, :, None]
    key = lax.dynamic_index_in_dim(owner * OWNER_ROW_LIMIT + position, me, 0, False)[:, None]
    mine = lax.dynamic_index_in_dim(jnp.asarray(sources), me, 0, False)

    own = pair_rows(states)
    mate = send(own, perm=swap)
    groups = [[own, mate]]
    first, second = own, mate
    chips = owner_count // 2
    for hops in range(1, chips // 2 + 1):
        first = send(first, perm=step)
        group = [first, send(first, perm=swap)]
        if 2 * hops < chips:
            second = send(second, perm=step)
            group += [second, send(second, perm=swap)]
        groups.append(group)
    pieces = []
    at = 0
    for group in groups:
        pieces.append(
            block_products(
                mine[at : at + len(group)], code, group, *held, rank, owner_count
            )
        )
        at += len(group)
    packed = pack(mine, pieces, owner_count)
    received = lax.all_to_all(packed, "owner", split_axis=0, concat_axis=0, tiled=True)
    return assemble(key, received, rows)


def solution(mesh):
    return jax.shard_map(
        per_device,
        mesh=mesh,
        in_specs=(
            P(("groups", "owner"), None),
            P("groups"),
            P("groups"),
            P(None, "owner"),
            P("owner", None, None),
            P("owner", None, None),
        ),
        out_specs=P(("groups", "owner"), None),
        check_vma=False,
    )
```

time: 152 us -> 102 us (0.67)
  other arithmetic: 42.7 us -> 1.98 us
  Pallas kernels: 0 us -> 25.8 us
  matrix products: 15.7 us -> 0 us
  starting transfers between devices: 8.23 us -> 23.4 us
  between operations: 13.6 us -> 0.16 us
  local copies, waits for them, and re-layouts: 25 us -> 11.7 us
  waiting for transfers between devices: 45.2 us -> 37.2 us
    eq x1 -> x0, other arithmetic: 40.6 us -> none  [per_device(): owners == my_index]
    all_gather x1 -> x0, waiting for transfers between devices: 30.2 us -> none  [per_device(): full_states = lax.all_gather(states, 'owner', axis=0, tiled=True)]
    pallas_call x0 -> x9, Pallas kernels: none -> 25.8 us  [the longest x5 21.5 us: block_products(): pl.pallas_call(kernel, out_shape=jax.ShapeDtypeStruct((count, pairs + own...]
    ppermute x0 -> x15, starting transfers between devices: none -> 17 us  [the longest x4 8.87 us: per_device(): first = send(first, perm=step)]
    ppermute x0 -> x15, waiting for transfers between devices: none -> 16 us  [the longest x4 14.3 us: per_device(): first = send(first, perm=step)]
    dot_general x9 -> x0, matrix products: 15.7 us -> none  [the longest x1 8.99 us: per_device(): jnp.dot(full_states, base_weight, preferred_element_type=jnp.float32)]
    gather x6 -> x0, local copies, waits for them, and re-layouts: 13.8 us -> none  [the longest x4 7.82 us: per_device(): slot_per_row = jnp.take(adapter_storage_slot, row_adapter_index)]
    all_to_all x2 -> x1, waiting for transfers between devices: 14.3 us -> 21.3 us  [per_device(): lax.all_to_all(packed, 'owner', split_axis=0, concat_axis=0, tiled=True)]
  transfers between devices with their start and end apart: 3 -> 16, of which waited for: 3 -> 7; matrix products, arithmetic and copies ran while one was open for 43% -> 4% of each run, Pallas kernels for 0% -> 19%
where the time goes in v1:
time: 102 us; the launch traced here: 100 us
  waiting for transfers between devices  37.2 us (36%)
  Pallas kernels  25.8 us (25%)
  starting transfers between devices  23.4 us (23%)
  local copies, waits for them, and re-layouts  11.7 us (11%)
  other arithmetic  1.98 us (2%)
    pallas_call x5, Pallas kernels, block_products(): pl.pallas_call(kernel, out_shape=jax.ShapeDtypeStruct((count, pairs + own...  21.5 us
    all_to_all x1, waiting for transfers between devices, per_device(): lax.all_to_all(packed, 'owner', split_axis=0, concat_axis=0, tiled=True)  21.3 us
    ppermute x4, waiting for transfers between devices, per_device(): first = send(first, perm=step)  14.3 us
    unnamed x12, local copies, waits for them, and re-layouts  9.55 us
    ppermute x4, starting transfers between devices, per_device(): first = send(first, perm=step)  8.87 us
    all_to_all x1, starting transfers between devices, per_device(): lax.all_to_all(packed, 'owner', split_axis=0, concat_axis=0, tiled=True)  6.49 us
    ppermute x3, starting transfers between devices, per_device(): second = send(second, perm=step)  5.77 us
  transfers between devices with their start and end apart: 16, of which 7 were waited for; matrix products, arithmetic and copies ran while one was open for 4% of the time, Pallas kernels for 19%

profile of v1, /device:TPU:0, one launch (start us, length us, event | category | flops | bytes accessed | tf_op | source)
XLA Modules:
  0.0 100.3 jit_solution(14164433197570095534)
XLA Ops:
  1.6 2.6 %collective-permute-start.1 = (bf16[13,2,8192]{2,1,0:T(2,128)(2,1)S(1)}, bf16[13,2,8192]{2,1,0:T(2,128)(2,1)S(1)}, u32[]{:S(2)}, u32[]{:S(2)}) collective-permute-start(bf16[13,2,8192]{2,1,0:T(2,128)(2,1)S(1)} %pair_rows.1.refs_0_), channel_id=1, source_target_pairs={{0,4},{1,3},{2,0},{3,7},{4,8},{5,1},{6,2},{7,11},{8,12},{9,5},{10,... | collective-permute-start | bytes 1277960 | tf_op jit(solution)/shard_map/ppermute | solution.py:268
  5.1 1.6 %collective-permute-start.3 = (bf16[13,2,8192]{2,1,0:T(2,128)(2,1)S(1)}, bf16[13,2,8192]{2,1,0:T(2,128)(2,1)S(1)}, u32[]{:S(2)}, u32[]{:S(2)}) collective-permute-start(bf16[13,2,8192]{2,1,0:T(2,128)(2,1)S(1)} %collective-permute-done.refs_1_), channel_id=1, source_target_pairs={{0,4},{1,3},{2,0},{3,7},{4,8},{5,1},{6,2},{7,11},{8,12},{9,5},{10,... | collective-permute-start | bytes 1277960 | tf_op jit(solution)/shard_map/ppermute | solution.py:271
  6.7 3.6 %collective-permute-done.1.refs_0_ = bf16[13,2,8192]{2,1,0:T(2,128)(2,1)S(1)} collective-permute-done((bf16[13,2,8192]{2,1,0:T(2,128)(2,1)S(1)}, bf16[13,2,8192]{2,1,0:T(2,128)(2,1)S(1)}, u32[]{:S(2)}, u32[]{:S(2)}) %collective-permute-start.1) | collective-permute-done | bytes 426016 | tf_op jit(solution)/shard_map/ppermute | solution.py:268
  10.3 2.1 %collective-permute-start.5 = (bf16[13,2,8192]{2,1,0:T(2,128)(2,1)S(1)}, bf16[13,2,8192]{2,1,0:T(2,128)(2,1)S(1)}, u32[]{:S(2)}, u32[]{:S(2)}) collective-permute-start(bf16[13,2,8192]{2,1,0:T(2,128)(2,1)S(1)} %collective-permute-done.1.refs_0_), channel_id=1, source_target_pairs={{0,4},{1,3},{2,0},{3,7},{4,8},{5,1},{6,2},{7,11},{8,12},{9,5},{10,... | collective-permute-start | bytes 1277960 | tf_op jit(solution)/shard_map/ppermute | solution.py:268
  14.9 2.1 %collective-permute-start.7 = (bf16[13,2,8192]{2,1,0:T(2,128)(2,1)S(1)}, bf16[13,2,8192]{2,1,0:T(2,128)(2,1)S(1)}, u32[]{:S(2)}, u32[]{:S(2)}) collective-permute-start(bf16[13,2,8192]{2,1,0:T(2,128)(2,1)S(1)} %collective-permute-done.3.refs_2_), channel_id=1, source_target_pairs={{0,4},{1,3},{2,0},{3,7},{4,8},{5,1},{6,2},{7,11},{8,12},{9,5},{10,... | collective-permute-start | bytes 1277960 | tf_op jit(solution)/shard_map/ppermute | solution.py:271
  16.9 2.5 %collective-permute-done.5.refs_0_ = bf16[13,2,8192]{2,1,0:T(2,128)(2,1)S(1)} collective-permute-done((bf16[13,2,8192]{2,1,0:T(2,128)(2,1)S(1)}, bf16[13,2,8192]{2,1,0:T(2,128)(2,1)S(1)}, u32[]{:S(2)}, u32[]{:S(2)}) %collective-permute-start.5) | collective-permute-done | bytes 426016 | tf_op jit(solution)/shard_map/ppermute | solution.py:268
  19.4 2.1 %collective-permute-start.9 = (bf16[13,2,8192]{2,1,0:T(2,128)(2,1)S(1)}, bf16[13,2,8192]{2,1,0:T(2,128)(2,1)S(1)}, u32[]{:S(2)}, u32[]{:S(2)}) collective-permute-start(bf16[13,2,8192]{2,1,0:T(2,128)(2,1)S(1)} %collective-permute-done.5.refs_0_), channel_id=1, source_target_pairs={{0,4},{1,3},{2,0},{3,7},{4,8},{5,1},{6,2},{7,11},{8,12},{9,5},{10,... | collective-permute-start | bytes 1277960 | tf_op jit(solution)/shard_map/ppermute | solution.py:268
  24.0 2.1 %collective-permute-start.11 = (bf16[13,2,8192]{2,1,0:T(2,128)(2,1)S(1)}, bf16[13,2,8192]{2,1,0:T(2,128)(2,1)}, u32[]{:S(2)}, u32[]{:S(2)}) collective-permute-start(bf16[13,2,8192]{2,1,0:T(2,128)(2,1)S(1)} %collective-permute-done.7.refs_2_), channel_id=1, source_target_pairs={{0,4},{1,3},{2,0},{3,7},{4,8},{5,1},{6,2},{7,11},{8,12},{9,5},{10,... | collective-permute-start | bytes 1277960 | tf_op jit(solution)/shard_map/ppermute | solution.py:271
  26.1 2.5 %collective-permute-done.9.refs_0_ = bf16[13,2,8192]{2,1,0:T(2,128)(2,1)S(1)} collective-permute-done((bf16[13,2,8192]{2,1,0:T(2,128)(2,1)S(1)}, bf16[13,2,8192]{2,1,0:T(2,128)(2,1)S(1)}, u32[]{:S(2)}, u32[]{:S(2)}) %collective-permute-start.9) | collective-permute-done | bytes 426016 | tf_op jit(solution)/shard_map/ppermute | solution.py:268
  28.6 2.1 %collective-permute-start.13 = (bf16[13,2,8192]{2,1,0:T(2,128)(2,1)S(1)}, bf16[13,2,8192]{2,1,0:T(2,128)(2,1)}, u32[]{:S(2)}, u32[]{:S(2)}) collective-permute-start(bf16[13,2,8192]{2,1,0:T(2,128)(2,1)S(1)} %collective-permute-done.9.refs_0_), channel_id=1, source_target_pairs={{0,4},{1,3},{2,0},{3,7},{4,8},{5,1},{6,2},{7,11},{8,12},{9,5},{10,... | collective-permute-start | bytes 1277960 | tf_op jit(solution)/shard_map/ppermute | solution.py:268
  32.1 5.7 %collective-permute-done.13.refs_0_ = bf16[13,2,8192]{2,1,0:T(2,128)(2,1)} collective-permute-done((bf16[13,2,8192]{2,1,0:T(2,128)(2,1)S(1)}, bf16[13,2,8192]{2,1,0:T(2,128)(2,1)}, u32[]{:S(2)}, u32[]{:S(2)}) %collective-permute-start.13) | collective-permute-done | bytes 426016 | tf_op jit(solution)/shard_map/ppermute | solution.py:268
  38.2 3.4 %copy-done = bf16[8192,512]{1,0:T(8,128)(2,1)S(1)} copy-done((bf16[8192,512]{1,0:T(8,128)(2,1)S(1)}, bf16[8192,512]{1,0:T(8,128)(2,1)}, u32[]{:S(2)}) %copy-start) | copy-done | bytes 8388632
  41.5 2.2 %copy-done.1 = bf16[4,8192,64]{1,2,0:T(8,128)(2,1)S(1)} copy-done((bf16[4,8192,64]{1,2,0:T(8,128)(2,1)S(1)}, bf16[4,8192,64]{1,2,0:T(8,128)(2,1)}, u32[]{:S(2)}) %copy-start.1) | copy-done | bytes 4194328
  43.7 2.2 %copy-done.2 = bf16[4,64,8192]{2,1,0:T(8,128)(2,1)S(1)} copy-done((bf16[4,64,8192]{2,1,0:T(8,128)(2,1)S(1)}, bf16[4,64,8192]{2,1,0:T(8,128)(2,1)}, u32[]{:S(2)}) %copy-start.2) | copy-done | bytes 4194328
  45.9 1.3 %hold.1 = (bf16[8192,512]{1,0:T(8,128)(2,1)S(1)}, bf16[256,8192]{1,0:T(8,128)(2,1)S(1)}, bf16[256,8192]{1,0:T(8,128)(2,1)S(1)}) custom-call(bf16[8192,512]{1,0:T(8,128)(2,1)S(1)} %copy-done, bf16[256,8192]{1,0:T(8,128)(2,1)S(1)} %bitcast.20, bf16[256,8192]{1,0:T(8,128)(2,1)S(1)} %bitcast.21), custom_call_target="tpu_custom_call" | custom-call | tf_op jit(solution)/shard_map/hold/pallas_call | solution.py:81
  47.9 4.0 %block_products.5.refs_0_ = bf16[2,29,2,512]{3,2,1,0:T(2,128)(2,1)S(1)} custom-call(s32[2]{0:T(128)S(1)} %get-tuple-element.14.src_ref, s32[16,32,1]{2,1,0:T(8,128)S(1)} %copy.26.code_ref, bf16[13,2,8192]{2,1,0:T(2,128)(2,1)S(1)} %pair_rows.1.refs_0_, bf16[13,2,8192]{2,1,0:T(2,128)(2,1)S(1)} %collective-permute-done.refs_1_, ...), custom_call_target="tpu_custom_call" | custom-call | flops 805306368 | bytes 16777216 | tf_op jit(solution)/shard_map/block_products/pallas_call | solution.py:152
  51.9 4.3 %block_products.6.refs_1_ = bf16[4,29,2,512]{3,2,1,0:T(2,128)(2,1)S(1)} custom-call(s32[4]{0:T(128)S(1)} %get-tuple-element.17.src_ref, s32[16,32,1]{2,1,0:T(8,128)S(1)} %copy.26.code_ref, bf16[13,2,8192]{2,1,0:T(2,128)(2,1)S(1)} %collective-permute-done.1.refs_0_, bf16[13,2,8192]{2,1,0:T(2,128)(2,1)S(1)} %copy-done.5, ...), custom_call_target="tpu_custom_call" | custom-call | flops 1610612736 | bytes 16777216 | tf_op jit(solution)/shard_map/block_products/pallas_call | solution.py:152
  56.2 4.4 %block_products.7.refs_2_ = bf16[4,29,2,512]{3,2,1,0:T(2,128)(2,1)S(1)} custom-call(s32[4]{0:T(128)S(1)} %get-tuple-element.16.src_ref, s32[16,32,1]{2,1,0:T(8,128)S(1)} %copy.26.code_ref, bf16[13,2,8192]{2,1,0:T(2,128)(2,1)S(1)} %collective-permute-done.5.refs_0_, bf16[13,2,8192]{2,1,0:T(2,128)(2,1)} %collective-permute-done.6.refs_1_, ...), custom_call_target="tpu_custom_call" | custom-call | flops 1610612736 | bytes 16777216 | tf_op jit(solution)/shard_map/block_products/pallas_call | solution.py:152
  60.6 4.6 %block_products.9.refs_4_ = bf16[2,29,2,512]{3,2,1,0:T(2,128)(2,1)S(1)} custom-call(s32[2]{0:T(128)S(1)} %get-tuple-element.13.src_ref, s32[16,32,1]{2,1,0:T(8,128)S(1)} %copy.26.code_ref, bf16[13,2,8192]{2,1,0:T(2,128)(2,1)} %collective-permute-done.13.refs_0_, bf16[13,2,8192]{2,1,0:T(2,128)(2,1)} %collective-permute-done.14.refs_1_, ...), custom_call_target="tpu_custom_call" | custom-call | flops 805306368 | bytes 16777216 | tf_op jit(solution)/shard_map/block_products/pallas_call | solution.py:152
  65.2 4.3 %block_products.8.refs_3_ = bf16[4,29,2,512]{3,2,1,0:T(2,128)(2,1)S(1)} custom-call(s32[4]{0:T(128)S(1)} %get-tuple-element.15.src_ref, s32[16,32,1]{2,1,0:T(8,128)S(1)} %copy.26.code_ref, bf16[13,2,8192]{2,1,0:T(2,128)(2,1)S(1)} %collective-permute-done.9.refs_0_, bf16[13,2,8192]{2,1,0:T(2,128)(2,1)S(1)} %collective-permute-done.10.refs_1_, ...), custom_call_target="tpu_custom_call" | custom-call | flops 1610612736 | bytes 16777216 | tf_op jit(solution)/shard_map/block_products/pallas_call | solution.py:152
  69.5 1.6 %pack.1 = bf16[16,29,2,512]{3,2,1,0:T(2,128)(2,1)} custom-call(s32[16]{0:T(128)S(1)} %get-tuple-element.12.src_ref, bf16[2,29,2,512]{3,2,1,0:T(2,128)(2,1)S(1)} %block_products.5.refs_0_, bf16[4,29,2,512]{3,2,1,0:T(2,128)(2,1)S(1)} %block_products.6.refs_1_, bf16[4,29,2,512]{3,2,1,0:T(2,128)(2,1)S(1)} %block_products.7.refs_2_, ...), custom_call_target="tpu_custom_call" | custom-call | tf_op jit(solution)/shard_map/pack/pallas_call | solution.py:186
  71.2 6.5 %all-to-all-start = ((bf16[16,29,2,512]{3,2,1,0:T(2,128)(2,1)}), bf16[16,29,2,512]{3,2,1,0:T(2,128)(2,1)S(1)}, u32[]{:S(2)}, u32[]{:S(2)}) async-start(bf16[16,29,2,512]{3,2,1,0:T(2,128)(2,1)} %pack.1), calls=%async_computation | async-start | bytes 1900544 | tf_op jit(solution)/shard_map/all_to_all | solution.py:284
  77.8 21.3 %all-to-all-done.r_ref = bf16[16,29,2,512]{3,2,1,0:T(2,128)(2,1)S(1)} async-done(((bf16[16,29,2,512]{3,2,1,0:T(2,128)(2,1)}), bf16[16,29,2,512]{3,2,1,0:T(2,128)(2,1)S(1)}, u32[]{:S(2)}, u32[]{:S(2)}) %all-to-all-start) | async-done | bytes 950304 | tf_op jit(solution)/shard_map/all_to_all | solution.py:284
  99.0 1.3 %assemble.1 = bf16[26,8192]{1,0:T(8,128)(2,1)} custom-call(s32[26,1]{1,0:T(8,128)S(1)} %fusion.1.key_ref, bf16[16,29,2,512]{3,2,1,0:T(2,128)(2,1)S(1)} %all-to-all-done.r_ref), custom_call_target="tpu_custom_call" | custom-call | tf_op jit(solution)/shard_map/assemble/pallas_call | solution.py:217
  (43 shorter events, 9.9 us)
Async XLA Ops:
  0.0 1.0 %copy-start.3 = (bf16[26,8192]{1,0:T(8,128)(2,1)S(1)}, bf16[26,8192]{1,0:T(8,128)(2,1)}, u32[]{:S(2)}) copy-start(bf16[26,8192]{1,0:T(8,128)(2,1)} %x_ref.1) | copy-start | bytes 1277956
  1.1 4.0 %collective-permute-start = (bf16[13,2,8192]{2,1,0:T(2,128)(2,1)S(1)}, bf16[13,2,8192]{2,1,0:T(2,128)(2,1)S(1)}, u32[]{:S(2)}, u32[]{:S(2)}) collective-permute-start(bf16[13,2,8192]{2,1,0:T(2,128)(2,1)S(1)} %pair_rows.1.refs_0_), channel_id=1, source_target_pairs={{0,1},{1,0},{2,3},{3,2},{4,5},{5,4},{6,7},{7,6},{8,9},{9,8},{10,11... | collective-permute-start | bytes 1277960 | tf_op jit(solution)/shard_map/ppermute | solution.py:263
  1.6 8.7 %collective-permute-start.1 = (bf16[13,2,8192]{2,1,0:T(2,128)(2,1)S(1)}, bf16[13,2,8192]{2,1,0:T(2,128)(2,1)S(1)}, u32[]{:S(2)}, u32[]{:S(2)}) collective-permute-start(bf16[13,2,8192]{2,1,0:T(2,128)(2,1)S(1)} %pair_rows.1.refs_0_), channel_id=1, source_target_pairs={{0,4},{1,3},{2,0},{3,7},{4,8},{5,1},{6,2},{7,11},{8,12},{9,5},{10,... | collective-permute-start | bytes 1277960 | tf_op jit(solution)/shard_map/ppermute | solution.py:268
  5.1 9.8 %collective-permute-start.3 = (bf16[13,2,8192]{2,1,0:T(2,128)(2,1)S(1)}, bf16[13,2,8192]{2,1,0:T(2,128)(2,1)S(1)}, u32[]{:S(2)}, u32[]{:S(2)}) collective-permute-start(bf16[13,2,8192]{2,1,0:T(2,128)(2,1)S(1)} %collective-permute-done.refs_1_), channel_id=1, source_target_pairs={{0,4},{1,3},{2,0},{3,7},{4,8},{5,1},{6,2},{7,11},{8,12},{9,5},{10,... | collective-permute-start | bytes 1277960 | tf_op jit(solution)/shard_map/ppermute | solution.py:271
  10.3 9.1 %collective-permute-start.5 = (bf16[13,2,8192]{2,1,0:T(2,128)(2,1)S(1)}, bf16[13,2,8192]{2,1,0:T(2,128)(2,1)S(1)}, u32[]{:S(2)}, u32[]{:S(2)}) collective-permute-start(bf16[13,2,8192]{2,1,0:T(2,128)(2,1)S(1)} %collective-permute-done.1.refs_0_), channel_id=1, source_target_pairs={{0,4},{1,3},{2,0},{3,7},{4,8},{5,1},{6,2},{7,11},{8,12},{9,5},{10,... | collective-permute-start | bytes 1277960 | tf_op jit(solution)/shard_map/ppermute | solution.py:268
  14.9 9.1 %collective-permute-start.7 = (bf16[13,2,8192]{2,1,0:T(2,128)(2,1)S(1)}, bf16[13,2,8192]{2,1,0:T(2,128)(2,1)S(1)}, u32[]{:S(2)}, u32[]{:S(2)}) collective-permute-start(bf16[13,2,8192]{2,1,0:T(2,128)(2,1)S(1)} %collective-permute-done.3.refs_2_), channel_id=1, source_target_pairs={{0,4},{1,3},{2,0},{3,7},{4,8},{5,1},{6,2},{7,11},{8,12},{9,5},{10,... | collective-permute-start | bytes 1277960 | tf_op jit(solution)/shard_map/ppermute | solution.py:271
  19.4 9.1 %collective-permute-start.9 = (bf16[13,2,8192]{2,1,0:T(2,128)(2,1)S(1)}, bf16[13,2,8192]{2,1,0:T(2,128)(2,1)S(1)}, u32[]{:S(2)}, u32[]{:S(2)}) collective-permute-start(bf16[13,2,8192]{2,1,0:T(2,128)(2,1)S(1)} %collective-permute-done.5.refs_0_), channel_id=1, source_target_pairs={{0,4},{1,3},{2,0},{3,7},{4,8},{5,1},{6,2},{7,11},{8,12},{9,5},{10,... | collective-permute-start | bytes 1277960 | tf_op jit(solution)/shard_map/ppermute | solution.py:268
  22.8 7.9 %collective-permute-start.2 = (bf16[13,2,8192]{2,1,0:T(2,128)(2,1)S(1)}, bf16[13,2,8192]{2,1,0:T(2,128)(2,1)S(1)}, u32[]{:S(2)}, u32[]{:S(2)}) collective-permute-start(bf16[13,2,8192]{2,1,0:T(2,128)(2,1)S(1)} %collective-permute-done.1.refs_0_), channel_id=1, source_target_pairs={{0,1},{1,0},{2,3},{3,2},{4,5},{5,4},{6,7},{7,6},{8,9},{9,8},{10,11... | collective-permute-start | bytes 1277960 | tf_op jit(solution)/shard_map/ppermute | solution.py:269
  22.9 24.3 %collective-permute-start.4 = (bf16[13,2,8192]{2,1,0:T(2,128)(2,1)S(1)}, bf16[13,2,8192]{2,1,0:T(2,128)(2,1)}, u32[]{:S(2)}, u32[]{:S(2)}) collective-permute-start(bf16[13,2,8192]{2,1,0:T(2,128)(2,1)S(1)} %collective-permute-done.3.refs_2_), channel_id=1, source_target_pairs={{0,1},{1,0},{2,3},{3,2},{4,5},{5,4},{6,7},{7,6},{8,9},{9,8},{10,11... | collective-permute-start | bytes 1277960 | tf_op jit(solution)/shard_map/ppermute | solution.py:272
  24.0 23.8 %collective-permute-start.11 = (bf16[13,2,8192]{2,1,0:T(2,128)(2,1)S(1)}, bf16[13,2,8192]{2,1,0:T(2,128)(2,1)}, u32[]{:S(2)}, u32[]{:S(2)}) collective-permute-start(bf16[13,2,8192]{2,1,0:T(2,128)(2,1)S(1)} %collective-permute-done.7.refs_2_), channel_id=1, source_target_pairs={{0,4},{1,3},{2,0},{3,7},{4,8},{5,1},{6,2},{7,11},{8,12},{9,5},{10,... | collective-permute-start | bytes 1277960 | tf_op jit(solution)/shard_map/ppermute | solution.py:271
  28.6 9.2 %collective-permute-start.13 = (bf16[13,2,8192]{2,1,0:T(2,128)(2,1)S(1)}, bf16[13,2,8192]{2,1,0:T(2,128)(2,1)}, u32[]{:S(2)}, u32[]{:S(2)}) collective-permute-start(bf16[13,2,8192]{2,1,0:T(2,128)(2,1)S(1)} %collective-permute-done.9.refs_0_), channel_id=1, source_target_pairs={{0,4},{1,3},{2,0},{3,7},{4,8},{5,1},{6,2},{7,11},{8,12},{9,5},{10,... | collective-permute-start | bytes 1277960 | tf_op jit(solution)/shard_map/ppermute | solution.py:268
  30.7 25.5 %collective-permute-start.6 = (bf16[13,2,8192]{2,1,0:T(2,128)(2,1)S(1)}, bf16[13,2,8192]{2,1,0:T(2,128)(2,1)}, u32[]{:S(2)}, u32[]{:S(2)}) collective-permute-start(bf16[13,2,8192]{2,1,0:T(2,128)(2,1)S(1)} %collective-permute-done.5.refs_0_), channel_id=1, source_target_pairs={{0,1},{1,0},{2,3},{3,2},{4,5},{5,4},{6,7},{7,6},{8,9},{9,8},{10,11... | collective-permute-start | bytes 1277960 | tf_op jit(solution)/shard_map/ppermute | solution.py:269
  30.7 0.8 copy-start.4
  31.5 24.7 %collective-permute-start.8 = (bf16[13,2,8192]{2,1,0:T(2,128)(2,1)S(1)}, bf16[13,2,8192]{2,1,0:T(2,128)(2,1)}, u32[]{:S(2)}, u32[]{:S(2)}) collective-permute-start(bf16[13,2,8192]{2,1,0:T(2,128)(2,1)S(1)} %collective-permute-done.7.refs_2_), channel_id=1, source_target_pairs={{0,1},{1,0},{2,3},{3,2},{4,5},{5,4},{6,7},{7,6},{8,9},{9,8},{10,11... | collective-permute-start | bytes 1277960 | tf_op jit(solution)/shard_map/ppermute | solution.py:272
  37.8 22.8 %collective-permute-start.14 = (bf16[13,2,8192]{2,1,0:T(2,128)(2,1)}, bf16[13,2,8192]{2,1,0:T(2,128)(2,1)}, u32[]{:S(2)}, u32[]{:S(2)}) collective-permute-start(bf16[13,2,8192]{2,1,0:T(2,128)(2,1)} %collective-permute-done.13.refs_0_), channel_id=1, source_target_pairs={{0,1},{1,0},{2,3},{3,2},{4,5},{5,4},{6,7},{7,6},{8,9},{9,8},{10,11... | collective-permute-start | bytes 1277960 | tf_op jit(solution)/shard_map/ppermute | solution.py:269
  38.2 3.4 %copy-start = (bf16[8192,512]{1,0:T(8,128)(2,1)S(1)}, bf16[8192,512]{1,0:T(8,128)(2,1)}, u32[]{:S(2)}) copy-start(bf16[8192,512]{1,0:T(8,128)(2,1)} %refs_0_.1) | copy-start | bytes 25165828
  41.5 2.2 %copy-start.1 = (bf16[4,8192,64]{1,2,0:T(8,128)(2,1)S(1)}, bf16[4,8192,64]{1,2,0:T(8,128)(2,1)}, u32[]{:S(2)}) copy-start(bf16[4,8192,64]{1,2,0:T(8,128)(2,1)} %param.11) | copy-start | bytes 12582916
  43.7 2.2 %copy-start.2 = (bf16[4,64,8192]{2,1,0:T(8,128)(2,1)S(1)}, bf16[4,64,8192]{2,1,0:T(8,128)(2,1)}, u32[]{:S(2)}) copy-start(bf16[4,64,8192]{2,1,0:T(8,128)(2,1)} %param.12) | copy-start | bytes 12582916
  47.3 18.0 %collective-permute-start.10 = (bf16[13,2,8192]{2,1,0:T(2,128)(2,1)S(1)}, bf16[13,2,8192]{2,1,0:T(2,128)(2,1)S(1)}, u32[]{:S(2)}, u32[]{:S(2)}) collective-permute-start(bf16[13,2,8192]{2,1,0:T(2,128)(2,1)S(1)} %collective-permute-done.9.refs_0_), channel_id=1, source_target_pairs={{0,1},{1,0},{2,3},{3,2},{4,5},{5,4},{6,7},{7,6},{8,9},{9,8},{10,11... | collective-permute-start | bytes 1277960 | tf_op jit(solution)/shard_map/ppermute | solution.py:269
  47.8 17.4 %collective-permute-start.12 = (bf16[13,2,8192]{2,1,0:T(2,128)(2,1)}, bf16[13,2,8192]{2,1,0:T(2,128)(2,1)S(1)}, u32[]{:S(2)}, u32[]{:S(2)}) collective-permute-start(bf16[13,2,8192]{2,1,0:T(2,128)(2,1)} %collective-permute-done.11.refs_2_), channel_id=1, source_target_pairs={{0,1},{1,0},{2,3},{3,2},{4,5},{5,4},{6,7},{7,6},{8,9},{9,8},{10,11... | collective-permute-start | bytes 1277960 | tf_op jit(solution)/shard_map/ppermute | solution.py:272
  47.9 4.0 %copy-start.5 = (bf16[13,2,8192]{2,1,0:T(2,128)(2,1)S(1)}, bf16[13,2,8192]{2,1,0:T(2,128)(2,1)}, u32[]{:S(2)}) copy-start(bf16[13,2,8192]{2,1,0:T(2,128)(2,1)} %copy-done.4) | copy-start | bytes 1277956
  71.2 27.8 %all-to-all-start = ((bf16[16,29,2,512]{3,2,1,0:T(2,128)(2,1)}), bf16[16,29,2,512]{3,2,1,0:T(2,128)(2,1)S(1)}, u32[]{:S(2)}, u32[]{:S(2)}) async-start(bf16[16,29,2,512]{3,2,1,0:T(2,128)(2,1)} %pack.1), calls=%async_computation | async-start | bytes 1900544 | tf_op jit(solution)/shard_map/all_to_all | solution.py:284

commit v2 on v0

v2 whole, which is shorter than its diff:
```python
import functools

import jax
import jax.numpy as jnp
import numpy as np
from jax import lax
from jax.experimental import pallas as pl
from jax.experimental.pallas import tpu as pltpu
from jax.sharding import PartitionSpec as P

OWNER_ROW_LIMIT = 2
ROW_PAD = 16
adapter_scale = 0.5

VMEM = pl.BlockSpec(memory_space=pltpu.VMEM)
SMEM = pl.BlockSpec(memory_space=pltpu.SMEM)
ANY = pl.BlockSpec(memory_space=pl.ANY)
MIB = 1 << 20


def ring_order(chips):
    return list(range(0, chips, 2)) + list(range(1, chips, 2))[::-1]


def ring_tables(owner_count):
    chips = owner_count // 2
    order = ring_order(chips)
    place = {chip: at for at, chip in enumerate(order)}

    def beside(chip, hops):
        return order[(place[chip] + hops) % chips]

    def turned(hops):
        return [
            (2 * chip + core, 2 * beside(chip, -hops if core else hops) + core)
            for chip in range(chips)
            for core in range(2)
        ]

    swap = [(device, device ^ 1) for device in range(owner_count)]
    sources = np.zeros((2, owner_count, owner_count), np.int32)
    for device in range(owner_count):
        chip, core = divmod(device, 2)
        blocks, pieces = [device, device ^ 1], [[device, device ^ 1]]
        for hops in range(1, chips // 2 + 1):
            mine = 2 * beside(chip, hops if core else -hops)
            mates = 2 * beside(chip, -hops if core else hops)
            if 2 * hops < chips:
                blocks += [mine + core, mates + 1 - core, mine + 1 - core, mates + core]
                pieces += [[mates + core, mine + 1 - core], [mine + core, mates + 1 - core]]
            else:
                blocks += [mine + core, mates + 1 - core]
                pieces += [[mine + core, mine + 1 - core]]
        assert sorted(blocks) == sorted(sum(pieces, [])) == list(range(owner_count))
        sources[0, device], sources[1, device] = blocks, sum(pieces, [])
    return turned, swap, sources


def pair_rows(x):
    rows, width = x.shape

    def kernel(x_ref, o_ref):
        o_ref[...] = x_ref[...].reshape(rows // 2, 2, width)

    return pl.pallas_call(
        kernel,
        out_shape=jax.ShapeDtypeStruct((rows // 2, 2, width), x.dtype),
        in_specs=[VMEM],
        out_specs=VMEM,
        compiler_params=pltpu.CompilerParams(vmem_limit_bytes=4 * MIB),
        name="pair_rows",
    )(x)


def row_places(row_adapter_index, adapter_storage_slot, rows, adapters):
    total, slots = row_adapter_index.shape[0], adapter_storage_slot.shape[0]

    def kernel(index_ref, table_ref, o_ref):
        adapter = lax.broadcasted_iota(jnp.int32, (slots, total), 0)
        slot = jnp.sum(
            jnp.where(adapter == index_ref[...], table_ref[...], 0), axis=0, keepdims=True
        )
        owner = slot // adapters
        at = lax.broadcasted_iota(jnp.int32, (1, total), 1) % rows
        earlier = jnp.zeros_like(slot)
        for back in range(1, rows):
            same = (pltpu.roll(owner, back, 1) == owner) & (at >= back)
            earlier += same.astype(jnp.int32)
        place = slot * OWNER_ROW_LIMIT + earlier
        for group in range(total // rows):
            o_ref[group : group + 1] = place[:, group * rows : (group + 1) * rows]

    return pl.pallas_call(
        kernel,
        out_shape=jax.ShapeDtypeStruct((total // rows, rows), jnp.int32),
        in_specs=[VMEM, VMEM],
        out_specs=VMEM,
        compiler_params=pltpu.CompilerParams(vmem_limit_bytes=8 * MIB),
        name="row_places",
    )(row_adapter_index.reshape(1, total), adapter_storage_slot.reshape(slots, 1))


def hold(weight, carry, before, turn=False):
    shape = weight.shape[::-1] if turn else weight.shape
    parts = 8

    def kernel(*refs):
        src, dst, sem = refs[0], refs[2 + len(before)], refs[-1]
        landing = refs[-2] if turn else dst
        copies = []
        size = weight.shape[1 if turn else 0] // parts
        spans = [pl.ds(part * size, size) for part in range(parts)]
        for part, span in enumerate(spans):
            at = (slice(None), span) if turn else (span,)
            copies.append(pltpu.make_async_copy(src.at[at], landing.at[at], sem.at[part]))
        for copy in copies:
            copy.start()
        for copy, span in zip(copies, spans):
            copy.wait()
            if turn:
                dst[span, :] = landing[:, span].T

    return pl.pallas_call(
        kernel,
        out_shape=[
            pltpu.VMEM(shape, weight.dtype),
            jax.ShapeDtypeStruct(carry.shape, carry.dtype),
        ],
        in_specs=[ANY] * (2 + len(before)),
        out_specs=[VMEM, ANY],
        input_output_aliases={1: 1},
        scratch_shapes=([pltpu.VMEM(weight.shape, weight.dtype)] if turn else [])
        + [pltpu.SemaphoreType.DMA((parts,))],
        compiler_params=pltpu.CompilerParams(vmem_limit_bytes=(8 if turn else 1) * MIB),
        name="hold",
    )(weight, carry, *before)


def after(x, before):
    def kernel(*refs):
        pass

    return pl.pallas_call(
        kernel,
        out_shape=jax.ShapeDtypeStruct(x.shape, x.dtype),
        in_specs=[ANY] * (1 + len(before)),
        out_specs=ANY,
        input_output_aliases={0: 0},
        compiler_params=pltpu.CompilerParams(vmem_limit_bytes=1 * MIB),
        name="after",
    )(x, *before)


def block_products(sources, start, row_place, blocks, places, weights, rank, owner_count):
    base_weight, down, up = weights
    count = len(blocks)
    results = 1 + max(result for result, _ in places)
    pairs, _, width = blocks[0].shape
    rows = 2 * pairs
    padded = -(-rows // ROW_PAD) * ROW_PAD
    columns = base_weight.shape[1]
    ranks = down.shape[1]
    depth = min(width, 1024)
    parts = width // depth
    adapters = ranks // rank
    taken = OWNER_ROW_LIMIT * adapters
    takes = -(-OWNER_ROW_LIMIT * count // 8) * 8

    def kernel(src_ref, place_ref, *refs):
        me = lax.axis_index("owner")
        block_refs = refs[:count]
        w_ref, d_ref, u_ref = refs[count : count + 3]
        out_refs = refs[count + 3 :][:results]
        x_ref, code_ref = refs[-2:]
        for b in range(count):
            x_ref[padded * b : padded * b + rows] = block_refs[b][...].reshape(rows, width)
            x_ref[padded * b + rows : padded * (b + 1)] = jnp.zeros(
                (padded - rows, width), x_ref.dtype
            )
        low = jnp.zeros((padded * count, ranks), jnp.float32)
        for part in range(parts):
            at = part * depth
            low += jnp.dot(
                x_ref[:, at : at + depth],
                d_ref[at : at + depth, :],
                preferred_element_type=jnp.float32,
            )
        low = low.astype(jnp.bfloat16)
        code_ref[...] = jnp.full_like(code_ref, -1)
        for b in range(count):
            code_ref[:, padded * b : padded * b + rows] = (
                place_ref[pl.ds(src_ref[me, start + b], 1), :] - me * taken
            )
        row = lax.broadcasted_iota(jnp.int32, (adapters * takes, padded * count), 0)
        lane = lax.broadcasted_iota(jnp.int32, (adapters * takes, padded * count), 1)
        place = row % takes
        wanted = row // takes * OWNER_ROW_LIMIT + place % OWNER_ROW_LIMIT
        match = (code_ref[...] == wanted) & (lane // padded == place // OWNER_ROW_LIMIT)
        found = jnp.dot(match.astype(jnp.bfloat16), low, preferred_element_type=jnp.float32)
        adapter = lax.broadcasted_iota(jnp.int32, (takes, ranks), 1) // rank
        chosen = jnp.zeros((takes, ranks), jnp.float32)
        for a in range(adapters):
            chosen = jnp.where(adapter == a, found[takes * a : takes * (a + 1)], chosen)
        chosen = chosen.astype(jnp.bfloat16)
        base = jnp.zeros((padded * count, columns), jnp.float32)
        for part in range(parts):
            at = part * depth
            base += jnp.dot(
                x_ref[:, at : at + depth],
                w_ref[at : at + depth, :],
                preferred_element_type=jnp.float32,
            )
        for b, (result, place) in enumerate(places):
            out_refs[result][place, :pairs] = (
                base[padded * b : padded * b + rows]
                .astype(jnp.bfloat16)
                .reshape(pairs, 2, columns)
            )
        for k in range(owner_count):
            delta = jnp.dot(
                chosen, u_ref[:, columns * k : columns * (k + 1)], preferred_element_type=jnp.float32
            ).astype(jnp.bfloat16)
            for b, (result, place) in enumerate(places):
                out_refs[result][place, pairs + k] = delta[
                    OWNER_ROW_LIMIT * b : OWNER_ROW_LIMIT * (b + 1)
                ]

    return pl.pallas_call(
        kernel,
        out_shape=[
            jax.ShapeDtypeStruct((2, pairs + owner_count, 2, columns), jnp.bfloat16)
            for _ in range(results)
        ],
        in_specs=[SMEM] + [VMEM] * (count + 4),
        out_specs=[VMEM] * results,
        scratch_shapes=[
            pltpu.VMEM((padded * count, width), jnp.bfloat16),
            pltpu.VMEM((1, padded * count), jnp.int32),
        ],
        compiler_params=pltpu.CompilerParams(vmem_limit_bytes=16 * MIB),
        cost_estimate=pl.CostEstimate(
            flops=2 * padded * count * width * (columns + ranks),
            bytes_accessed=width * (columns + 2 * ranks) * 2,
            transcendentals=0,
        ),
        name="block_products",
    )(sources, row_place, *blocks, base_weight, down, up)


def others(received, before):
    count = len(received)

    def kernel(*refs):
        o_ref, sem = refs[-2], refs[-1]
        copies = [
            pltpu.make_async_copy(refs[i].at[1], o_ref.at[i], sem.at[i]) for i in range(count)
        ]
        for copy in copies:
            copy.start()
        for copy in copies:
            copy.wait()

    return pl.pallas_call(
        kernel,
        out_shape=jax.ShapeDtypeStruct((count,) + received[0].shape[1:], received[0].dtype),
        in_specs=[VMEM] * count + [ANY] * len(before),
        out_specs=VMEM,
        scratch_shapes=[pltpu.SemaphoreType.DMA((count,))],
        compiler_params=pltpu.CompilerParams(vmem_limit_bytes=8 * MIB),
        name="others",
    )(*received, *before)


def assemble(sources, row_place, received, adapters, rows):
    arrays = [array for array, _ in received]
    at_of = [(i, at) for i, (_, ats) in enumerate(received) for at in ats]
    count = len(at_of)
    pairs = rows // 2
    columns = arrays[0].shape[-1]
    slots = OWNER_ROW_LIMIT * count

    def kernel(src_ref, place_ref, *refs):
        me = lax.axis_index("owner")
        o_ref, delta_ref, sem = refs[-3:]
        piece_refs = [refs[i].at[at] for i, at in at_of]
        copies = [
            pltpu.make_async_copy(ref.at[pl.ds(pairs, count)], delta_ref.at[:, a], sem.at[a])
            for a, ref in enumerate(piece_refs)
        ]
        for copy in copies:
            copy.start()
        place = place_ref[pl.ds(me, 1), :]
        owner = place // (adapters * OWNER_ROW_LIMIT)
        place = place % OWNER_ROW_LIMIT
        slot = lax.broadcasted_iota(jnp.int32, (slots, rows), 0)
        piece, second = slot // OWNER_ROW_LIMIT, slot % OWNER_ROW_LIMIT
        match = jnp.zeros((slots, rows), jnp.float32)
        for a in range(count):
            match = jnp.where(
                (piece == a) & (owner == src_ref[me, a]) & (place == second), 1.0, match
            )
        pick = match.T.astype(jnp.bfloat16)
        for copy in copies:
            copy.wait()
        for a, ref in enumerate(piece_refs):
            delta = jnp.dot(
                pick,
                delta_ref[src_ref[me, a]].reshape(slots, columns),
                preferred_element_type=jnp.float32,
            )
            base = ref[:pairs].reshape(rows, columns).astype(jnp.float32)
            span = pl.ds(pl.multiple_of(src_ref[me, a] * columns, columns), columns)
            o_ref[:, span] = (base + adapter_scale * delta).astype(o_ref.dtype)

    return pl.pallas_call(
        kernel,
        out_shape=jax.ShapeDtypeStruct((rows, count * columns), jnp.bfloat16),
        in_specs=[SMEM] + [VMEM] * (len(arrays) + 1),
        out_specs=VMEM,
        scratch_shapes=[
            pltpu.VMEM((count, count, 2, columns), jnp.bfloat16),
            pltpu.SemaphoreType.DMA((count,)),
        ],
        compiler_params=pltpu.CompilerParams(vmem_limit_bytes=16 * MIB),
        name="assemble",
    )(sources, row_place, *arrays)


def per_device(
    states, row_adapter_index, adapter_storage_slot, base_weight, down_weight, up_weight
):
    owner_count = lax.axis_size("owner")
    rows, width = states.shape
    adapters, rank = down_weight.shape[0], down_weight.shape[2]
    turned, swap, sources = ring_tables(owner_count)
    send = functools.partial(lax.ppermute, axis_name="owner")

    down = down_weight.transpose(0, 2, 1).reshape(adapters * rank, width)
    up = up_weight.reshape(adapters * rank, width)

    row_place = row_places(row_adapter_index, adapter_storage_slot, rows, adapters)
    chips = owner_count // 2
    last = chips // 2
    split = [list(range(at - 1, at + 1)) for at in range(last, 2, -2)][::-1]
    split = [list(range(split[0][0] if split else last + 1))] + split
    order, at = [], 0
    for hops in split:
        came = sum(2 if 0 < 2 * hop < chips else 1 for hop in hops)
        order += [at + 2 * i for i in range(came)] + [at + 2 * i + 1 for i in range(came)]
        at += 2 * came
    block_from, piece_from = jnp.asarray(sources[0]), jnp.asarray(sources[1][:, order])

    base_weight, down, up = (
        pltpu.with_memory_space_constraint(w, pltpu.HBM) for w in (base_weight, down, up)
    )
    own = pair_rows(states)
    first, second = own, send(own, perm=swap)
    groups = [[first, second]]
    held = [None] * 3
    received = []

    def products(hops, start):
        blocks, places, result = [], [], 0
        for hop in hops:
            blocks += groups[hop]
            if len(groups[hop]) == 4:
                places += [(result, 0), (result + 1, 1), (result, 1), (result + 1, 0)]
                result += 2
            else:
                places += [(result, 0), (result, 1)]
                result += 1
        out = block_products(
            block_from, start, row_place, blocks, places, held, rank, owner_count
        )
        came, at = [], 0
        for hop in hops:
            came.append(send(out[at], perm=turned(-hop)) if hop else out[at])
            at += 1
            if len(groups[hop]) == 4:
                came.append(send(out[at], perm=turned(hop)))
                at += 1
        received.append(came)
        return len(blocks), out[0]

    done = 0
    for hops in range(1, last + 1):
        first = send(first, perm=turned(1))
        if hops == 1:
            held[0], first = hold(base_weight, first, [row_place])
        if hops == min(2, last):
            held[2], first = hold(up, first, [])
        if hops == last and len(split) > 1:
            for early in split[:-1]:
                count, made = products(early, done)
                done += count
            first = after(first, [made])
        group = [first, send(first, perm=swap)]
        if 2 * hops < chips:
            second = send(second, perm=turned(1))
            if hops == 1:
                held[1], second = hold(down, second, [], turn=True)
            group += [second, send(second, perm=swap)]
        groups.append(group)
    if held[1] is None:
        held[1], row_place = hold(down, row_place, [], turn=True)
    _, made = products(split[-1], done)
    arrays = []
    for came in received:
        passed = send(others(came, [made]), perm=swap)
        arrays += [(array, (0,)) for array in came] + [(passed, tuple(range(len(came))))]
    return assemble(piece_from, row_place, arrays, adapters, rows)


def solution(mesh):
    return jax.shard_map(
        per_device,
        mesh=mesh,
        in_specs=(
            P(("groups", "owner"), None),
            P("groups"),
            P("groups"),
            P(None, "owner"),
            P("owner", None, None),
            P("owner", None, None),
        ),
        out_specs=P(("groups", "owner"), None),
        check_vma=False,
    )
```

time: 152 us -> 76.4 us (0.50)
  other arithmetic: 42.7 us -> 0 us
  waiting for transfers between devices: 45.2 us -> 16.8 us
  Pallas kernels: 0 us -> 26.7 us
  local copies, waits for them, and re-layouts: 25 us -> 2.47 us
  starting transfers between devices: 8.23 us -> 29.8 us
  matrix products: 15.7 us -> 0 us
  between operations: 13.6 us -> 0.31 us
    eq x1 -> x0, other arithmetic: 40.6 us -> none  [per_device(): owners == my_index]
    all_gather x1 -> x0, waiting for transfers between devices: 30.2 us -> none  [per_device(): full_states = lax.all_gather(states, 'owner', axis=0, tiled=True)]
    ppermute x0 -> x24, starting transfers between devices: none -> 29.8 us  [the longest x4 10.2 us: products(): came.append(send(out[at], perm=turned(-hop)) if hop else out[at])]
    pallas_call x0 -> x11, Pallas kernels: none -> 26.7 us  [the longest x2 14.4 us: block_products(): pl.pallas_call(kernel, out_shape=[jax.ShapeDtypeStruct((2, pairs + owner_...]
    ppermute x0 -> x24, waiting for transfers between devices: none -> 16.8 us  [the longest x4 8.83 us: per_device(): first = send(first, perm=turned(1))]
    dot_general x9 -> x0, matrix products: 15.7 us -> none  [the longest x1 8.99 us: per_device(): jnp.dot(full_states, base_weight, preferred_element_type=jnp.float32)]
    all_to_all x2 -> x0, waiting for transfers between devices: 14.3 us -> none  [the longest x1 13 us: per_device(): lax.all_to_all(adapter_delta.astype(jnp.bfloat16).reshape(owner_count, OW...]
    gather x6 -> x0, local copies, waits for them, and re-layouts: 13.8 us -> none  [the longest x4 7.82 us: per_device(): slot_per_row = jnp.take(adapter_storage_slot, row_adapter_index)]
  transfers between devices with their start and end apart: 3 -> 24, of which waited for: 3 -> 5; matrix products, arithmetic and copies ran while one was open for 43% -> 1% of each run, Pallas kernels for 0% -> 32%
where the time goes in v2:
time: 76.4 us; the launch traced here: 76.1 us
  starting transfers between devices  29.8 us (39%)
  Pallas kernels  26.7 us (35%)
  waiting for transfers between devices  16.8 us (22%)
  local copies, waits for them, and re-layouts  2.47 us (3%)
    pallas_call x2, Pallas kernels, block_products(): pl.pallas_call(kernel, out_shape=[jax.ShapeDtypeStruct((2, pairs + owner_...  14.4 us
    ppermute x4, starting transfers between devices, products(): came.append(send(out[at], perm=turned(-hop)) if hop else out[at])  10.2 us
    ppermute x4, starting transfers between devices, per_device(): first = send(first, perm=turned(1))  8.97 us
    ppermute x4, waiting for transfers between devices, per_device(): first = send(first, perm=turned(1))  8.83 us
    pallas_call x3, Pallas kernels, hold(): pl.pallas_call(kernel, out_shape=[pltpu.VMEM(shape, weight.dtype), jax.Sh...  8.35 us
    ppermute x3, waiting for transfers between devices, products(): came.append(send(out[at], perm=turned(hop)))  6.52 us
    ppermute x3, starting transfers between devices, per_device(): second = send(second, perm=turned(1))  4.91 us
    ppermute x3, starting transfers between devices, products(): came.append(send(out[at], perm=turned(hop)))  3.46 us
  transfers between devices with their start and end apart: 24, of which 5 were waited for; matrix products, arithmetic and copies ran while one was open for 1% of the time, Pallas kernels for 32%

profile of v2, /device:TPU:0, one launch (start us, length us, event | category | flops | bytes accessed | tf_op | source)
XLA Modules:
  0.0 76.1 jit_solution(8385948132453501191)
XLA Ops:
  0.0 1.0 %copy-done = bf16[26,8192]{1,0:T(8,128)(2,1)S(1)} copy-done((bf16[26,8192]{1,0:T(8,128)(2,1)S(1)}, bf16[26,8192]{1,0:T(8,128)(2,1)}, u32[]{:S(2)}) %copy-start) | copy-done | bytes 426008
  1.6 2.6 %collective-permute-start.1 = (bf16[13,2,8192]{2,1,0:T(2,128)(2,1)S(1)}, bf16[13,2,8192]{2,1,0:T(2,128)(2,1)S(1)}, u32[]{:S(2)}, u32[]{:S(2)}) collective-permute-start(bf16[13,2,8192]{2,1,0:T(2,128)(2,1)S(1)} %pair_rows.1.refs_0_), channel_id=1, source_target_pairs={{0,4},{1,3},{2,0},{3,7},{4,8},{5,1},{6,2},{7,11},{8,12},{9,5},{10,... | collective-permute-start | bytes 1277960 | tf_op jit(solution)/shard_map/ppermute | solution.py:387
  4.3 1.7 %collective-permute-start.3 = (bf16[13,2,8192]{2,1,0:T(2,128)(2,1)S(1)}, bf16[13,2,8192]{2,1,0:T(2,128)(2,1)S(1)}, u32[]{:S(2)}, u32[]{:S(2)}) collective-permute-start(bf16[13,2,8192]{2,1,0:T(2,128)(2,1)S(1)} %collective-permute-done.refs_1_), channel_id=1, source_target_pairs={{0,4},{1,3},{2,0},{3,7},{4,8},{5,1},{6,2},{7,11},{8,12},{9,5},{10,... | collective-permute-start | bytes 1277960 | tf_op jit(solution)/shard_map/ppermute | solution.py:399
  8.2 2.1 %collective-permute-done.1.refs_1_ = bf16[13,2,8192]{2,1,0:T(2,128)(2,1)S(1)} collective-permute-done((bf16[13,2,8192]{2,1,0:T(2,128)(2,1)S(1)}, bf16[13,2,8192]{2,1,0:T(2,128)(2,1)S(1)}, u32[]{:S(2)}, u32[]{:S(2)}) %collective-permute-start.1) | collective-permute-done | bytes 426016 | tf_op jit(solution)/shard_map/ppermute | solution.py:387
  10.3 3.5 %hold.3 = (bf16[8192,512]{1,0:T(8,128)(2,1)S(1)}, bf16[13,2,8192]{2,1,0:T(2,128)(2,1)S(1)}) custom-call(bf16[8192,512]{1,0:T(8,128)(2,1)} %refs_0_.1, bf16[13,2,8192]{2,1,0:T(2,128)(2,1)S(1)} %collective-permute-done.1.refs_1_, s32[16,26]{1,0:T(8,128)S(1)} %row_places.1.refs_2_.place_ref), custom_call_target="tpu_custom_call", output_to_operand_aliasing={{1}: (1, {})} | custom-call | tf_op jit(solution)/shard_map/hold/pallas_call | solution.py:123
  13.8 2.1 %collective-permute-start.5 = (bf16[13,2,8192]{2,1,0:T(2,128)(2,1)S(1)}, bf16[13,2,8192]{2,1,0:T(2,128)(2,1)S(1)}, u32[]{:S(2)}, u32[]{:S(2)}) collective-permute-start(bf16[13,2,8192]{2,1,0:T(2,128)(2,1)S(1)} %get-tuple-element.19.refs_2_), channel_id=1, source_target_pairs={{0,4},{1,3},{2,0},{3,7},{4,8},{5,1},{6,2},{7,11},{8,12},{9,5},{10,... | collective-permute-start | bytes 1277960 | tf_op jit(solution)/shard_map/ppermute | solution.py:387
  15.9 2.7 %hold.4 = (bf16[8192,256]{1,0:T(8,128)(2,1)S(1)}, bf16[13,2,8192]{2,1,0:T(2,128)(2,1)S(1)}) custom-call(bf16[256,8192]{1,0:T(8,128)(2,1)} %bitcast.7, bf16[13,2,8192]{2,1,0:T(2,128)(2,1)S(1)} %collective-permute-done.3.refs_1_), custom_call_target="tpu_custom_call", output_to_operand_aliasing={{1}: (1, {})} | custom-call | tf_op jit(solution)/shard_map/hold/pallas_call | solution.py:123
  18.6 1.6 %collective-permute-start.7 = (bf16[13,2,8192]{2,1,0:T(2,128)(2,1)S(1)}, bf16[13,2,8192]{2,1,0:T(2,128)(2,1)S(1)}, u32[]{:S(2)}, u32[]{:S(2)}) collective-permute-start(bf16[13,2,8192]{2,1,0:T(2,128)(2,1)S(1)} %get-tuple-element.20.refs_4_), channel_id=1, source_target_pairs={{0,4},{1,3},{2,0},{3,7},{4,8},{5,1},{6,2},{7,11},{8,12},{9,5},{10,... | collective-permute-start | bytes 1277960 | tf_op jit(solution)/shard_map/ppermute | solution.py:399
  20.2 1.7 %collective-permute-done.5.refs_1_ = bf16[13,2,8192]{2,1,0:T(2,128)(2,1)S(1)} collective-permute-done((bf16[13,2,8192]{2,1,0:T(2,128)(2,1)S(1)}, bf16[13,2,8192]{2,1,0:T(2,128)(2,1)S(1)}, u32[]{:S(2)}, u32[]{:S(2)}) %collective-permute-start.5) | collective-permute-done | bytes 426016 | tf_op jit(solution)/shard_map/ppermute | solution.py:387
  22.0 2.2 %hold.5 = (bf16[256,8192]{1,0:T(8,128)(2,1)S(1)}, bf16[13,2,8192]{2,1,0:T(2,128)(2,1)S(1)}) custom-call(bf16[256,8192]{1,0:T(8,128)(2,1)} %bitcast.8, bf16[13,2,8192]{2,1,0:T(2,128)(2,1)S(1)} %collective-permute-done.5.refs_1_), custom_call_target="tpu_custom_call", output_to_operand_aliasing={{1}: (1, {})} | custom-call | tf_op jit(solution)/shard_map/hold/pallas_call | solution.py:123
  24.2 2.1 %collective-permute-start.13 = (bf16[13,2,8192]{2,1,0:T(2,128)(2,1)S(1)}, bf16[13,2,8192]{2,1,0:T(2,128)(2,1)S(1)}, u32[]{:S(2)}, u32[]{:S(2)}) collective-permute-start(bf16[13,2,8192]{2,1,0:T(2,128)(2,1)S(1)} %get-tuple-element.21.refs_6_), channel_id=1, source_target_pairs={{0,4},{1,3},{2,0},{3,7},{4,8},{5,1},{6,2},{7,11},{8,12},{9,5},{10,... | collective-permute-start | bytes 1277960 | tf_op jit(solution)/shard_map/ppermute | solution.py:387
  27.3 5.0 %collective-permute-done.13.refs_0_ = bf16[13,2,8192]{2,1,0:T(2,128)(2,1)S(1)} collective-permute-done((bf16[13,2,8192]{2,1,0:T(2,128)(2,1)S(1)}, bf16[13,2,8192]{2,1,0:T(2,128)(2,1)S(1)}, u32[]{:S(2)}, u32[]{:S(2)}) %collective-permute-start.13) | collective-permute-done | bytes 426016 | tf_op jit(solution)/shard_map/ppermute | solution.py:387
  32.4 2.1 %collective-permute-start.17 = (bf16[13,2,8192]{2,1,0:T(2,128)(2,1)S(1)}, bf16[13,2,8192]{2,1,0:T(2,128)(2,1)S(1)}, u32[]{:S(2)}, u32[]{:S(2)}) collective-permute-start(bf16[13,2,8192]{2,1,0:T(2,128)(2,1)S(1)} %collective-permute-done.13.refs_0_), channel_id=1, source_target_pairs={{0,4},{1,3},{2,0},{3,7},{4,8},{5,1},{6,2},{7,11},{8,12},{9,5},{10,... | collective-permute-start | bytes 1277960 | tf_op jit(solution)/shard_map/ppermute | solution.py:387
  34.5 1.6 %collective-permute-start.15 = (bf16[13,2,8192]{2,1,0:T(2,128)(2,1)S(1)}, bf16[13,2,8192]{2,1,0:T(2,128)(2,1)S(1)}, u32[]{:S(2)}, u32[]{:S(2)}) collective-permute-start(bf16[13,2,8192]{2,1,0:T(2,128)(2,1)S(1)} %collective-permute-done.7.refs_8_), channel_id=1, source_target_pairs={{0,4},{1,3},{2,0},{3,7},{4,8},{5,1},{6,2},{7,11},{8,12},{9,5},{10,... | collective-permute-start | bytes 1277960 | tf_op jit(solution)/shard_map/ppermute | solution.py:399
  36.1 8.6 %block_products.2 = (bf16[2,29,2,512]{3,2,1,0:T(2,128)(2,1)S(1)}, bf16[2,29,2,512]{3,2,1,0:T(2,128)(2,1)S(1)}, bf16[2,29,2,512]{3,2,1,0:T(2,128)(2,1)S(1)}, bf16...) custom-call(s32[16,16]{1,0:T(8,128)S(1)} %copy-done.1, s32[16,26]{1,0:T(8,128)S(1)} %row_places.1.refs_2_.place_ref, ...), custom_call_target="tpu_custom_call" | custom-call | flops 4026531840 | bytes 16777216 | tf_op jit(solution)/shard_map/block_products/pallas_call | solution.py:228
  45.3 1.8 %collective-permute-start.10 = (bf16[2,29,2,512]{3,2,1,0:T(2,128)(2,1)S(1)}, bf16[2,29,2,512]{3,2,1,0:T(2,128)(2,1)S(1)}, u32[]{:S(2)}, u32[]{:S(2)}) collective-permute-start(bf16[2,29,2,512]{3,2,1,0:T(2,128)(2,1)S(1)} %get-tuple-element.27), channel_id=1, source_target_pairs={{0,4},{1,3},{2,0},{3,7},{4,8},{5,1},{6,2},{7,11},{8,12},{9,5},{10,... | collective-permute-start | bytes 356360 | tf_op jit(solution)/shard_map/ppermute | solution.py:380
  47.1 1.4 %collective-permute-start.11 = (bf16[2,29,2,512]{3,2,1,0:T(2,128)(2,1)S(1)}, bf16[2,29,2,512]{3,2,1,0:T(2,128)(2,1)S(1)}, u32[]{:S(2)}, u32[]{:S(2)}) collective-permute-start(bf16[2,29,2,512]{3,2,1,0:T(2,128)(2,1)S(1)} %get-tuple-element.28), channel_id=1, source_target_pairs={{0,6},{1,9},{2,10},{3,5},{4,2},{5,13},{6,14},{7,1},{8,0},{9,15},{1... | collective-permute-start | bytes 356360 | tf_op jit(solution)/shard_map/ppermute | solution.py:377
  48.6 1.5 %collective-permute-start.12 = (bf16[2,29,2,512]{3,2,1,0:T(2,128)(2,1)S(1)}, bf16[2,29,2,512]{3,2,1,0:T(2,128)(2,1)S(1)}, u32[]{:S(2)}, u32[]{:S(2)}) collective-permute-start(bf16[2,29,2,512]{3,2,1,0:T(2,128)(2,1)S(1)} %get-tuple-element.29), channel_id=1, source_target_pairs={{0,8},{1,7},{2,4},{3,11},{4,12},{5,3},{6,0},{7,15},{8,14},{9,1},{1... | collective-permute-start | bytes 356360 | tf_op jit(solution)/shard_map/ppermute | solution.py:380
  50.4 5.8 %block_products.3 = (bf16[2,29,2,512]{3,2,1,0:T(2,128)(2,1)S(1)}, bf16[2,29,2,512]{3,2,1,0:T(2,128)(2,1)S(1)}, bf16[2,29,2,512]{3,2,1,0:T(2,128)(2,1)S(1)}) custom-call(s32[16,16]{1,0:T(8,128)S(1)} %copy-done.1, s32[16,26]{1,0:T(8,128)S(1)} %row_places.1.refs_2_.place_ref, bf16[13,2,8192]{2,1,0:T(2,128)(2,1)S(1)} %collective-permute-done.13.refs_0_, ...), custom_call_target="tpu_custom_call" | custom-call | flops 2415919104 | bytes 16777216 | tf_op jit(solution)/shard_map/block_products/pallas_call | solution.py:228
  56.2 3.7 %collective-permute-start.20 = (bf16[2,29,2,512]{3,2,1,0:T(2,128)(2,1)S(1)}, bf16[2,29,2,512]{3,2,1,0:T(2,128)(2,1)S(1)}, u32[]{:S(2)}, u32[]{:S(2)}) collective-permute-start(bf16[2,29,2,512]{3,2,1,0:T(2,128)(2,1)S(1)} %get-tuple-element.30.refs_5_.refs_3_), channel_id=1, source_target_pairs={{0,10},{1,13},{2,14},{3,9},{4,6},{5,15},{6,12},{7,5},{8,2},{9,11},... | collective-permute-start | bytes 356360 | tf_op jit(solution)/shard_map/ppermute | solution.py:377
  60.1 4.7 %collective-permute-start.22 = (bf16[2,29,2,512]{3,2,1,0:T(2,128)(2,1)S(1)}, bf16[2,29,2,512]{3,2,1,0:T(2,128)(2,1)S(1)}, u32[]{:S(2)}, u32[]{:S(2)}) collective-permute-start(bf16[2,29,2,512]{3,2,1,0:T(2,128)(2,1)S(1)} %get-tuple-element.32), channel_id=1, source_target_pairs={{0,14},{1,15},{2,12},{3,13},{4,10},{5,11},{6,8},{7,9},{8,6},{9,7},... | collective-permute-start | bytes 356360 | tf_op jit(solution)/shard_map/ppermute | solution.py:377
  65.3 6.5 %collective-permute-done.21.refs_1_.refs_7_ = bf16[2,29,2,512]{3,2,1,0:T(2,128)(2,1)S(1)} collective-permute-done((bf16[2,29,2,512]{3,2,1,0:T(2,128)(2,1)S(1)}, bf16[2,29,2,512]{3,2,1,0:T(2,128)(2,1)S(1)}, u32[]{:S(2)}, u32[]{:S(2)}) %collective-permute-start.21) | collective-permute-done | bytes 118816 | tf_op jit(solution)/shard_map/ppermute | solution.py:380
  72.2 1.4 %collective-permute-done.23.refs_9_ = bf16[3,29,2,512]{3,2,1,0:T(2,128)(2,1)S(1)} collective-permute-done((bf16[3,29,2,512]{3,2,1,0:T(2,128)(2,1)S(1)}, bf16[3,29,2,512]{3,2,1,0:T(2,128)(2,1)S(1)}, u32[]{:S(2)}, u32[]{:S(2)}) %collective-permute-start.23) | collective-permute-done | bytes 178208 | tf_op jit(solution)/shard_map/ppermute | solution.py:409
  73.6 2.3 %assemble.1 = bf16[26,8192]{1,0:T(8,128)(2,1)} custom-call(s32[16,16]{1,0:T(8,128)S(1)} %copy-done.2, s32[16,26]{1,0:T(8,128)S(1)} %row_places.1.refs_2_.place_ref, bf16[2,29,2,512]{3,2,1,0:T(2,128)(2,1)S(1)} %get-tuple-element.25.refs_1_.refs_0_, bf16[2,29,2,512]{3,2,1,0:T(2,128)(2,1)S(1)} %collective-permute-done.9.refs_1_, ...), custom_call_target="tpu_custom_call" | custom-call | tf_op jit(solution)/shard_map/assemble/pallas_call | solution.py:315
  (44 shorter events, 5.8 us)
Async XLA Ops:
  1.1 3.2 %collective-permute-start = (bf16[13,2,8192]{2,1,0:T(2,128)(2,1)S(1)}, bf16[13,2,8192]{2,1,0:T(2,128)(2,1)S(1)}, u32[]{:S(2)}, u32[]{:S(2)}) collective-permute-start(bf16[13,2,8192]{2,1,0:T(2,128)(2,1)S(1)} %pair_rows.1.refs_0_), channel_id=1, source_target_pairs={{0,1},{1,0},{2,3},{3,2},{4,5},{5,4},{6,7},{7,6},{8,9},{9,8},{10,11... | collective-permute-start | bytes 1277960 | tf_op jit(solution)/shard_map/ppermute | solution.py:357
  1.6 8.7 %collective-permute-start.1 = (bf16[13,2,8192]{2,1,0:T(2,128)(2,1)S(1)}, bf16[13,2,8192]{2,1,0:T(2,128)(2,1)S(1)}, u32[]{:S(2)}, u32[]{:S(2)}) collective-permute-start(bf16[13,2,8192]{2,1,0:T(2,128)(2,1)S(1)} %pair_rows.1.refs_0_), channel_id=1, source_target_pairs={{0,4},{1,3},{2,0},{3,7},{4,8},{5,1},{6,2},{7,11},{8,12},{9,5},{10,... | collective-permute-start | bytes 1277960 | tf_op jit(solution)/shard_map/ppermute | solution.py:387
  4.3 11.7 %collective-permute-start.3 = (bf16[13,2,8192]{2,1,0:T(2,128)(2,1)S(1)}, bf16[13,2,8192]{2,1,0:T(2,128)(2,1)S(1)}, u32[]{:S(2)}, u32[]{:S(2)}) collective-permute-start(bf16[13,2,8192]{2,1,0:T(2,128)(2,1)S(1)} %collective-permute-done.refs_1_), channel_id=1, source_target_pairs={{0,4},{1,3},{2,0},{3,7},{4,8},{5,1},{6,2},{7,11},{8,12},{9,5},{10,... | collective-permute-start | bytes 1277960 | tf_op jit(solution)/shard_map/ppermute | solution.py:399
  13.8 8.2 %collective-permute-start.5 = (bf16[13,2,8192]{2,1,0:T(2,128)(2,1)S(1)}, bf16[13,2,8192]{2,1,0:T(2,128)(2,1)S(1)}, u32[]{:S(2)}, u32[]{:S(2)}) collective-permute-start(bf16[13,2,8192]{2,1,0:T(2,128)(2,1)S(1)} %get-tuple-element.19.refs_2_), channel_id=1, source_target_pairs={{0,4},{1,3},{2,0},{3,7},{4,8},{5,1},{6,2},{7,11},{8,12},{9,5},{10,... | collective-permute-start | bytes 1277960 | tf_op jit(solution)/shard_map/ppermute | solution.py:387
  18.6 8.2 %collective-permute-start.7 = (bf16[13,2,8192]{2,1,0:T(2,128)(2,1)S(1)}, bf16[13,2,8192]{2,1,0:T(2,128)(2,1)S(1)}, u32[]{:S(2)}, u32[]{:S(2)}) collective-permute-start(bf16[13,2,8192]{2,1,0:T(2,128)(2,1)S(1)} %get-tuple-element.20.refs_4_), channel_id=1, source_target_pairs={{0,4},{1,3},{2,0},{3,7},{4,8},{5,1},{6,2},{7,11},{8,12},{9,5},{10,... | collective-permute-start | bytes 1277960 | tf_op jit(solution)/shard_map/ppermute | solution.py:399
  24.2 8.2 %collective-permute-start.13 = (bf16[13,2,8192]{2,1,0:T(2,128)(2,1)S(1)}, bf16[13,2,8192]{2,1,0:T(2,128)(2,1)S(1)}, u32[]{:S(2)}, u32[]{:S(2)}) collective-permute-start(bf16[13,2,8192]{2,1,0:T(2,128)(2,1)S(1)} %get-tuple-element.21.refs_6_), channel_id=1, source_target_pairs={{0,4},{1,3},{2,0},{3,7},{4,8},{5,1},{6,2},{7,11},{8,12},{9,5},{10,... | collective-permute-start | bytes 1277960 | tf_op jit(solution)/shard_map/ppermute | solution.py:387
  26.3 8.1 %collective-permute-start.2 = (bf16[13,2,8192]{2,1,0:T(2,128)(2,1)S(1)}, bf16[13,2,8192]{2,1,0:T(2,128)(2,1)S(1)}, u32[]{:S(2)}, u32[]{:S(2)}) collective-permute-start(bf16[13,2,8192]{2,1,0:T(2,128)(2,1)S(1)} %get-tuple-element.19.refs_2_), channel_id=1, source_target_pairs={{0,1},{1,0},{2,3},{3,2},{4,5},{5,4},{6,7},{7,6},{8,9},{9,8},{10,11... | collective-permute-start | bytes 1277960 | tf_op jit(solution)/shard_map/ppermute | solution.py:397
  26.3 9.7 %collective-permute-start.6 = (bf16[13,2,8192]{2,1,0:T(2,128)(2,1)S(1)}, bf16[13,2,8192]{2,1,0:T(2,128)(2,1)S(1)}, u32[]{:S(2)}, u32[]{:S(2)}) collective-permute-start(bf16[13,2,8192]{2,1,0:T(2,128)(2,1)S(1)} %get-tuple-element.21.refs_6_), channel_id=1, source_target_pairs={{0,1},{1,0},{2,3},{3,2},{4,5},{5,4},{6,7},{7,6},{8,9},{9,8},{10,11... | collective-permute-start | bytes 1277960 | tf_op jit(solution)/shard_map/ppermute | solution.py:397
  26.8 9.2 %collective-permute-start.4 = (bf16[13,2,8192]{2,1,0:T(2,128)(2,1)S(1)}, bf16[13,2,8192]{2,1,0:T(2,128)(2,1)S(1)}, u32[]{:S(2)}, u32[]{:S(2)}) collective-permute-start(bf16[13,2,8192]{2,1,0:T(2,128)(2,1)S(1)} %get-tuple-element.20.refs_4_), channel_id=1, source_target_pairs={{0,1},{1,0},{2,3},{3,2},{4,5},{5,4},{6,7},{7,6},{8,9},{9,8},{10,11... | collective-permute-start | bytes 1277960 | tf_op jit(solution)/shard_map/ppermute | solution.py:402
  26.8 9.2 %collective-permute-start.8 = (bf16[13,2,8192]{2,1,0:T(2,128)(2,1)S(1)}, bf16[13,2,8192]{2,1,0:T(2,128)(2,1)S(1)}, u32[]{:S(2)}, u32[]{:S(2)}) collective-permute-start(bf16[13,2,8192]{2,1,0:T(2,128)(2,1)S(1)} %collective-permute-done.7.refs_8_), channel_id=1, source_target_pairs={{0,1},{1,0},{2,3},{3,2},{4,5},{5,4},{6,7},{7,6},{8,9},{9,8},{10,11... | collective-permute-start | bytes 1277960 | tf_op jit(solution)/shard_map/ppermute | solution.py:402
  32.4 12.3 %collective-permute-start.17 = (bf16[13,2,8192]{2,1,0:T(2,128)(2,1)S(1)}, bf16[13,2,8192]{2,1,0:T(2,128)(2,1)S(1)}, u32[]{:S(2)}, u32[]{:S(2)}) collective-permute-start(bf16[13,2,8192]{2,1,0:T(2,128)(2,1)S(1)} %collective-permute-done.13.refs_0_), channel_id=1, source_target_pairs={{0,4},{1,3},{2,0},{3,7},{4,8},{5,1},{6,2},{7,11},{8,12},{9,5},{10,... | collective-permute-start | bytes 1277960 | tf_op jit(solution)/shard_map/ppermute | solution.py:387
  34.5 10.8 %collective-permute-start.15 = (bf16[13,2,8192]{2,1,0:T(2,128)(2,1)S(1)}, bf16[13,2,8192]{2,1,0:T(2,128)(2,1)S(1)}, u32[]{:S(2)}, u32[]{:S(2)}) collective-permute-start(bf16[13,2,8192]{2,1,0:T(2,128)(2,1)S(1)} %collective-permute-done.7.refs_8_), channel_id=1, source_target_pairs={{0,4},{1,3},{2,0},{3,7},{4,8},{5,1},{6,2},{7,11},{8,12},{9,5},{10,... | collective-permute-start | bytes 1277960 | tf_op jit(solution)/shard_map/ppermute | solution.py:399
  36.0 12.5 %collective-permute-start.14 = (bf16[13,2,8192]{2,1,0:T(2,128)(2,1)S(1)}, bf16[13,2,8192]{2,1,0:T(2,128)(2,1)S(1)}, u32[]{:S(2)}, u32[]{:S(2)}) collective-permute-start(bf16[13,2,8192]{2,1,0:T(2,128)(2,1)S(1)} %collective-permute-done.13.refs_0_), channel_id=1, source_target_pairs={{0,1},{1,0},{2,3},{3,2},{4,5},{5,4},{6,7},{7,6},{8,9},{9,8},{10,11... | collective-permute-start | bytes 1277960 | tf_op jit(solution)/shard_map/ppermute | solution.py:397
  44.7 5.4 %collective-permute-start.18 = (bf16[13,2,8192]{2,1,0:T(2,128)(2,1)S(1)}, bf16[13,2,8192]{2,1,0:T(2,128)(2,1)S(1)}, u32[]{:S(2)}, u32[]{:S(2)}) collective-permute-start(bf16[13,2,8192]{2,1,0:T(2,128)(2,1)S(1)} %after.1.refs_4_), channel_id=1, source_target_pairs={{0,1},{1,0},{2,3},{3,2},{4,5},{5,4},{6,7},{7,6},{8,9},{9,8},{10,11... | collective-permute-start | bytes 1277960 | tf_op jit(solution)/shard_map/ppermute | solution.py:397
  45.3 5.1 %collective-permute-start.16 = (bf16[13,2,8192]{2,1,0:T(2,128)(2,1)S(1)}, bf16[13,2,8192]{2,1,0:T(2,128)(2,1)S(1)}, u32[]{:S(2)}, u32[]{:S(2)}) collective-permute-start(bf16[13,2,8192]{2,1,0:T(2,128)(2,1)S(1)} %collective-permute-done.15.refs_2_), channel_id=1, source_target_pairs={{0,1},{1,0},{2,3},{3,2},{4,5},{5,4},{6,7},{7,6},{8,9},{9,8},{10,11... | collective-permute-start | bytes 1277960 | tf_op jit(solution)/shard_map/ppermute | solution.py:402
  45.3 14.6 %collective-permute-start.10 = (bf16[2,29,2,512]{3,2,1,0:T(2,128)(2,1)S(1)}, bf16[2,29,2,512]{3,2,1,0:T(2,128)(2,1)S(1)}, u32[]{:S(2)}, u32[]{:S(2)}) collective-permute-start(bf16[2,29,2,512]{3,2,1,0:T(2,128)(2,1)S(1)} %get-tuple-element.27), channel_id=1, source_target_pairs={{0,4},{1,3},{2,0},{3,7},{4,8},{5,1},{6,2},{7,11},{8,12},{9,5},{10,... | collective-permute-start | bytes 356360 | tf_op jit(solution)/shard_map/ppermute | solution.py:380
  47.1 13.0 %collective-permute-start.11 = (bf16[2,29,2,512]{3,2,1,0:T(2,128)(2,1)S(1)}, bf16[2,29,2,512]{3,2,1,0:T(2,128)(2,1)S(1)}, u32[]{:S(2)}, u32[]{:S(2)}) collective-permute-start(bf16[2,29,2,512]{3,2,1,0:T(2,128)(2,1)S(1)} %get-tuple-element.28), channel_id=1, source_target_pairs={{0,6},{1,9},{2,10},{3,5},{4,2},{5,13},{6,14},{7,1},{8,0},{9,15},{1... | collective-permute-start | bytes 356360 | tf_op jit(solution)/shard_map/ppermute | solution.py:377
  48.6 16.3 %collective-permute-start.12 = (bf16[2,29,2,512]{3,2,1,0:T(2,128)(2,1)S(1)}, bf16[2,29,2,512]{3,2,1,0:T(2,128)(2,1)S(1)}, u32[]{:S(2)}, u32[]{:S(2)}) collective-permute-start(bf16[2,29,2,512]{3,2,1,0:T(2,128)(2,1)S(1)} %get-tuple-element.29), channel_id=1, source_target_pairs={{0,8},{1,7},{2,4},{3,11},{4,12},{5,3},{6,0},{7,15},{8,14},{9,1},{1... | collective-permute-start | bytes 356360 | tf_op jit(solution)/shard_map/ppermute | solution.py:380
  50.1 14.7 %collective-permute-start.9 = (bf16[2,29,2,512]{3,2,1,0:T(2,128)(2,1)S(1)}, bf16[2,29,2,512]{3,2,1,0:T(2,128)(2,1)S(1)}, u32[]{:S(2)}, u32[]{:S(2)}) collective-permute-start(bf16[2,29,2,512]{3,2,1,0:T(2,128)(2,1)S(1)} %get-tuple-element.26), channel_id=1, source_target_pairs={{0,2},{1,5},{2,6},{3,1},{4,0},{5,9},{6,10},{7,3},{8,4},{9,13},{10,... | collective-permute-start | bytes 356360 | tf_op jit(solution)/shard_map/ppermute | solution.py:377
  56.2 9.1 %collective-permute-start.20 = (bf16[2,29,2,512]{3,2,1,0:T(2,128)(2,1)S(1)}, bf16[2,29,2,512]{3,2,1,0:T(2,128)(2,1)S(1)}, u32[]{:S(2)}, u32[]{:S(2)}) collective-permute-start(bf16[2,29,2,512]{3,2,1,0:T(2,128)(2,1)S(1)} %get-tuple-element.30.refs_5_.refs_3_), channel_id=1, source_target_pairs={{0,10},{1,13},{2,14},{3,9},{4,6},{5,15},{6,12},{7,5},{8,2},{9,11},... | collective-permute-start | bytes 356360 | tf_op jit(solution)/shard_map/ppermute | solution.py:377
  60.0 11.9 %collective-permute-start.21 = (bf16[2,29,2,512]{3,2,1,0:T(2,128)(2,1)S(1)}, bf16[2,29,2,512]{3,2,1,0:T(2,128)(2,1)S(1)}, u32[]{:S(2)}, u32[]{:S(2)}) collective-permute-start(bf16[2,29,2,512]{3,2,1,0:T(2,128)(2,1)S(1)} %get-tuple-element.31), channel_id=1, source_target_pairs={{0,12},{1,11},{2,8},{3,15},{4,14},{5,7},{6,4},{7,13},{8,10},{9,3},... | collective-permute-start | bytes 356360 | tf_op jit(solution)/shard_map/ppermute | solution.py:380
  60.1 11.7 %collective-permute-start.22 = (bf16[2,29,2,512]{3,2,1,0:T(2,128)(2,1)S(1)}, bf16[2,29,2,512]{3,2,1,0:T(2,128)(2,1)S(1)}, u32[]{:S(2)}, u32[]{:S(2)}) collective-permute-start(bf16[2,29,2,512]{3,2,1,0:T(2,128)(2,1)S(1)} %get-tuple-element.32), channel_id=1, source_target_pairs={{0,14},{1,15},{2,12},{3,13},{4,10},{5,11},{6,8},{7,9},{8,6},{9,7},... | collective-permute-start | bytes 356360 | tf_op jit(solution)/shard_map/ppermute | solution.py:377
  65.2 8.3 %collective-permute-start.19 = (bf16[5,29,2,512]{3,2,1,0:T(2,128)(2,1)S(1)}, bf16[5,29,2,512]{3,2,1,0:T(2,128)(2,1)S(1)}, u32[]{:S(2)}, u32[]{:S(2)}) collective-permute-start(bf16[5,29,2,512]{3,2,1,0:T(2,128)(2,1)S(1)} %others.2), channel_id=1, source_target_pairs={{0,1},{1,0},{2,3},{3,2},{4,5},{5,4},{6,7},{7,6},{8,9},{9,8},{10,11... | collective-permute-start | bytes 890888 | tf_op jit(solution)/shard_map/ppermute | solution.py:409
  72.1 1.5 %collective-permute-start.23 = (bf16[3,29,2,512]{3,2,1,0:T(2,128)(2,1)S(1)}, bf16[3,29,2,512]{3,2,1,0:T(2,128)(2,1)S(1)}, u32[]{:S(2)}, u32[]{:S(2)}) collective-permute-start(bf16[3,29,2,512]{3,2,1,0:T(2,128)(2,1)S(1)} %others.3), channel_id=1, source_target_pairs={{0,1},{1,0},{2,3},{3,2},{4,5},{5,4},{6,7},{7,6},{8,9},{9,8},{10,11... | collective-permute-start | bytes 534536 | tf_op jit(solution)/shard_map/ppermute | solution.py:409
  (4 other events, 45.4 us)

commit v3 on v2

--- a/solution.py
+++ b/solution.py
@@ -151,7 +151,9 @@
     )(x, *before)
 
 
-def block_products(sources, start, row_place, blocks, places, weights, rank, owner_count):
+def block_products(
+    sources, start, row_place, blocks, places, weights, rank, owner_count, before
+):
     base_weight, down, up = weights
     count = len(blocks)
     results = 1 + max(result for result, _ in places)
@@ -170,7 +172,7 @@
         me = lax.axis_index("owner")
         block_refs = refs[:count]
         w_ref, d_ref, u_ref = refs[count : count + 3]
-        out_refs = refs[count + 3 :][:results]
+        out_refs = refs[count + 3 + len(before) :][:results]
         x_ref, code_ref = refs[-2:]
         for b in range(count):
             x_ref[padded * b : padded * b + rows] = block_refs[b][...].reshape(rows, width)
@@ -186,6 +188,14 @@
                 preferred_element_type=jnp.float32,
             )
         low = low.astype(jnp.bfloat16)
+        base = jnp.zeros((padded * count, columns), jnp.float32)
+        for part in range(parts):
+            at = part * depth
+            base += jnp.dot(
+                x_ref[:, at : at + depth],
+                w_ref[at : at + depth, :],
+                preferred_element_type=jnp.float32,
+            )
         code_ref[...] = jnp.full_like(code_ref, -1)
         for b in range(count):
             code_ref[:, padded * b : padded * b + rows] = (
@@ -202,14 +212,6 @@
         for a in range(adapters):
             chosen = jnp.where(adapter == a, found[takes * a : takes * (a + 1)], chosen)
         chosen = chosen.astype(jnp.bfloat16)
-        base = jnp.zeros((padded * count, columns), jnp.float32)
-        for part in range(parts):
-            at = part * depth
-            base += jnp.dot(
-                x_ref[:, at : at + depth],
-                w_ref[at : at + depth, :],
-                preferred_element_type=jnp.float32,
-            )
         for b, (result, place) in enumerate(places):
             out_refs[result][place, :pairs] = (
                 base[padded * b : padded * b + rows]
@@ -231,7 +233,7 @@
             jax.ShapeDtypeStruct((2, pairs + owner_count, 2, columns), jnp.bfloat16)
             for _ in range(results)
         ],
-        in_specs=[SMEM] + [VMEM] * (count + 4),
+        in_specs=[SMEM] + [VMEM] * (count + 4) + [ANY] * len(before),
         out_specs=[VMEM] * results,
         scratch_shapes=[
             pltpu.VMEM((padded * count, width), jnp.bfloat16),
@@ -244,7 +246,7 @@
             transcendentals=0,
         ),
         name="block_products",
-    )(sources, row_place, *blocks, base_weight, down, up)
+    )(sources, row_place, *blocks, base_weight, down, up, *before)
 
 
 def others(received, before):
@@ -359,7 +361,7 @@
     held = [None] * 3
     received = []
 
-    def products(hops, start):
+    def products(hops, start, before):
         blocks, places, result = [], [], 0
         for hop in hops:
             blocks += groups[hop]
@@ -370,7 +372,7 @@
                 places += [(result, 0), (result, 1)]
                 result += 1
         out = block_products(
-            block_from, start, row_place, blocks, places, held, rank, owner_count
+            block_from, start, row_place, blocks, places, held, rank, owner_count, before
         )
         came, at = [], 0
         for hop in hops:
@@ -391,7 +393,7 @@
             held[2], first = hold(up, first, [])
         if hops == last and len(split) > 1:
             for early in split[:-1]:
-                count, made = products(early, done)
+                count, made = products(early, done, [second])
                 done += count
             first = after(first, [made])
         group = [first, send(first, perm=swap)]
@@ -403,7 +405,7 @@
         groups.append(group)
     if held[1] is None:
         held[1], row_place = hold(down, row_place, [], turn=True)
-    _, made = products(split[-1], done)
+    _, made = products(split[-1], done, [])
     arrays = []
     for came in received:
         passed = send(others(came, [made]), perm=swap)

time: 76.4 us -> 73.4 us (0.961)
  Pallas kernels: 26.7 us -> 22.9 us
  waiting for transfers between devices: 16.8 us -> 18 us
    pallas_call x2, Pallas kernels: 14.4 us -> 10.7 us  [block_products(): pl.pallas_call(kernel, out_shape=[jax.ShapeDtypeStruct((2, pairs + owner_...]
    ppermute x4, starting transfers between devices: 10.2 us -> 13.5 us  [products(): came.append(send(out[at], perm=turned(-hop)) if hop else out[at])]
    ppermute x3, starting transfers between devices: 3.46 us -> 0.31 us  [products(): came.append(send(out[at], perm=turned(hop)))]
    ppermute x3, waiting for transfers between devices: 0.01 us -> 2.48 us  [per_device(): second = send(second, perm=turned(1))]
    ppermute x4, waiting for transfers between devices: 8.83 us -> 7.56 us  [per_device(): first = send(first, perm=turned(1))]
    ppermute x4, starting transfers between devices: 1.07 us -> 0.08 us  [per_device(): group = [first, send(first, perm=swap)]]
  transfers between devices with their start and end apart: 24 -> 24, of which waited for: 5 -> 6; matrix products, arithmetic and copies ran while one was open for 1% -> 1% of each run, Pallas kernels for 32% -> 28%
where the time goes in v3:
time: 73.4 us; the launch traced here: 73.2 us
  starting transfers between devices  29.7 us (40%)
  Pallas kernels  22.9 us (31%)
  waiting for transfers between devices  18 us (25%)
  local copies, waits for them, and re-layouts  2.47 us (3%)
    ppermute x4, starting transfers between devices, products(): came.append(send(out[at], perm=turned(-hop)) if hop else out[at])  13.5 us
    pallas_call x2, Pallas kernels, block_products(): pl.pallas_call(kernel, out_shape=[jax.ShapeDtypeStruct((2, pairs + owner_...  10.7 us
    ppermute x4, starting transfers between devices, per_device(): first = send(first, perm=turned(1))  8.97 us
    pallas_call x3, Pallas kernels, hold(): pl.pallas_call(kernel, out_shape=[pltpu.VMEM(shape, weight.dtype), jax.Sh...  8.35 us
    ppermute x4, waiting for transfers between devices, per_device(): first = send(first, perm=turned(1))  7.56 us
    ppermute x3, waiting for transfers between devices, products(): came.append(send(out[at], perm=turned(hop)))  6.54 us
    ppermute x3, starting transfers between devices, per_device(): second = send(second, perm=turned(1))  5.11 us
    ppermute x3, waiting for transfers between devices, per_device(): second = send(second, perm=turned(1))  2.48 us
  transfers between devices with their start and end apart: 24, of which 6 were waited for; matrix products, arithmetic and copies ran while one was open for 1% of the time, Pallas kernels for 28%

profile of v3, /device:TPU:0, one launch (start us, length us, event | category | flops | bytes accessed | tf_op | source)
XLA Modules:
  0.0 73.2 jit_solution(15598132923224101026)
XLA Ops:
  0.0 1.0 %copy-done = bf16[26,8192]{1,0:T(8,128)(2,1)S(1)} copy-done((bf16[26,8192]{1,0:T(8,128)(2,1)S(1)}, bf16[26,8192]{1,0:T(8,128)(2,1)}, u32[]{:S(2)}) %copy-start) | copy-done | bytes 426008
  1.6 2.6 %collective-permute-start.1 = (bf16[13,2,8192]{2,1,0:T(2,128)(2,1)S(1)}, bf16[13,2,8192]{2,1,0:T(2,128)(2,1)S(1)}, u32[]{:S(2)}, u32[]{:S(2)}) collective-permute-start(bf16[13,2,8192]{2,1,0:T(2,128)(2,1)S(1)} %pair_rows.1.refs_0_), channel_id=1, source_target_pairs={{0,4},{1,3},{2,0},{3,7},{4,8},{5,1},{6,2},{7,11},{8,12},{9,5},{10,... | collective-permute-start | bytes 1277960 | tf_op jit(solution)/shard_map/ppermute | solution.py:389
  4.3 1.7 %collective-permute-start.3 = (bf16[13,2,8192]{2,1,0:T(2,128)(2,1)S(1)}, bf16[13,2,8192]{2,1,0:T(2,128)(2,1)S(1)}, u32[]{:S(2)}, u32[]{:S(2)}) collective-permute-start(bf16[13,2,8192]{2,1,0:T(2,128)(2,1)S(1)} %collective-permute-done.refs_1_), channel_id=1, source_target_pairs={{0,4},{1,3},{2,0},{3,7},{4,8},{5,1},{6,2},{7,11},{8,12},{9,5},{10,... | collective-permute-start | bytes 1277960 | tf_op jit(solution)/shard_map/ppermute | solution.py:401
  8.2 2.1 %collective-permute-done.1.refs_1_ = bf16[13,2,8192]{2,1,0:T(2,128)(2,1)S(1)} collective-permute-done((bf16[13,2,8192]{2,1,0:T(2,128)(2,1)S(1)}, bf16[13,2,8192]{2,1,0:T(2,128)(2,1)S(1)}, u32[]{:S(2)}, u32[]{:S(2)}) %collective-permute-start.1) | collective-permute-done | bytes 426016 | tf_op jit(solution)/shard_map/ppermute | solution.py:389
  10.3 3.5 %hold.3 = (bf16[8192,512]{1,0:T(8,128)(2,1)S(1)}, bf16[13,2,8192]{2,1,0:T(2,128)(2,1)S(1)}) custom-call(bf16[8192,512]{1,0:T(8,128)(2,1)} %refs_0_.1, bf16[13,2,8192]{2,1,0:T(2,128)(2,1)S(1)} %collective-permute-done.1.refs_1_, s32[16,26]{1,0:T(8,128)S(1)} %row_places.1.refs_2_.place_ref), custom_call_target="tpu_custom_call", output_to_operand_aliasing={{1}: (1, {})} | custom-call | tf_op jit(solution)/shard_map/hold/pallas_call | solution.py:123
  13.8 2.1 %collective-permute-start.5 = (bf16[13,2,8192]{2,1,0:T(2,128)(2,1)S(1)}, bf16[13,2,8192]{2,1,0:T(2,128)(2,1)S(1)}, u32[]{:S(2)}, u32[]{:S(2)}) collective-permute-start(bf16[13,2,8192]{2,1,0:T(2,128)(2,1)S(1)} %get-tuple-element.19.refs_2_), channel_id=1, source_target_pairs={{0,4},{1,3},{2,0},{3,7},{4,8},{5,1},{6,2},{7,11},{8,12},{9,5},{10,... | collective-permute-start | bytes 1277960 | tf_op jit(solution)/shard_map/ppermute | solution.py:389
  15.9 2.7 %hold.4 = (bf16[8192,256]{1,0:T(8,128)(2,1)S(1)}, bf16[13,2,8192]{2,1,0:T(2,128)(2,1)S(1)}) custom-call(bf16[256,8192]{1,0:T(8,128)(2,1)} %bitcast.7, bf16[13,2,8192]{2,1,0:T(2,128)(2,1)S(1)} %collective-permute-done.3.refs_1_), custom_call_target="tpu_custom_call", output_to_operand_aliasing={{1}: (1, {})} | custom-call | tf_op jit(solution)/shard_map/hold/pallas_call | solution.py:123
  18.6 1.6 %collective-permute-start.7 = (bf16[13,2,8192]{2,1,0:T(2,128)(2,1)S(1)}, bf16[13,2,8192]{2,1,0:T(2,128)(2,1)S(1)}, u32[]{:S(2)}, u32[]{:S(2)}) collective-permute-start(bf16[13,2,8192]{2,1,0:T(2,128)(2,1)S(1)} %get-tuple-element.20.refs_4_), channel_id=1, source_target_pairs={{0,4},{1,3},{2,0},{3,7},{4,8},{5,1},{6,2},{7,11},{8,12},{9,5},{10,... | collective-permute-start | bytes 1277960 | tf_op jit(solution)/shard_map/ppermute | solution.py:401
  20.2 1.7 %collective-permute-done.5.refs_1_ = bf16[13,2,8192]{2,1,0:T(2,128)(2,1)S(1)} collective-permute-done((bf16[13,2,8192]{2,1,0:T(2,128)(2,1)S(1)}, bf16[13,2,8192]{2,1,0:T(2,128)(2,1)S(1)}, u32[]{:S(2)}, u32[]{:S(2)}) %collective-permute-start.5) | collective-permute-done | bytes 426016 | tf_op jit(solution)/shard_map/ppermute | solution.py:389
  22.0 2.2 %hold.5 = (bf16[256,8192]{1,0:T(8,128)(2,1)S(1)}, bf16[13,2,8192]{2,1,0:T(2,128)(2,1)S(1)}) custom-call(bf16[256,8192]{1,0:T(8,128)(2,1)} %bitcast.8, bf16[13,2,8192]{2,1,0:T(2,128)(2,1)S(1)} %collective-permute-done.5.refs_1_), custom_call_target="tpu_custom_call", output_to_operand_aliasing={{1}: (1, {})} | custom-call | tf_op jit(solution)/shard_map/hold/pallas_call | solution.py:123
  24.2 2.1 %collective-permute-start.14 = (bf16[13,2,8192]{2,1,0:T(2,128)(2,1)S(1)}, bf16[13,2,8192]{2,1,0:T(2,128)(2,1)S(1)}, u32[]{:S(2)}, u32[]{:S(2)}) collective-permute-start(bf16[13,2,8192]{2,1,0:T(2,128)(2,1)S(1)} %get-tuple-element.21.refs_6_), channel_id=1, source_target_pairs={{0,4},{1,3},{2,0},{3,7},{4,8},{5,1},{6,2},{7,11},{8,12},{9,5},{10,... | collective-permute-start | bytes 1277960 | tf_op jit(solution)/shard_map/ppermute | solution.py:389
  26.8 1.8 %collective-permute-start.9 = (bf16[13,2,8192]{2,1,0:T(2,128)(2,1)S(1)}, bf16[13,2,8192]{2,1,0:T(2,128)(2,1)S(1)}, u32[]{:S(2)}, u32[]{:S(2)}) collective-permute-start(bf16[13,2,8192]{2,1,0:T(2,128)(2,1)S(1)} %collective-permute-done.7.refs_8_), channel_id=1, source_target_pairs={{0,4},{1,3},{2,0},{3,7},{4,8},{5,1},{6,2},{7,11},{8,12},{9,5},{10,... | collective-permute-start | bytes 1277960 | tf_op jit(solution)/shard_map/ppermute | solution.py:401
  28.6 3.8 %collective-permute-done.14.refs_0_ = bf16[13,2,8192]{2,1,0:T(2,128)(2,1)S(1)} collective-permute-done((bf16[13,2,8192]{2,1,0:T(2,128)(2,1)S(1)}, bf16[13,2,8192]{2,1,0:T(2,128)(2,1)S(1)}, u32[]{:S(2)}, u32[]{:S(2)}) %collective-permute-start.14) | collective-permute-done | bytes 426016 | tf_op jit(solution)/shard_map/ppermute | solution.py:389
  32.4 2.1 %collective-permute-start.17 = (bf16[13,2,8192]{2,1,0:T(2,128)(2,1)S(1)}, bf16[13,2,8192]{2,1,0:T(2,128)(2,1)S(1)}, u32[]{:S(2)}, u32[]{:S(2)}) collective-permute-start(bf16[13,2,8192]{2,1,0:T(2,128)(2,1)S(1)} %collective-permute-done.14.refs_0_), channel_id=1, source_target_pairs={{0,4},{1,3},{2,0},{3,7},{4,8},{5,1},{6,2},{7,11},{8,12},{9,5},{10,... | collective-permute-start | bytes 1277960 | tf_op jit(solution)/shard_map/ppermute | solution.py:389
  34.5 2.5 %collective-permute-done.9.refs_13_.refs_2_ = bf16[13,2,8192]{2,1,0:T(2,128)(2,1)S(1)} collective-permute-done((bf16[13,2,8192]{2,1,0:T(2,128)(2,1)S(1)}, bf16[13,2,8192]{2,1,0:T(2,128)(2,1)S(1)}, u32[]{:S(2)}, u32[]{:S(2)}) %collective-permute-start.9) | collective-permute-done | bytes 426016 | tf_op jit(solution)/shard_map/ppermute | solution.py:401
  36.9 6.2 %block_products.2 = (bf16[2,29,2,512]{3,2,1,0:T(2,128)(2,1)S(1)}, bf16[2,29,2,512]{3,2,1,0:T(2,128)(2,1)S(1)}, bf16[2,29,2,512]{3,2,1,0:T(2,128)(2,1)S(1)}, bf16...) custom-call(s32[16,16]{1,0:T(8,128)S(1)} %copy-done.1, s32[16,26]{1,0:T(8,128)S(1)} %row_places.1.refs_2_.place_ref, ...), custom_call_target="tpu_custom_call" | custom-call | flops 4026531840 | bytes 16777216 | tf_op jit(solution)/shard_map/block_products/pallas_call | solution.py:230
  43.8 2.0 %collective-permute-start.10 = (bf16[2,29,2,512]{3,2,1,0:T(2,128)(2,1)S(1)}, bf16[2,29,2,512]{3,2,1,0:T(2,128)(2,1)S(1)}, u32[]{:S(2)}, u32[]{:S(2)}) collective-permute-start(bf16[2,29,2,512]{3,2,1,0:T(2,128)(2,1)S(1)} %get-tuple-element.26), channel_id=1, source_target_pairs={{0,2},{1,5},{2,6},{3,1},{4,0},{5,9},{6,10},{7,3},{8,4},{9,13},{10,... | collective-permute-start | bytes 356360 | tf_op jit(solution)/shard_map/ppermute | solution.py:379
  45.9 3.0 %collective-permute-start.12 = (bf16[2,29,2,512]{3,2,1,0:T(2,128)(2,1)S(1)}, bf16[2,29,2,512]{3,2,1,0:T(2,128)(2,1)S(1)}, u32[]{:S(2)}, u32[]{:S(2)}) collective-permute-start(bf16[2,29,2,512]{3,2,1,0:T(2,128)(2,1)S(1)} %get-tuple-element.28), channel_id=1, source_target_pairs={{0,6},{1,9},{2,10},{3,5},{4,2},{5,13},{6,14},{7,1},{8,0},{9,15},{1... | collective-permute-start | bytes 356360 | tf_op jit(solution)/shard_map/ppermute | solution.py:379
  49.0 4.4 %block_products.3 = (bf16[2,29,2,512]{3,2,1,0:T(2,128)(2,1)S(1)}, bf16[2,29,2,512]{3,2,1,0:T(2,128)(2,1)S(1)}, bf16[2,29,2,512]{3,2,1,0:T(2,128)(2,1)S(1)}) custom-call(s32[16,16]{1,0:T(8,128)S(1)} %copy-done.1, s32[16,26]{1,0:T(8,128)S(1)} %row_places.1.refs_2_.place_ref, bf16[13,2,8192]{2,1,0:T(2,128)(2,1)S(1)} %collective-permute-done.14.refs_0_, ...), custom_call_target="tpu_custom_call" | custom-call | flops 2415919104 | bytes 16777216 | tf_op jit(solution)/shard_map/block_products/pallas_call | solution.py:230
  53.4 3.8 %collective-permute-start.20 = (bf16[2,29,2,512]{3,2,1,0:T(2,128)(2,1)S(1)}, bf16[2,29,2,512]{3,2,1,0:T(2,128)(2,1)S(1)}, u32[]{:S(2)}, u32[]{:S(2)}) collective-permute-start(bf16[2,29,2,512]{3,2,1,0:T(2,128)(2,1)S(1)} %get-tuple-element.30.refs_5_.refs_3_), channel_id=1, source_target_pairs={{0,10},{1,13},{2,14},{3,9},{4,6},{5,15},{6,12},{7,5},{8,2},{9,11},... | collective-permute-start | bytes 356360 | tf_op jit(solution)/shard_map/ppermute | solution.py:379
  57.4 4.7 %collective-permute-start.22 = (bf16[2,29,2,512]{3,2,1,0:T(2,128)(2,1)S(1)}, bf16[2,29,2,512]{3,2,1,0:T(2,128)(2,1)S(1)}, u32[]{:S(2)}, u32[]{:S(2)}) collective-permute-start(bf16[2,29,2,512]{3,2,1,0:T(2,128)(2,1)S(1)} %get-tuple-element.32), channel_id=1, source_target_pairs={{0,14},{1,15},{2,12},{3,13},{4,10},{5,11},{6,8},{7,9},{8,6},{9,7},... | collective-permute-start | bytes 356360 | tf_op jit(solution)/shard_map/ppermute | solution.py:379
  62.6 6.5 %collective-permute-done.21.refs_1_.refs_7_ = bf16[2,29,2,512]{3,2,1,0:T(2,128)(2,1)S(1)} collective-permute-done((bf16[2,29,2,512]{3,2,1,0:T(2,128)(2,1)S(1)}, bf16[2,29,2,512]{3,2,1,0:T(2,128)(2,1)S(1)}, u32[]{:S(2)}, u32[]{:S(2)}) %collective-permute-start.21) | collective-permute-done | bytes 118816 | tf_op jit(solution)/shard_map/ppermute | solution.py:382
  69.5 1.4 %collective-permute-done.23.refs_9_ = bf16[3,29,2,512]{3,2,1,0:T(2,128)(2,1)S(1)} collective-permute-done((bf16[3,29,2,512]{3,2,1,0:T(2,128)(2,1)S(1)}, bf16[3,29,2,512]{3,2,1,0:T(2,128)(2,1)S(1)}, u32[]{:S(2)}, u32[]{:S(2)}) %collective-permute-start.23) | collective-permute-done | bytes 178208 | tf_op jit(solution)/shard_map/ppermute | solution.py:411
  70.9 2.3 %assemble.1 = bf16[26,8192]{1,0:T(8,128)(2,1)} custom-call(s32[16,16]{1,0:T(8,128)S(1)} %copy-done.2, s32[16,26]{1,0:T(8,128)S(1)} %row_places.1.refs_2_.place_ref, bf16[2,29,2,512]{3,2,1,0:T(2,128)(2,1)S(1)} %get-tuple-element.25.refs_1_.refs_0_, bf16[2,29,2,512]{3,2,1,0:T(2,128)(2,1)S(1)} %collective-permute-done.10.refs_1_, ...), custom_call_target="tpu_custom_call" | custom-call | tf_op jit(solution)/shard_map/assemble/pallas_call | solution.py:317
  (44 shorter events, 5.1 us)
Async XLA Ops:
  1.1 3.2 %collective-permute-start = (bf16[13,2,8192]{2,1,0:T(2,128)(2,1)S(1)}, bf16[13,2,8192]{2,1,0:T(2,128)(2,1)S(1)}, u32[]{:S(2)}, u32[]{:S(2)}) collective-permute-start(bf16[13,2,8192]{2,1,0:T(2,128)(2,1)S(1)} %pair_rows.1.refs_0_), channel_id=1, source_target_pairs={{0,1},{1,0},{2,3},{3,2},{4,5},{5,4},{6,7},{7,6},{8,9},{9,8},{10,11... | collective-permute-start | bytes 1277960 | tf_op jit(solution)/shard_map/ppermute | solution.py:359
  1.6 8.7 %collective-permute-start.1 = (bf16[13,2,8192]{2,1,0:T(2,128)(2,1)S(1)}, bf16[13,2,8192]{2,1,0:T(2,128)(2,1)S(1)}, u32[]{:S(2)}, u32[]{:S(2)}) collective-permute-start(bf16[13,2,8192]{2,1,0:T(2,128)(2,1)S(1)} %pair_rows.1.refs_0_), channel_id=1, source_target_pairs={{0,4},{1,3},{2,0},{3,7},{4,8},{5,1},{6,2},{7,11},{8,12},{9,5},{10,... | collective-permute-start | bytes 1277960 | tf_op jit(solution)/shard_map/ppermute | solution.py:389
  4.3 11.7 %collective-permute-start.3 = (bf16[13,2,8192]{2,1,0:T(2,128)(2,1)S(1)}, bf16[13,2,8192]{2,1,0:T(2,128)(2,1)S(1)}, u32[]{:S(2)}, u32[]{:S(2)}) collective-permute-start(bf16[13,2,8192]{2,1,0:T(2,128)(2,1)S(1)} %collective-permute-done.refs_1_), channel_id=1, source_target_pairs={{0,4},{1,3},{2,0},{3,7},{4,8},{5,1},{6,2},{7,11},{8,12},{9,5},{10,... | collective-permute-start | bytes 1277960 | tf_op jit(solution)/shard_map/ppermute | solution.py:401
  13.8 8.2 %collective-permute-start.5 = (bf16[13,2,8192]{2,1,0:T(2,128)(2,1)S(1)}, bf16[13,2,8192]{2,1,0:T(2,128)(2,1)S(1)}, u32[]{:S(2)}, u32[]{:S(2)}) collective-permute-start(bf16[13,2,8192]{2,1,0:T(2,128)(2,1)S(1)} %get-tuple-element.19.refs_2_), channel_id=1, source_target_pairs={{0,4},{1,3},{2,0},{3,7},{4,8},{5,1},{6,2},{7,11},{8,12},{9,5},{10,... | collective-permute-start | bytes 1277960 | tf_op jit(solution)/shard_map/ppermute | solution.py:389
  18.6 8.2 %collective-permute-start.7 = (bf16[13,2,8192]{2,1,0:T(2,128)(2,1)S(1)}, bf16[13,2,8192]{2,1,0:T(2,128)(2,1)S(1)}, u32[]{:S(2)}, u32[]{:S(2)}) collective-permute-start(bf16[13,2,8192]{2,1,0:T(2,128)(2,1)S(1)} %get-tuple-element.20.refs_4_), channel_id=1, source_target_pairs={{0,4},{1,3},{2,0},{3,7},{4,8},{5,1},{6,2},{7,11},{8,12},{9,5},{10,... | collective-permute-start | bytes 1277960 | tf_op jit(solution)/shard_map/ppermute | solution.py:401
  20.2 8.4 %collective-permute-start.2 = (bf16[13,2,8192]{2,1,0:T(2,128)(2,1)S(1)}, bf16[13,2,8192]{2,1,0:T(2,128)(2,1)S(1)}, u32[]{:S(2)}, u32[]{:S(2)}) collective-permute-start(bf16[13,2,8192]{2,1,0:T(2,128)(2,1)S(1)} %get-tuple-element.19.refs_2_), channel_id=1, source_target_pairs={{0,1},{1,0},{2,3},{3,2},{4,5},{5,4},{6,7},{7,6},{8,9},{9,8},{10,11... | collective-permute-start | bytes 1277960 | tf_op jit(solution)/shard_map/ppermute | solution.py:399
  24.2 8.2 %collective-permute-start.14 = (bf16[13,2,8192]{2,1,0:T(2,128)(2,1)S(1)}, bf16[13,2,8192]{2,1,0:T(2,128)(2,1)S(1)}, u32[]{:S(2)}, u32[]{:S(2)}) collective-permute-start(bf16[13,2,8192]{2,1,0:T(2,128)(2,1)S(1)} %get-tuple-element.21.refs_6_), channel_id=1, source_target_pairs={{0,4},{1,3},{2,0},{3,7},{4,8},{5,1},{6,2},{7,11},{8,12},{9,5},{10,... | collective-permute-start | bytes 1277960 | tf_op jit(solution)/shard_map/ppermute | solution.py:389
  26.3 8.1 %collective-permute-start.6 = (bf16[13,2,8192]{2,1,0:T(2,128)(2,1)S(1)}, bf16[13,2,8192]{2,1,0:T(2,128)(2,1)S(1)}, u32[]{:S(2)}, u32[]{:S(2)}) collective-permute-start(bf16[13,2,8192]{2,1,0:T(2,128)(2,1)S(1)} %get-tuple-element.21.refs_6_), channel_id=1, source_target_pairs={{0,1},{1,0},{2,3},{3,2},{4,5},{5,4},{6,7},{7,6},{8,9},{9,8},{10,11... | collective-permute-start | bytes 1277960 | tf_op jit(solution)/shard_map/ppermute | solution.py:399
  26.3 8.1 %collective-permute-start.4 = (bf16[13,2,8192]{2,1,0:T(2,128)(2,1)S(1)}, bf16[13,2,8192]{2,1,0:T(2,128)(2,1)S(1)}, u32[]{:S(2)}, u32[]{:S(2)}) collective-permute-start(bf16[13,2,8192]{2,1,0:T(2,128)(2,1)S(1)} %get-tuple-element.20.refs_4_), channel_id=1, source_target_pairs={{0,1},{1,0},{2,3},{3,2},{4,5},{5,4},{6,7},{7,6},{8,9},{9,8},{10,11... | collective-permute-start | bytes 1277960 | tf_op jit(solution)/shard_map/ppermute | solution.py:404
  26.8 10.1 %collective-permute-start.9 = (bf16[13,2,8192]{2,1,0:T(2,128)(2,1)S(1)}, bf16[13,2,8192]{2,1,0:T(2,128)(2,1)S(1)}, u32[]{:S(2)}, u32[]{:S(2)}) collective-permute-start(bf16[13,2,8192]{2,1,0:T(2,128)(2,1)S(1)} %collective-permute-done.7.refs_8_), channel_id=1, source_target_pairs={{0,4},{1,3},{2,0},{3,7},{4,8},{5,1},{6,2},{7,11},{8,12},{9,5},{10,... | collective-permute-start | bytes 1277960 | tf_op jit(solution)/shard_map/ppermute | solution.py:401
  28.6 8.3 %collective-permute-start.8 = (bf16[13,2,8192]{2,1,0:T(2,128)(2,1)S(1)}, bf16[13,2,8192]{2,1,0:T(2,128)(2,1)S(1)}, u32[]{:S(2)}, u32[]{:S(2)}) collective-permute-start(bf16[13,2,8192]{2,1,0:T(2,128)(2,1)S(1)} %collective-permute-done.7.refs_8_), channel_id=1, source_target_pairs={{0,1},{1,0},{2,3},{3,2},{4,5},{5,4},{6,7},{7,6},{8,9},{9,8},{10,11... | collective-permute-start | bytes 1277960 | tf_op jit(solution)/shard_map/ppermute | solution.py:404
  32.4 10.8 %collective-permute-start.17 = (bf16[13,2,8192]{2,1,0:T(2,128)(2,1)S(1)}, bf16[13,2,8192]{2,1,0:T(2,128)(2,1)S(1)}, u32[]{:S(2)}, u32[]{:S(2)}) collective-permute-start(bf16[13,2,8192]{2,1,0:T(2,128)(2,1)S(1)} %collective-permute-done.14.refs_0_), channel_id=1, source_target_pairs={{0,4},{1,3},{2,0},{3,7},{4,8},{5,1},{6,2},{7,11},{8,12},{9,5},{10,... | collective-permute-start | bytes 1277960 | tf_op jit(solution)/shard_map/ppermute | solution.py:389
  34.5 11.4 %collective-permute-start.15 = (bf16[13,2,8192]{2,1,0:T(2,128)(2,1)S(1)}, bf16[13,2,8192]{2,1,0:T(2,128)(2,1)S(1)}, u32[]{:S(2)}, u32[]{:S(2)}) collective-permute-start(bf16[13,2,8192]{2,1,0:T(2,128)(2,1)S(1)} %collective-permute-done.14.refs_0_), channel_id=1, source_target_pairs={{0,1},{1,0},{2,3},{3,2},{4,5},{5,4},{6,7},{7,6},{8,9},{9,8},{10,11... | collective-permute-start | bytes 1277960 | tf_op jit(solution)/shard_map/ppermute | solution.py:399
  43.2 5.6 %collective-permute-start.18 = (bf16[13,2,8192]{2,1,0:T(2,128)(2,1)S(1)}, bf16[13,2,8192]{2,1,0:T(2,128)(2,1)S(1)}, u32[]{:S(2)}, u32[]{:S(2)}) collective-permute-start(bf16[13,2,8192]{2,1,0:T(2,128)(2,1)S(1)} %after.1.refs_4_), channel_id=1, source_target_pairs={{0,1},{1,0},{2,3},{3,2},{4,5},{5,4},{6,7},{7,6},{8,9},{9,8},{10,11... | collective-permute-start | bytes 1277960 | tf_op jit(solution)/shard_map/ppermute | solution.py:399
  43.3 5.7 %collective-permute-start.16 = (bf16[13,2,8192]{2,1,0:T(2,128)(2,1)S(1)}, bf16[13,2,8192]{2,1,0:T(2,128)(2,1)S(1)}, u32[]{:S(2)}, u32[]{:S(2)}) collective-permute-start(bf16[13,2,8192]{2,1,0:T(2,128)(2,1)S(1)} %collective-permute-done.9.refs_13_.refs_2_), channel_id=1, source_target_pairs={{0,1},{1,0},{2,3},{3,2},{4,5},{5,4},{6,7},{7,6},{8,9},{9,8},{10,11... | collective-permute-start | bytes 1277960 | tf_op jit(solution)/shard_map/ppermute | solution.py:404
  43.8 13.5 %collective-permute-start.10 = (bf16[2,29,2,512]{3,2,1,0:T(2,128)(2,1)S(1)}, bf16[2,29,2,512]{3,2,1,0:T(2,128)(2,1)S(1)}, u32[]{:S(2)}, u32[]{:S(2)}) collective-permute-start(bf16[2,29,2,512]{3,2,1,0:T(2,128)(2,1)S(1)} %get-tuple-element.26), channel_id=1, source_target_pairs={{0,2},{1,5},{2,6},{3,1},{4,0},{5,9},{6,10},{7,3},{8,4},{9,13},{10,... | collective-permute-start | bytes 356360 | tf_op jit(solution)/shard_map/ppermute | solution.py:379
  45.8 11.6 %collective-permute-start.11 = (bf16[2,29,2,512]{3,2,1,0:T(2,128)(2,1)S(1)}, bf16[2,29,2,512]{3,2,1,0:T(2,128)(2,1)S(1)}, u32[]{:S(2)}, u32[]{:S(2)}) collective-permute-start(bf16[2,29,2,512]{3,2,1,0:T(2,128)(2,1)S(1)} %get-tuple-element.27), channel_id=1, source_target_pairs={{0,4},{1,3},{2,0},{3,7},{4,8},{5,1},{6,2},{7,11},{8,12},{9,5},{10,... | collective-permute-start | bytes 356360 | tf_op jit(solution)/shard_map/ppermute | solution.py:382
  45.9 16.2 %collective-permute-start.12 = (bf16[2,29,2,512]{3,2,1,0:T(2,128)(2,1)S(1)}, bf16[2,29,2,512]{3,2,1,0:T(2,128)(2,1)S(1)}, u32[]{:S(2)}, u32[]{:S(2)}) collective-permute-start(bf16[2,29,2,512]{3,2,1,0:T(2,128)(2,1)S(1)} %get-tuple-element.28), channel_id=1, source_target_pairs={{0,6},{1,9},{2,10},{3,5},{4,2},{5,13},{6,14},{7,1},{8,0},{9,15},{1... | collective-permute-start | bytes 356360 | tf_op jit(solution)/shard_map/ppermute | solution.py:379
  48.8 13.3 %collective-permute-start.13 = (bf16[2,29,2,512]{3,2,1,0:T(2,128)(2,1)S(1)}, bf16[2,29,2,512]{3,2,1,0:T(2,128)(2,1)S(1)}, u32[]{:S(2)}, u32[]{:S(2)}) collective-permute-start(bf16[2,29,2,512]{3,2,1,0:T(2,128)(2,1)S(1)} %get-tuple-element.29), channel_id=1, source_target_pairs={{0,8},{1,7},{2,4},{3,11},{4,12},{5,3},{6,0},{7,15},{8,14},{9,1},{1... | collective-permute-start | bytes 356360 | tf_op jit(solution)/shard_map/ppermute | solution.py:382
  53.4 9.2 %collective-permute-start.20 = (bf16[2,29,2,512]{3,2,1,0:T(2,128)(2,1)S(1)}, bf16[2,29,2,512]{3,2,1,0:T(2,128)(2,1)S(1)}, u32[]{:S(2)}, u32[]{:S(2)}) collective-permute-start(bf16[2,29,2,512]{3,2,1,0:T(2,128)(2,1)S(1)} %get-tuple-element.30.refs_5_.refs_3_), channel_id=1, source_target_pairs={{0,10},{1,13},{2,14},{3,9},{4,6},{5,15},{6,12},{7,5},{8,2},{9,11},... | collective-permute-start | bytes 356360 | tf_op jit(solution)/shard_map/ppermute | solution.py:379
  57.3 11.9 %collective-permute-start.21 = (bf16[2,29,2,512]{3,2,1,0:T(2,128)(2,1)S(1)}, bf16[2,29,2,512]{3,2,1,0:T(2,128)(2,1)S(1)}, u32[]{:S(2)}, u32[]{:S(2)}) collective-permute-start(bf16[2,29,2,512]{3,2,1,0:T(2,128)(2,1)S(1)} %get-tuple-element.31), channel_id=1, source_target_pairs={{0,12},{1,11},{2,8},{3,15},{4,14},{5,7},{6,4},{7,13},{8,10},{9,3},... | collective-permute-start | bytes 356360 | tf_op jit(solution)/shard_map/ppermute | solution.py:382
  57.4 11.8 %collective-permute-start.22 = (bf16[2,29,2,512]{3,2,1,0:T(2,128)(2,1)S(1)}, bf16[2,29,2,512]{3,2,1,0:T(2,128)(2,1)S(1)}, u32[]{:S(2)}, u32[]{:S(2)}) collective-permute-start(bf16[2,29,2,512]{3,2,1,0:T(2,128)(2,1)S(1)} %get-tuple-element.32), channel_id=1, source_target_pairs={{0,14},{1,15},{2,12},{3,13},{4,10},{5,11},{6,8},{7,9},{8,6},{9,7},... | collective-permute-start | bytes 356360 | tf_op jit(solution)/shard_map/ppermute | solution.py:379
  62.5 8.4 %collective-permute-start.19 = (bf16[5,29,2,512]{3,2,1,0:T(2,128)(2,1)S(1)}, bf16[5,29,2,512]{3,2,1,0:T(2,128)(2,1)S(1)}, u32[]{:S(2)}, u32[]{:S(2)}) collective-permute-start(bf16[5,29,2,512]{3,2,1,0:T(2,128)(2,1)S(1)} %others.2), channel_id=1, source_target_pairs={{0,1},{1,0},{2,3},{3,2},{4,5},{5,4},{6,7},{7,6},{8,9},{9,8},{10,11... | collective-permute-start | bytes 890888 | tf_op jit(solution)/shard_map/ppermute | solution.py:411
  69.4 1.5 %collective-permute-start.23 = (bf16[3,29,2,512]{3,2,1,0:T(2,128)(2,1)S(1)}, bf16[3,29,2,512]{3,2,1,0:T(2,128)(2,1)S(1)}, u32[]{:S(2)}, u32[]{:S(2)}) collective-permute-start(bf16[3,29,2,512]{3,2,1,0:T(2,128)(2,1)S(1)} %others.3), channel_id=1, source_target_pairs={{0,1},{1,0},{2,3},{3,2},{4,5},{5,4},{6,7},{7,6},{8,9},{9,8},{10,11... | collective-permute-start | bytes 534536 | tf_op jit(solution)/shard_map/ppermute | solution.py:411
  (4 other events, 44.8 us)

commit v4 on v3

--- a/solution.py
+++ b/solution.py
@@ -2,7 +2,6 @@
 
 import jax
 import jax.numpy as jnp
-import numpy as np
 from jax import lax
 from jax.experimental import pallas as pl
 from jax.experimental.pallas import tpu as pltpu
@@ -13,47 +12,51 @@
 adapter_scale = 0.5
 
 VMEM = pl.BlockSpec(memory_space=pltpu.VMEM)
-SMEM = pl.BlockSpec(memory_space=pltpu.SMEM)
 ANY = pl.BlockSpec(memory_space=pl.ANY)
 MIB = 1 << 20
 
 
-def ring_order(chips):
-    return list(range(0, chips, 2)) + list(range(1, chips, 2))[::-1]
+def on_ring(chips, at):
+    at = at % chips
+    out = 2 * at < chips
+    back = 2 * (chips - 1 - at) + 1
+    return jnp.where(out, 2 * at, back) if isinstance(at, jax.Array) else (2 * at if out else back)
+
+
+def ring_place(chips, chip):
+    back = chips - 1 - chip // 2
+    if isinstance(chip, jax.Array):
+        return jnp.where(chip % 2 == 0, chip // 2, back)
+    return back if chip % 2 else chip // 2
+
+
+def device_of(chips, me, what):
+    hops, same = what
+    chip, core = me // 2, me % 2
+    place = ring_place(chips, chip) + hops * (2 * core - 1)
+    return 2 * on_ring(chips, place + chips) + (core if same else 1 - core)
 
 
 def ring_tables(owner_count):
     chips = owner_count // 2
-    order = ring_order(chips)
-    place = {chip: at for at, chip in enumerate(order)}
-
-    def beside(chip, hops):
-        return order[(place[chip] + hops) % chips]
+    devices = range(owner_count)
 
     def turned(hops):
-        return [
-            (2 * chip + core, 2 * beside(chip, -hops if core else hops) + core)
-            for chip in range(chips)
-            for core in range(2)
-        ]
-
-    swap = [(device, device ^ 1) for device in range(owner_count)]
-    sources = np.zeros((2, owner_count, owner_count), np.int32)
-    for device in range(owner_count):
-        chip, core = divmod(device, 2)
-        blocks, pieces = [device, device ^ 1], [[device, device ^ 1]]
-        for hops in range(1, chips // 2 + 1):
-            mine = 2 * beside(chip, hops if core else -hops)
-            mates = 2 * beside(chip, -hops if core else hops)
-            if 2 * hops < chips:
-                blocks += [mine + core, mates + 1 - core, mine + 1 - core, mates + core]
-                pieces += [[mates + core, mine + 1 - core], [mine + core, mates + 1 - core]]
-            else:
-                blocks += [mine + core, mates + 1 - core]
-                pieces += [[mine + core, mine + 1 - core]]
-        assert sorted(blocks) == sorted(sum(pieces, [])) == list(range(owner_count))
-        sources[0, device], sources[1, device] = blocks, sum(pieces, [])
-    return turned, swap, sources
+        return [(device, device_of(chips, device, (-hops, True))) for device in devices]
+
+    swap = [(device, device ^ 1) for device in devices]
+    blocks, pieces = [(0, True), (0, False)], [(0, True), (0, False)]
+    for hops in range(1, chips // 2 + 1):
+        if 2 * hops < chips:
+            blocks += [(hops, True), (-hops, False), (hops, False), (-hops, True)]
+            pieces += [(-hops, True), (hops, False), (hops, True), (-hops, False)]
+        else:
+            blocks += [(hops, True), (-hops, False)]
+            pieces += [(hops, True), (hops, False)]
+    for device in devices:
+        for what in (blocks, pieces):
+            assert sorted(device_of(chips, device, w) for w in what) == list(devices)
+    return turned, swap, blocks, pieces
 
 
 def pair_rows(x):
@@ -100,19 +103,22 @@
     )(row_adapter_index.reshape(1, total), adapter_storage_slot.reshape(slots, 1))
 
 
-def hold(weight, carry, before, turn=False):
+def hold(weight, carry, before, turn=False, half=None):
     shape = weight.shape[::-1] if turn else weight.shape
+    if half is not None:
+        shape = (shape[0] // 2, shape[1])
     parts = 8
 
     def kernel(*refs):
         src, dst, sem = refs[0], refs[2 + len(before)], refs[-1]
         landing = refs[-2] if turn else dst
         copies = []
-        size = weight.shape[1 if turn else 0] // parts
+        size = shape[0] // parts
         spans = [pl.ds(part * size, size) for part in range(parts)]
         for part, span in enumerate(spans):
             at = (slice(None), span) if turn else (span,)
-            copies.append(pltpu.make_async_copy(src.at[at], landing.at[at], sem.at[part]))
+            of = (pl.ds(half * shape[0] + part * size, size),) if half else at
+            copies.append(pltpu.make_async_copy(src.at[of], landing.at[at], sem.at[part]))
         for copy in copies:
             copy.start()
         for copy, span in zip(copies, spans):
@@ -152,27 +158,27 @@
 
 
 def block_products(
-    sources, start, row_place, blocks, places, weights, rank, owner_count, before
+    sources, row_place, blocks, places, weights, rank, owner_count, before
 ):
-    base_weight, down, up = weights
+    base_low, base_high, down, up = weights
     count = len(blocks)
     results = 1 + max(result for result, _ in places)
     pairs, _, width = blocks[0].shape
     rows = 2 * pairs
     padded = -(-rows // ROW_PAD) * ROW_PAD
-    columns = base_weight.shape[1]
+    columns = base_low.shape[1]
     ranks = down.shape[1]
-    depth = min(width, 1024)
+    depth = min(width // 2, 1024)
     parts = width // depth
     adapters = ranks // rank
     taken = OWNER_ROW_LIMIT * adapters
     takes = -(-OWNER_ROW_LIMIT * count // 8) * 8
 
-    def kernel(src_ref, place_ref, *refs):
+    def kernel(place_ref, *refs):
         me = lax.axis_index("owner")
         block_refs = refs[:count]
-        w_ref, d_ref, u_ref = refs[count : count + 3]
-        out_refs = refs[count + 3 + len(before) :][:results]
+        *w_refs, d_ref, u_ref = refs[count : count + 4]
+        out_refs = refs[count + 4 + len(before) :][:results]
         x_ref, code_ref = refs[-2:]
         for b in range(count):
             x_ref[padded * b : padded * b + rows] = block_refs[b][...].reshape(rows, width)
@@ -193,13 +199,13 @@
             at = part * depth
             base += jnp.dot(
                 x_ref[:, at : at + depth],
-                w_ref[at : at + depth, :],
+                w_refs[2 * part // parts][at % (width // 2) : at % (width // 2) + depth, :],
                 preferred_element_type=jnp.float32,
             )
         code_ref[...] = jnp.full_like(code_ref, -1)
         for b in range(count):
             code_ref[:, padded * b : padded * b + rows] = (
-                place_ref[pl.ds(src_ref[me, start + b], 1), :] - me * taken
+                place_ref[pl.ds(device_of(owner_count // 2, me, sources[b]), 1), :] - me * taken
             )
         row = lax.broadcasted_iota(jnp.int32, (adapters * takes, padded * count), 0)
         lane = lax.broadcasted_iota(jnp.int32, (adapters * takes, padded * count), 1)
@@ -233,7 +239,7 @@
             jax.ShapeDtypeStruct((2, pairs + owner_count, 2, columns), jnp.bfloat16)
             for _ in range(results)
         ],
-        in_specs=[SMEM] + [VMEM] * (count + 4) + [ANY] * len(before),
+        in_specs=[VMEM] * (count + 5) + [ANY] * len(before),
         out_specs=[VMEM] * results,
         scratch_shapes=[
             pltpu.VMEM((padded * count, width), jnp.bfloat16),
@@ -246,7 +252,7 @@
             transcendentals=0,
         ),
         name="block_products",
-    )(sources, row_place, *blocks, base_weight, down, up, *before)
+    )(row_place, *blocks, base_low, base_high, down, up, *before)
 
 
 def others(received, before):
@@ -281,16 +287,13 @@
     columns = arrays[0].shape[-1]
     slots = OWNER_ROW_LIMIT * count
 
-    def kernel(src_ref, place_ref, *refs):
+    def kernel(place_ref, *refs):
         me = lax.axis_index("owner")
-        o_ref, delta_ref, sem = refs[-3:]
+        source = [device_of(count // 2, me, what) for what in sources]
+        o_ref, delta_ref, row_ref, out_sem = refs[-4:]
         piece_refs = [refs[i].at[at] for i, at in at_of]
-        copies = [
-            pltpu.make_async_copy(ref.at[pl.ds(pairs, count)], delta_ref.at[:, a], sem.at[a])
-            for a, ref in enumerate(piece_refs)
-        ]
-        for copy in copies:
-            copy.start()
+        for a, ref in enumerate(piece_refs):
+            delta_ref[:, a] = ref[pairs:]
         place = place_ref[pl.ds(me, 1), :]
         owner = place // (adapters * OWNER_ROW_LIMIT)
         place = place % OWNER_ROW_LIMIT
@@ -299,33 +302,37 @@
         match = jnp.zeros((slots, rows), jnp.float32)
         for a in range(count):
             match = jnp.where(
-                (piece == a) & (owner == src_ref[me, a]) & (place == second), 1.0, match
+                (piece == a) & (owner == source[a]) & (place == second), 1.0, match
             )
         pick = match.T.astype(jnp.bfloat16)
-        for copy in copies:
-            copy.wait()
+        outs = []
         for a, ref in enumerate(piece_refs):
             delta = jnp.dot(
                 pick,
-                delta_ref[src_ref[me, a]].reshape(slots, columns),
+                delta_ref[source[a]].reshape(slots, columns),
                 preferred_element_type=jnp.float32,
             )
             base = ref[:pairs].reshape(rows, columns).astype(jnp.float32)
-            span = pl.ds(pl.multiple_of(src_ref[me, a] * columns, columns), columns)
-            o_ref[:, span] = (base + adapter_scale * delta).astype(o_ref.dtype)
+            row_ref[a] = (base + adapter_scale * delta).astype(row_ref.dtype)
+            span = pl.ds(pl.multiple_of(source[a] * columns, columns), columns)
+            outs.append(pltpu.make_async_copy(row_ref.at[a], o_ref.at[:, span], out_sem.at[a]))
+            outs[-1].start()
+        for copy in outs:
+            copy.wait()
 
     return pl.pallas_call(
         kernel,
         out_shape=jax.ShapeDtypeStruct((rows, count * columns), jnp.bfloat16),
-        in_specs=[SMEM] + [VMEM] * (len(arrays) + 1),
-        out_specs=VMEM,
+        in_specs=[VMEM] * (len(arrays) + 1),
+        out_specs=ANY,
         scratch_shapes=[
             pltpu.VMEM((count, count, 2, columns), jnp.bfloat16),
+            pltpu.VMEM((count, rows, columns), jnp.bfloat16),
             pltpu.SemaphoreType.DMA((count,)),
         ],
         compiler_params=pltpu.CompilerParams(vmem_limit_bytes=16 * MIB),
         name="assemble",
-    )(sources, row_place, *arrays)
+    )(row_place, *arrays)
 
 
 def per_device(
@@ -334,7 +341,7 @@
     owner_count = lax.axis_size("owner")
     rows, width = states.shape
     adapters, rank = down_weight.shape[0], down_weight.shape[2]
-    turned, swap, sources = ring_tables(owner_count)
+    turned, swap, block_from, piece_from = ring_tables(owner_count)
     send = functools.partial(lax.ppermute, axis_name="owner")
 
     down = down_weight.transpose(0, 2, 1).reshape(adapters * rank, width)
@@ -350,7 +357,7 @@
         came = sum(2 if 0 < 2 * hop < chips else 1 for hop in hops)
         order += [at + 2 * i for i in range(came)] + [at + 2 * i + 1 for i in range(came)]
         at += 2 * came
-    block_from, piece_from = jnp.asarray(sources[0]), jnp.asarray(sources[1][:, order])
+    piece_from = [piece_from[i] for i in order]
 
     base_weight, down, up = (
         pltpu.with_memory_space_constraint(w, pltpu.HBM) for w in (base_weight, down, up)
@@ -358,7 +365,7 @@
     own = pair_rows(states)
     first, second = own, send(own, perm=swap)
     groups = [[first, second]]
-    held = [None] * 3
+    held = [None] * 4
     received = []
 
     def products(hops, start, before):
@@ -372,7 +379,14 @@
                 places += [(result, 0), (result, 1)]
                 result += 1
         out = block_products(
-            block_from, start, row_place, blocks, places, held, rank, owner_count, before
+            block_from[start : start + len(blocks)],
+            row_place,
+            blocks,
+            places,
+            held,
+            rank,
+            owner_count,
+            before,
         )
         came, at = [], 0
         for hop in hops:
@@ -388,9 +402,9 @@
     for hops in range(1, last + 1):
         first = send(first, perm=turned(1))
         if hops == 1:
-            held[0], first = hold(base_weight, first, [row_place])
-        if hops == min(2, last):
-            held[2], first = hold(up, first, [])
+            held[0], first = hold(base_weight, first, [row_place], half=0)
+        if hops == 2:
+            held[3], first = hold(up, first, [])
         if hops == last and len(split) > 1:
             for early in split[:-1]:
                 count, made = products(early, done, [second])
@@ -400,11 +414,16 @@
         if 2 * hops < chips:
             second = send(second, perm=turned(1))
             if hops == 1:
-                held[1], second = hold(down, second, [], turn=True)
+                held[1], second = hold(base_weight, second, [], half=1)
+            if hops == 2:
+                held[2], second = hold(down, second, [], turn=True)
             group += [second, send(second, perm=swap)]
         groups.append(group)
-    if held[1] is None:
-        held[1], row_place = hold(down, row_place, [], turn=True)
+    for i, (weight, how) in enumerate(
+        [(base_weight, dict(half=0)), (base_weight, dict(half=1)), (down, dict(turn=True)), (up, {})]
+    ):
+        if held[i] is None:
+            held[i], row_place = hold(weight, row_place, [], **how)
     _, made = products(split[-1], done, [])
     arrays = []
     for came in received:

time: 73.4 us -> 70.3 us (0.958)
  waiting for transfers between devices: 18 us -> 15.9 us
  Pallas kernels: 22.9 us -> 21.6 us
    ppermute x4, waiting for transfers between devices: 7.56 us -> 4.6 us  [per_device(): first = send(first, perm=turned(1))]
    pallas_call x2, Pallas kernels: 10.7 us -> 9.42 us  [block_products(): pl.pallas_call(kernel, out_shape=[jax.ShapeDtypeStruct((2, pairs + owner_...]
    pallas_call x1, Pallas kernels: 2.32 us -> 1.36 us  [assemble(): pl.pallas_call(kernel, out_shape=jax.ShapeDtypeStruct((rows, count * colu...]
    ppermute x3, waiting for transfers between devices: 2.48 us -> 3.42 us  [per_device(): second = send(second, perm=turned(1))]
    pallas_call x3 -> x4, Pallas kernels: 8.35 us -> 9.29 us  [hold(): pl.pallas_call(kernel, out_shape=[pltpu.VMEM(shape, weight.dtype), jax.Sh...]
    unnamed x8 -> x4, local copies, waits for them, and re-layouts: 1.73 us -> 1.72 us
  transfers between devices with their start and end apart: 24 -> 24, of which waited for: 6 -> 7; matrix products, arithmetic and copies ran while one was open for 1% -> 1% of each run, Pallas kernels for 28% -> 29%
where the time goes in v4:
time: 70.3 us; the launch traced here: 70.1 us
  starting transfers between devices  29.9 us (43%)
  Pallas kernels  21.6 us (31%)
  waiting for transfers between devices  15.9 us (23%)
  local copies, waits for them, and re-layouts  2.47 us (4%)
    ppermute x4, starting transfers between devices, products(): came.append(send(out[at], perm=turned(-hop)) if hop else out[at])  12.9 us
    pallas_call x2, Pallas kernels, block_products(): pl.pallas_call(kernel, out_shape=[jax.ShapeDtypeStruct((2, pairs + owner_...  9.42 us
    pallas_call x4, Pallas kernels, hold(): pl.pallas_call(kernel, out_shape=[pltpu.VMEM(shape, weight.dtype), jax.Sh...  9.29 us
    ppermute x4, starting transfers between devices, per_device(): first = send(first, perm=turned(1))  8.97 us
    ppermute x3, waiting for transfers between devices, products(): came.append(send(out[at], perm=turned(hop)))  6.48 us
    ppermute x3, starting transfers between devices, per_device(): second = send(second, perm=turned(1))  5.66 us
    ppermute x4, waiting for transfers between devices, per_device(): first = send(first, perm=turned(1))  4.6 us
    ppermute x3, waiting for transfers between devices, per_device(): second = send(second, perm=turned(1))  3.42 us
  transfers between devices with their start and end apart: 24, of which 7 were waited for; matrix products, arithmetic and copies ran while one was open for 1% of the time, Pallas kernels for 29%

profile of v4, /device:TPU:0, one launch (start us, length us, event | category | flops | bytes accessed | tf_op | source)
XLA Modules:
  0.0 70.1 jit_solution(4510664310226997938)
XLA Ops:
  1.6 2.6 %collective-permute-start.1 = (bf16[13,2,8192]{2,1,0:T(2,128)(2,1)S(1)}, bf16[13,2,8192]{2,1,0:T(2,128)(2,1)S(1)}, u32[]{:S(2)}, u32[]{:S(2)}) collective-permute-start(bf16[13,2,8192]{2,1,0:T(2,128)(2,1)S(1)} %pair_rows.1.refs_0_), channel_id=1, source_target_pairs={{0,4},{1,3},{2,0},{3,7},{4,8},{5,1},{6,2},{7,11},{8,12},{9,5},{10,... | collective-permute-start | bytes 1277960 | tf_op jit(solution)/shard_map/ppermute | solution.py:403
  4.3 1.7 %collective-permute-start.3 = (bf16[13,2,8192]{2,1,0:T(2,128)(2,1)S(1)}, bf16[13,2,8192]{2,1,0:T(2,128)(2,1)S(1)}, u32[]{:S(2)}, u32[]{:S(2)}) collective-permute-start(bf16[13,2,8192]{2,1,0:T(2,128)(2,1)S(1)} %collective-permute-done.refs_1_), channel_id=1, source_target_pairs={{0,4},{1,3},{2,0},{3,7},{4,8},{5,1},{6,2},{7,11},{8,12},{9,5},{10,... | collective-permute-start | bytes 1277960 | tf_op jit(solution)/shard_map/ppermute | solution.py:415
  8.2 2.1 %collective-permute-done.1.refs_1_ = bf16[13,2,8192]{2,1,0:T(2,128)(2,1)S(1)} collective-permute-done((bf16[13,2,8192]{2,1,0:T(2,128)(2,1)S(1)}, bf16[13,2,8192]{2,1,0:T(2,128)(2,1)S(1)}, u32[]{:S(2)}, u32[]{:S(2)}) %collective-permute-start.1) | collective-permute-done | bytes 426016 | tf_op jit(solution)/shard_map/ppermute | solution.py:403
  10.3 2.2 %hold.4 = (bf16[4096,512]{1,0:T(8,128)(2,1)S(1)}, bf16[13,2,8192]{2,1,0:T(2,128)(2,1)S(1)}) custom-call(bf16[8192,512]{1,0:T(8,128)(2,1)} %refs_0_.3, bf16[13,2,8192]{2,1,0:T(2,128)(2,1)S(1)} %collective-permute-done.1.refs_1_, s32[16,26]{1,0:T(8,128)S(1)} %row_places.1.refs_2_.place_ref), custom_call_target="tpu_custom_call", output_to_operand_aliasing={{1}: (1, {})} | custom-call | tf_op jit(solution)/shard_map/hold/pallas_call | solution.py:129
  12.5 2.1 %collective-permute-start.5 = (bf16[13,2,8192]{2,1,0:T(2,128)(2,1)S(1)}, bf16[13,2,8192]{2,1,0:T(2,128)(2,1)S(1)}, u32[]{:S(2)}, u32[]{:S(2)}) collective-permute-start(bf16[13,2,8192]{2,1,0:T(2,128)(2,1)S(1)} %get-tuple-element.21.refs_2_), channel_id=1, source_target_pairs={{0,4},{1,3},{2,0},{3,7},{4,8},{5,1},{6,2},{7,11},{8,12},{9,5},{10,... | collective-permute-start | bytes 1277960 | tf_op jit(solution)/shard_map/ppermute | solution.py:403
  14.9 2.2 %hold.5 = (bf16[4096,512]{1,0:T(8,128)(2,1)S(1)}, bf16[13,2,8192]{2,1,0:T(2,128)(2,1)S(1)}) custom-call(bf16[8192,512]{1,0:T(8,128)(2,1)} %refs_0_.3, bf16[13,2,8192]{2,1,0:T(2,128)(2,1)S(1)} %collective-permute-done.3.refs_1_), custom_call_target="tpu_custom_call", output_to_operand_aliasing={{1}: (1, {})} | custom-call | tf_op jit(solution)/shard_map/hold/pallas_call | solution.py:129
  17.1 2.1 %collective-permute-start.7 = (bf16[13,2,8192]{2,1,0:T(2,128)(2,1)S(1)}, bf16[13,2,8192]{2,1,0:T(2,128)(2,1)S(1)}, u32[]{:S(2)}, u32[]{:S(2)}) collective-permute-start(bf16[13,2,8192]{2,1,0:T(2,128)(2,1)S(1)} %get-tuple-element.22.refs_4_), channel_id=1, source_target_pairs={{0,4},{1,3},{2,0},{3,7},{4,8},{5,1},{6,2},{7,11},{8,12},{9,5},{10,... | collective-permute-start | bytes 1277960 | tf_op jit(solution)/shard_map/ppermute | solution.py:415
  19.2 1.5 %collective-permute-done.5.refs_1_ = bf16[13,2,8192]{2,1,0:T(2,128)(2,1)S(1)} collective-permute-done((bf16[13,2,8192]{2,1,0:T(2,128)(2,1)S(1)}, bf16[13,2,8192]{2,1,0:T(2,128)(2,1)S(1)}, u32[]{:S(2)}, u32[]{:S(2)}) %collective-permute-start.5) | collective-permute-done | bytes 426016 | tf_op jit(solution)/shard_map/ppermute | solution.py:403
  20.7 2.2 %hold.6 = (bf16[256,8192]{1,0:T(8,128)(2,1)S(1)}, bf16[13,2,8192]{2,1,0:T(2,128)(2,1)S(1)}) custom-call(bf16[256,8192]{1,0:T(8,128)(2,1)} %bitcast.7, bf16[13,2,8192]{2,1,0:T(2,128)(2,1)S(1)} %collective-permute-done.5.refs_1_), custom_call_target="tpu_custom_call", output_to_operand_aliasing={{1}: (1, {})} | custom-call | tf_op jit(solution)/shard_map/hold/pallas_call | solution.py:129
  22.9 2.1 %collective-permute-start.14 = (bf16[13,2,8192]{2,1,0:T(2,128)(2,1)S(1)}, bf16[13,2,8192]{2,1,0:T(2,128)(2,1)S(1)}, u32[]{:S(2)}, u32[]{:S(2)}) collective-permute-start(bf16[13,2,8192]{2,1,0:T(2,128)(2,1)S(1)} %get-tuple-element.23.refs_6_), channel_id=1, source_target_pairs={{0,4},{1,3},{2,0},{3,7},{4,8},{5,1},{6,2},{7,11},{8,12},{9,5},{10,... | collective-permute-start | bytes 1277960 | tf_op jit(solution)/shard_map/ppermute | solution.py:403
  25.6 2.6 %hold.7 = (bf16[8192,256]{1,0:T(8,128)(2,1)S(1)}, bf16[13,2,8192]{2,1,0:T(2,128)(2,1)S(1)}) custom-call(bf16[256,8192]{1,0:T(8,128)(2,1)} %bitcast.8, bf16[13,2,8192]{2,1,0:T(2,128)(2,1)S(1)} %collective-permute-done.7.refs_1_), custom_call_target="tpu_custom_call", output_to_operand_aliasing={{1}: (1, {})} | custom-call | tf_op jit(solution)/shard_map/hold/pallas_call | solution.py:129
  28.2 1.8 %collective-permute-start.9 = (bf16[13,2,8192]{2,1,0:T(2,128)(2,1)S(1)}, bf16[13,2,8192]{2,1,0:T(2,128)(2,1)S(1)}, u32[]{:S(2)}, u32[]{:S(2)}) collective-permute-start(bf16[13,2,8192]{2,1,0:T(2,128)(2,1)S(1)} %get-tuple-element.24.refs_8_), channel_id=1, source_target_pairs={{0,4},{1,3},{2,0},{3,7},{4,8},{5,1},{6,2},{7,11},{8,12},{9,5},{10,... | collective-permute-start | bytes 1277960 | tf_op jit(solution)/shard_map/ppermute | solution.py:415
  30.1 1.0 %collective-permute-done.14.refs_0_ = bf16[13,2,8192]{2,1,0:T(2,128)(2,1)S(1)} collective-permute-done((bf16[13,2,8192]{2,1,0:T(2,128)(2,1)S(1)}, bf16[13,2,8192]{2,1,0:T(2,128)(2,1)S(1)}, u32[]{:S(2)}, u32[]{:S(2)}) %collective-permute-start.14) | collective-permute-done | bytes 426016 | tf_op jit(solution)/shard_map/ppermute | solution.py:403
  31.1 2.1 %collective-permute-start.17 = (bf16[13,2,8192]{2,1,0:T(2,128)(2,1)S(1)}, bf16[13,2,8192]{2,1,0:T(2,128)(2,1)S(1)}, u32[]{:S(2)}, u32[]{:S(2)}) collective-permute-start(bf16[13,2,8192]{2,1,0:T(2,128)(2,1)S(1)} %collective-permute-done.14.refs_0_), channel_id=1, source_target_pairs={{0,4},{1,3},{2,0},{3,7},{4,8},{5,1},{6,2},{7,11},{8,12},{9,5},{10,... | collective-permute-start | bytes 1277960 | tf_op jit(solution)/shard_map/ppermute | solution.py:403
  33.2 3.2 %collective-permute-done.9.refs_14_.refs_2_ = bf16[13,2,8192]{2,1,0:T(2,128)(2,1)S(1)} collective-permute-done((bf16[13,2,8192]{2,1,0:T(2,128)(2,1)S(1)}, bf16[13,2,8192]{2,1,0:T(2,128)(2,1)S(1)}, u32[]{:S(2)}, u32[]{:S(2)}) %collective-permute-start.9) | collective-permute-done | bytes 426016 | tf_op jit(solution)/shard_map/ppermute | solution.py:415
  36.4 5.6 %block_products.2 = (bf16[2,29,2,512]{3,2,1,0:T(2,128)(2,1)S(1)}, bf16[2,29,2,512]{3,2,1,0:T(2,128)(2,1)S(1)}, bf16[2,29,2,512]{3,2,1,0:T(2,128)(2,1)S(1)}, bf16...) custom-call(s32[16,26]{1,0:T(8,128)S(1)} %row_places.1.refs_2_.place_ref, ...), custom_call_target="tpu_custom_call" | custom-call | flops 4026531840 | bytes 16777216 | tf_op jit(solution)/shard_map/block_products/pallas_call | solution.py:236
  42.7 1.7 %collective-permute-start.10 = (bf16[2,29,2,512]{3,2,1,0:T(2,128)(2,1)S(1)}, bf16[2,29,2,512]{3,2,1,0:T(2,128)(2,1)S(1)}, u32[]{:S(2)}, u32[]{:S(2)}) collective-permute-start(bf16[2,29,2,512]{3,2,1,0:T(2,128)(2,1)S(1)} %get-tuple-element.30), channel_id=1, source_target_pairs={{0,2},{1,5},{2,6},{3,1},{4,0},{5,9},{6,10},{7,3},{8,4},{9,13},{10,... | collective-permute-start | bytes 356360 | tf_op jit(solution)/shard_map/ppermute | solution.py:393
  44.7 2.7 %collective-permute-start.12 = (bf16[2,29,2,512]{3,2,1,0:T(2,128)(2,1)S(1)}, bf16[2,29,2,512]{3,2,1,0:T(2,128)(2,1)S(1)}, u32[]{:S(2)}, u32[]{:S(2)}) collective-permute-start(bf16[2,29,2,512]{3,2,1,0:T(2,128)(2,1)S(1)} %get-tuple-element.32), channel_id=1, source_target_pairs={{0,6},{1,9},{2,10},{3,5},{4,2},{5,13},{6,14},{7,1},{8,0},{9,15},{1... | collective-permute-start | bytes 356360 | tf_op jit(solution)/shard_map/ppermute | solution.py:393
  47.6 3.8 %block_products.3 = (bf16[2,29,2,512]{3,2,1,0:T(2,128)(2,1)S(1)}, bf16[2,29,2,512]{3,2,1,0:T(2,128)(2,1)S(1)}, bf16[2,29,2,512]{3,2,1,0:T(2,128)(2,1)S(1)}) custom-call(s32[16,26]{1,0:T(8,128)S(1)} %row_places.1.refs_2_.place_ref, bf16[13,2,8192]{2,1,0:T(2,128)(2,1)S(1)} %collective-permute-done.14.refs_0_, ...), custom_call_target="tpu_custom_call" | custom-call | flops 2415919104 | bytes 16777216 | tf_op jit(solution)/shard_map/block_products/pallas_call | solution.py:236
  51.4 3.8 %collective-permute-start.20 = (bf16[2,29,2,512]{3,2,1,0:T(2,128)(2,1)S(1)}, bf16[2,29,2,512]{3,2,1,0:T(2,128)(2,1)S(1)}, u32[]{:S(2)}, u32[]{:S(2)}) collective-permute-start(bf16[2,29,2,512]{3,2,1,0:T(2,128)(2,1)S(1)} %get-tuple-element.34.refs_5_.refs_3_), channel_id=1, source_target_pairs={{0,10},{1,13},{2,14},{3,9},{4,6},{5,15},{6,12},{7,5},{8,2},{9,11},... | collective-permute-start | bytes 356360 | tf_op jit(solution)/shard_map/ppermute | solution.py:393
  55.3 4.7 %collective-permute-start.22 = (bf16[2,29,2,512]{3,2,1,0:T(2,128)(2,1)S(1)}, bf16[2,29,2,512]{3,2,1,0:T(2,128)(2,1)S(1)}, u32[]{:S(2)}, u32[]{:S(2)}) collective-permute-start(bf16[2,29,2,512]{3,2,1,0:T(2,128)(2,1)S(1)} %get-tuple-element.36), channel_id=1, source_target_pairs={{0,14},{1,15},{2,12},{3,13},{4,10},{5,11},{6,8},{7,9},{8,6},{9,7},... | collective-permute-start | bytes 356360 | tf_op jit(solution)/shard_map/ppermute | solution.py:393
  60.5 6.5 %collective-permute-done.21.refs_1_.refs_7_ = bf16[2,29,2,512]{3,2,1,0:T(2,128)(2,1)S(1)} collective-permute-done((bf16[2,29,2,512]{3,2,1,0:T(2,128)(2,1)S(1)}, bf16[2,29,2,512]{3,2,1,0:T(2,128)(2,1)S(1)}, u32[]{:S(2)}, u32[]{:S(2)}) %collective-permute-start.21) | collective-permute-done | bytes 118816 | tf_op jit(solution)/shard_map/ppermute | solution.py:396
  67.3 1.4 %collective-permute-done.23.refs_9_ = bf16[3,29,2,512]{3,2,1,0:T(2,128)(2,1)S(1)} collective-permute-done((bf16[3,29,2,512]{3,2,1,0:T(2,128)(2,1)S(1)}, bf16[3,29,2,512]{3,2,1,0:T(2,128)(2,1)S(1)}, u32[]{:S(2)}, u32[]{:S(2)}) %collective-permute-start.23) | collective-permute-done | bytes 178208 | tf_op jit(solution)/shard_map/ppermute | solution.py:430
  68.7 1.4 %assemble.1 = bf16[26,8192]{1,0:T(8,128)(2,1)} custom-call(s32[16,26]{1,0:T(8,128)S(1)} %row_places.1.refs_2_.place_ref, bf16[2,29,2,512]{3,2,1,0:T(2,128)(2,1)S(1)} %get-tuple-element.29.refs_1_.refs_0_, bf16[2,29,2,512]{3,2,1,0:T(2,128)(2,1)S(1)} %collective-permute-done.10.refs_1_, bf16[2,29,2,512]{3,2,1,0:T(2,128)(2,1)S(1)} %collective-permute-done.11.refs_2_, ...), custom_call_target="tpu_custom_call" | custom-call | tf_op jit(solution)/shard_map/assemble/pallas_call | solution.py:323
  (41 shorter events, 6.7 us)
Async XLA Ops:
  1.1 3.2 %collective-permute-start = (bf16[13,2,8192]{2,1,0:T(2,128)(2,1)S(1)}, bf16[13,2,8192]{2,1,0:T(2,128)(2,1)S(1)}, u32[]{:S(2)}, u32[]{:S(2)}) collective-permute-start(bf16[13,2,8192]{2,1,0:T(2,128)(2,1)S(1)} %pair_rows.1.refs_0_), channel_id=1, source_target_pairs={{0,1},{1,0},{2,3},{3,2},{4,5},{5,4},{6,7},{7,6},{8,9},{9,8},{10,11... | collective-permute-start | bytes 1277960 | tf_op jit(solution)/shard_map/ppermute | solution.py:366
  1.6 8.7 %collective-permute-start.1 = (bf16[13,2,8192]{2,1,0:T(2,128)(2,1)S(1)}, bf16[13,2,8192]{2,1,0:T(2,128)(2,1)S(1)}, u32[]{:S(2)}, u32[]{:S(2)}) collective-permute-start(bf16[13,2,8192]{2,1,0:T(2,128)(2,1)S(1)} %pair_rows.1.refs_0_), channel_id=1, source_target_pairs={{0,4},{1,3},{2,0},{3,7},{4,8},{5,1},{6,2},{7,11},{8,12},{9,5},{10,... | collective-permute-start | bytes 1277960 | tf_op jit(solution)/shard_map/ppermute | solution.py:403
  4.3 10.6 %collective-permute-start.3 = (bf16[13,2,8192]{2,1,0:T(2,128)(2,1)S(1)}, bf16[13,2,8192]{2,1,0:T(2,128)(2,1)S(1)}, u32[]{:S(2)}, u32[]{:S(2)}) collective-permute-start(bf16[13,2,8192]{2,1,0:T(2,128)(2,1)S(1)} %collective-permute-done.refs_1_), channel_id=1, source_target_pairs={{0,4},{1,3},{2,0},{3,7},{4,8},{5,1},{6,2},{7,11},{8,12},{9,5},{10,... | collective-permute-start | bytes 1277960 | tf_op jit(solution)/shard_map/ppermute | solution.py:415
  12.5 8.2 %collective-permute-start.5 = (bf16[13,2,8192]{2,1,0:T(2,128)(2,1)S(1)}, bf16[13,2,8192]{2,1,0:T(2,128)(2,1)S(1)}, u32[]{:S(2)}, u32[]{:S(2)}) collective-permute-start(bf16[13,2,8192]{2,1,0:T(2,128)(2,1)S(1)} %get-tuple-element.21.refs_2_), channel_id=1, source_target_pairs={{0,4},{1,3},{2,0},{3,7},{4,8},{5,1},{6,2},{7,11},{8,12},{9,5},{10,... | collective-permute-start | bytes 1277960 | tf_op jit(solution)/shard_map/ppermute | solution.py:403
  17.1 8.5 %collective-permute-start.7 = (bf16[13,2,8192]{2,1,0:T(2,128)(2,1)S(1)}, bf16[13,2,8192]{2,1,0:T(2,128)(2,1)S(1)}, u32[]{:S(2)}, u32[]{:S(2)}) collective-permute-start(bf16[13,2,8192]{2,1,0:T(2,128)(2,1)S(1)} %get-tuple-element.22.refs_4_), channel_id=1, source_target_pairs={{0,4},{1,3},{2,0},{3,7},{4,8},{5,1},{6,2},{7,11},{8,12},{9,5},{10,... | collective-permute-start | bytes 1277960 | tf_op jit(solution)/shard_map/ppermute | solution.py:415
  19.2 10.8 %collective-permute-start.2 = (bf16[13,2,8192]{2,1,0:T(2,128)(2,1)S(1)}, bf16[13,2,8192]{2,1,0:T(2,128)(2,1)S(1)}, u32[]{:S(2)}, u32[]{:S(2)}) collective-permute-start(bf16[13,2,8192]{2,1,0:T(2,128)(2,1)S(1)} %get-tuple-element.21.refs_2_), channel_id=1, source_target_pairs={{0,1},{1,0},{2,3},{3,2},{4,5},{5,4},{6,7},{7,6},{8,9},{9,8},{10,11... | collective-permute-start | bytes 1277960 | tf_op jit(solution)/shard_map/ppermute | solution.py:413
  22.9 8.2 %collective-permute-start.14 = (bf16[13,2,8192]{2,1,0:T(2,128)(2,1)S(1)}, bf16[13,2,8192]{2,1,0:T(2,128)(2,1)S(1)}, u32[]{:S(2)}, u32[]{:S(2)}) collective-permute-start(bf16[13,2,8192]{2,1,0:T(2,128)(2,1)S(1)} %get-tuple-element.23.refs_6_), channel_id=1, source_target_pairs={{0,4},{1,3},{2,0},{3,7},{4,8},{5,1},{6,2},{7,11},{8,12},{9,5},{10,... | collective-permute-start | bytes 1277960 | tf_op jit(solution)/shard_map/ppermute | solution.py:403
  25.1 8.1 %collective-permute-start.6 = (bf16[13,2,8192]{2,1,0:T(2,128)(2,1)S(1)}, bf16[13,2,8192]{2,1,0:T(2,128)(2,1)S(1)}, u32[]{:S(2)}, u32[]{:S(2)}) collective-permute-start(bf16[13,2,8192]{2,1,0:T(2,128)(2,1)S(1)} %get-tuple-element.23.refs_6_), channel_id=1, source_target_pairs={{0,1},{1,0},{2,3},{3,2},{4,5},{5,4},{6,7},{7,6},{8,9},{9,8},{10,11... | collective-permute-start | bytes 1277960 | tf_op jit(solution)/shard_map/ppermute | solution.py:413
  25.1 8.1 %collective-permute-start.4 = (bf16[13,2,8192]{2,1,0:T(2,128)(2,1)S(1)}, bf16[13,2,8192]{2,1,0:T(2,128)(2,1)S(1)}, u32[]{:S(2)}, u32[]{:S(2)}) collective-permute-start(bf16[13,2,8192]{2,1,0:T(2,128)(2,1)S(1)} %get-tuple-element.22.refs_4_), channel_id=1, source_target_pairs={{0,1},{1,0},{2,3},{3,2},{4,5},{5,4},{6,7},{7,6},{8,9},{9,8},{10,11... | collective-permute-start | bytes 1277960 | tf_op jit(solution)/shard_map/ppermute | solution.py:420
  28.2 8.2 %collective-permute-start.9 = (bf16[13,2,8192]{2,1,0:T(2,128)(2,1)S(1)}, bf16[13,2,8192]{2,1,0:T(2,128)(2,1)S(1)}, u32[]{:S(2)}, u32[]{:S(2)}) collective-permute-start(bf16[13,2,8192]{2,1,0:T(2,128)(2,1)S(1)} %get-tuple-element.24.refs_8_), channel_id=1, source_target_pairs={{0,4},{1,3},{2,0},{3,7},{4,8},{5,1},{6,2},{7,11},{8,12},{9,5},{10,... | collective-permute-start | bytes 1277960 | tf_op jit(solution)/shard_map/ppermute | solution.py:415
  30.1 6.4 %collective-permute-start.8 = (bf16[13,2,8192]{2,1,0:T(2,128)(2,1)S(1)}, bf16[13,2,8192]{2,1,0:T(2,128)(2,1)S(1)}, u32[]{:S(2)}, u32[]{:S(2)}) collective-permute-start(bf16[13,2,8192]{2,1,0:T(2,128)(2,1)S(1)} %get-tuple-element.24.refs_8_), channel_id=1, source_target_pairs={{0,1},{1,0},{2,3},{3,2},{4,5},{5,4},{6,7},{7,6},{8,9},{9,8},{10,11... | collective-permute-start | bytes 1277960 | tf_op jit(solution)/shard_map/ppermute | solution.py:420
  31.1 10.9 %collective-permute-start.17 = (bf16[13,2,8192]{2,1,0:T(2,128)(2,1)S(1)}, bf16[13,2,8192]{2,1,0:T(2,128)(2,1)S(1)}, u32[]{:S(2)}, u32[]{:S(2)}) collective-permute-start(bf16[13,2,8192]{2,1,0:T(2,128)(2,1)S(1)} %collective-permute-done.14.refs_0_), channel_id=1, source_target_pairs={{0,4},{1,3},{2,0},{3,7},{4,8},{5,1},{6,2},{7,11},{8,12},{9,5},{10,... | collective-permute-start | bytes 1277960 | tf_op jit(solution)/shard_map/ppermute | solution.py:403
  33.2 11.5 %collective-permute-start.15 = (bf16[13,2,8192]{2,1,0:T(2,128)(2,1)S(1)}, bf16[13,2,8192]{2,1,0:T(2,128)(2,1)S(1)}, u32[]{:S(2)}, u32[]{:S(2)}) collective-permute-start(bf16[13,2,8192]{2,1,0:T(2,128)(2,1)S(1)} %collective-permute-done.14.refs_0_), channel_id=1, source_target_pairs={{0,1},{1,0},{2,3},{3,2},{4,5},{5,4},{6,7},{7,6},{8,9},{9,8},{10,11... | collective-permute-start | bytes 1277960 | tf_op jit(solution)/shard_map/ppermute | solution.py:413
  42.1 5.3 %collective-permute-start.18 = (bf16[13,2,8192]{2,1,0:T(2,128)(2,1)S(1)}, bf16[13,2,8192]{2,1,0:T(2,128)(2,1)S(1)}, u32[]{:S(2)}, u32[]{:S(2)}) collective-permute-start(bf16[13,2,8192]{2,1,0:T(2,128)(2,1)S(1)} %after.1.refs_4_), channel_id=1, source_target_pairs={{0,1},{1,0},{2,3},{3,2},{4,5},{5,4},{6,7},{7,6},{8,9},{9,8},{10,11... | collective-permute-start | bytes 1277960 | tf_op jit(solution)/shard_map/ppermute | solution.py:413
  42.2 5.5 %collective-permute-start.16 = (bf16[13,2,8192]{2,1,0:T(2,128)(2,1)S(1)}, bf16[13,2,8192]{2,1,0:T(2,128)(2,1)S(1)}, u32[]{:S(2)}, u32[]{:S(2)}) collective-permute-start(bf16[13,2,8192]{2,1,0:T(2,128)(2,1)S(1)} %collective-permute-done.9.refs_14_.refs_2_), channel_id=1, source_target_pairs={{0,1},{1,0},{2,3},{3,2},{4,5},{5,4},{6,7},{7,6},{8,9},{9,8},{10,11... | collective-permute-start | bytes 1277960 | tf_op jit(solution)/shard_map/ppermute | solution.py:420
  42.7 12.5 %collective-permute-start.10 = (bf16[2,29,2,512]{3,2,1,0:T(2,128)(2,1)S(1)}, bf16[2,29,2,512]{3,2,1,0:T(2,128)(2,1)S(1)}, u32[]{:S(2)}, u32[]{:S(2)}) collective-permute-start(bf16[2,29,2,512]{3,2,1,0:T(2,128)(2,1)S(1)} %get-tuple-element.30), channel_id=1, source_target_pairs={{0,2},{1,5},{2,6},{3,1},{4,0},{5,9},{6,10},{7,3},{8,4},{9,13},{10,... | collective-permute-start | bytes 356360 | tf_op jit(solution)/shard_map/ppermute | solution.py:393
  44.4 10.9 %collective-permute-start.11 = (bf16[2,29,2,512]{3,2,1,0:T(2,128)(2,1)S(1)}, bf16[2,29,2,512]{3,2,1,0:T(2,128)(2,1)S(1)}, u32[]{:S(2)}, u32[]{:S(2)}) collective-permute-start(bf16[2,29,2,512]{3,2,1,0:T(2,128)(2,1)S(1)} %get-tuple-element.31), channel_id=1, source_target_pairs={{0,4},{1,3},{2,0},{3,7},{4,8},{5,1},{6,2},{7,11},{8,12},{9,5},{10,... | collective-permute-start | bytes 356360 | tf_op jit(solution)/shard_map/ppermute | solution.py:396
  44.7 15.3 %collective-permute-start.12 = (bf16[2,29,2,512]{3,2,1,0:T(2,128)(2,1)S(1)}, bf16[2,29,2,512]{3,2,1,0:T(2,128)(2,1)S(1)}, u32[]{:S(2)}, u32[]{:S(2)}) collective-permute-start(bf16[2,29,2,512]{3,2,1,0:T(2,128)(2,1)S(1)} %get-tuple-element.32), channel_id=1, source_target_pairs={{0,6},{1,9},{2,10},{3,5},{4,2},{5,13},{6,14},{7,1},{8,0},{9,15},{1... | collective-permute-start | bytes 356360 | tf_op jit(solution)/shard_map/ppermute | solution.py:393
  47.4 12.6 %collective-permute-start.13 = (bf16[2,29,2,512]{3,2,1,0:T(2,128)(2,1)S(1)}, bf16[2,29,2,512]{3,2,1,0:T(2,128)(2,1)S(1)}, u32[]{:S(2)}, u32[]{:S(2)}) collective-permute-start(bf16[2,29,2,512]{3,2,1,0:T(2,128)(2,1)S(1)} %get-tuple-element.33), channel_id=1, source_target_pairs={{0,8},{1,7},{2,4},{3,11},{4,12},{5,3},{6,0},{7,15},{8,14},{9,1},{1... | collective-permute-start | bytes 356360 | tf_op jit(solution)/shard_map/ppermute | solution.py:396
  51.4 9.1 %collective-permute-start.20 = (bf16[2,29,2,512]{3,2,1,0:T(2,128)(2,1)S(1)}, bf16[2,29,2,512]{3,2,1,0:T(2,128)(2,1)S(1)}, u32[]{:S(2)}, u32[]{:S(2)}) collective-permute-start(bf16[2,29,2,512]{3,2,1,0:T(2,128)(2,1)S(1)} %get-tuple-element.34.refs_5_.refs_3_), channel_id=1, source_target_pairs={{0,10},{1,13},{2,14},{3,9},{4,6},{5,15},{6,12},{7,5},{8,2},{9,11},... | collective-permute-start | bytes 356360 | tf_op jit(solution)/shard_map/ppermute | solution.py:393
  55.2 11.8 %collective-permute-start.21 = (bf16[2,29,2,512]{3,2,1,0:T(2,128)(2,1)S(1)}, bf16[2,29,2,512]{3,2,1,0:T(2,128)(2,1)S(1)}, u32[]{:S(2)}, u32[]{:S(2)}) collective-permute-start(bf16[2,29,2,512]{3,2,1,0:T(2,128)(2,1)S(1)} %get-tuple-element.35), channel_id=1, source_target_pairs={{0,12},{1,11},{2,8},{3,15},{4,14},{5,7},{6,4},{7,13},{8,10},{9,3},... | collective-permute-start | bytes 356360 | tf_op jit(solution)/shard_map/ppermute | solution.py:396
  55.3 11.7 %collective-permute-start.22 = (bf16[2,29,2,512]{3,2,1,0:T(2,128)(2,1)S(1)}, bf16[2,29,2,512]{3,2,1,0:T(2,128)(2,1)S(1)}, u32[]{:S(2)}, u32[]{:S(2)}) collective-permute-start(bf16[2,29,2,512]{3,2,1,0:T(2,128)(2,1)S(1)} %get-tuple-element.36), channel_id=1, source_target_pairs={{0,14},{1,15},{2,12},{3,13},{4,10},{5,11},{6,8},{7,9},{8,6},{9,7},... | collective-permute-start | bytes 356360 | tf_op jit(solution)/shard_map/ppermute | solution.py:393
  60.4 8.3 %collective-permute-start.19 = (bf16[5,29,2,512]{3,2,1,0:T(2,128)(2,1)S(1)}, bf16[5,29,2,512]{3,2,1,0:T(2,128)(2,1)S(1)}, u32[]{:S(2)}, u32[]{:S(2)}) collective-permute-start(bf16[5,29,2,512]{3,2,1,0:T(2,128)(2,1)S(1)} %others.2), channel_id=1, source_target_pairs={{0,1},{1,0},{2,3},{3,2},{4,5},{5,4},{6,7},{7,6},{8,9},{9,8},{10,11... | collective-permute-start | bytes 890888 | tf_op jit(solution)/shard_map/ppermute | solution.py:430
  67.2 1.5 %collective-permute-start.23 = (bf16[3,29,2,512]{3,2,1,0:T(2,128)(2,1)S(1)}, bf16[3,29,2,512]{3,2,1,0:T(2,128)(2,1)S(1)}, u32[]{:S(2)}, u32[]{:S(2)}) collective-permute-start(bf16[3,29,2,512]{3,2,1,0:T(2,128)(2,1)S(1)} %others.3), channel_id=1, source_target_pairs={{0,1},{1,0},{2,3},{3,2},{4,5},{5,4},{6,7},{7,6},{8,9},{9,8},{10,11... | collective-permute-start | bytes 534536 | tf_op jit(solution)/shard_map/ppermute | solution.py:430
  (2 other events, 1.7 us)

commit v5 on v4

--- a/solution.py
+++ b/solution.py
@@ -351,12 +351,15 @@
     chips = owner_count // 2
     last = chips // 2
     split = [list(range(at - 1, at + 1)) for at in range(last, 2, -2)][::-1]
-    split = [list(range(split[0][0] if split else last + 1))] + split
-    order, at = [], 0
+    split = [list(range(1, split[0][0] if split else last + 1))] + split
+    order, at = [], 2
     for hops in split:
-        came = sum(2 if 0 < 2 * hop < chips else 1 for hop in hops)
-        order += [at + 2 * i for i in range(came)] + [at + 2 * i + 1 for i in range(came)]
+        came = sum(2 if 2 * hop < chips else 1 for hop in hops)
+        firsts, seconds = ([at + 2 * i + core for i in range(came)] for core in range(2))
         at += 2 * came
+        if hops is split[-1]:
+            firsts, seconds = firsts + [0], seconds + [1]
+        order += firsts + seconds
     piece_from = [piece_from[i] for i in order]
 
     base_weight, down, up = (
@@ -368,7 +371,7 @@
     held = [None] * 4
     received = []
 
-    def products(hops, start, before):
+    def products(hops, start, before, joined=False):
         blocks, places, result = [], [], 0
         for hop in hops:
             blocks += groups[hop]
@@ -395,10 +398,13 @@
             if len(groups[hop]) == 4:
                 came.append(send(out[at], perm=turned(hop)))
                 at += 1
-        received.append(came)
+        if joined:
+            received[-1] += came
+        else:
+            received.append(came)
         return len(blocks), out[0]
 
-    done = 0
+    done = 2
     for hops in range(1, last + 1):
         first = send(first, perm=turned(1))
         if hops == 1:
@@ -425,6 +431,7 @@
         if held[i] is None:
             held[i], row_place = hold(weight, row_place, [], **how)
     _, made = products(split[-1], done, [])
+    products([0], 0, [made], joined=True)
     arrays = []
     for came in received:
         passed = send(others(came, [made]), perm=swap)

time: 70.3 us -> 69.2 us (0.984)
  waiting for transfers between devices: 15.9 us -> 13.1 us
  Pallas kernels: 21.6 us -> 23.3 us
    ppermute x3, waiting for transfers between devices: 6.48 us -> 3.54 us  [products(): came.append(send(out[at], perm=turned(hop)))]
    pallas_call x2 -> x3, Pallas kernels: 9.42 us -> 11 us  [block_products(): pl.pallas_call(kernel, out_shape=[jax.ShapeDtypeStruct((2, pairs + owner_...]
  transfers between devices with their start and end apart: 24 -> 24, of which waited for: 7 -> 8; matrix products, arithmetic and copies ran while one was open for 1% -> 1% of each run, Pallas kernels for 29% -> 32%
where the time goes in v5:
time: 69.2 us; the launch traced here: 69 us
  starting transfers between devices  29.9 us (43%)
  Pallas kernels  23.3 us (34%)
  waiting for transfers between devices  13.1 us (19%)
  local copies, waits for them, and re-layouts  2.47 us (4%)
    ppermute x4, starting transfers between devices, products(): came.append(send(out[at], perm=turned(-hop)) if hop else out[at])  12.7 us
    pallas_call x3, Pallas kernels, block_products(): pl.pallas_call(kernel, out_shape=[jax.ShapeDtypeStruct((2, pairs + owner_...  11 us
    pallas_call x4, Pallas kernels, hold(): pl.pallas_call(kernel, out_shape=[pltpu.VMEM(shape, weight.dtype), jax.Sh...  9.29 us
    ppermute x4, starting transfers between devices, per_device(): first = send(first, perm=turned(1))  8.97 us
    ppermute x3, starting transfers between devices, per_device(): second = send(second, perm=turned(1))  5.66 us
    ppermute x4, waiting for transfers between devices, per_device(): first = send(first, perm=turned(1))  4.67 us
    ppermute x3, waiting for transfers between devices, products(): came.append(send(out[at], perm=turned(hop)))  3.54 us
    ppermute x3, waiting for transfers between devices, per_device(): second = send(second, perm=turned(1))  3.42 us
  transfers between devices with their start and end apart: 24, of which 8 were waited for; matrix products, arithmetic and copies ran while one was open for 1% of the time, Pallas kernels for 32%

profile of v5, /device:TPU:0, one launch (start us, length us, event | category | flops | bytes accessed | tf_op | source)
XLA Modules:
  0.0 69.0 jit_solution(17836541316457239359)
XLA Ops:
  1.6 2.6 %collective-permute-start = (bf16[13,2,8192]{2,1,0:T(2,128)(2,1)S(1)}, bf16[13,2,8192]{2,1,0:T(2,128)(2,1)S(1)}, u32[]{:S(2)}, u32[]{:S(2)}) collective-permute-start(bf16[13,2,8192]{2,1,0:T(2,128)(2,1)S(1)} %pair_rows.1.refs_0_), channel_id=1, source_target_pairs={{0,4},{1,3},{2,0},{3,7},{4,8},{5,1},{6,2},{7,11},{8,12},{9,5},{10,... | collective-permute-start | bytes 1277960 | tf_op jit(solution)/shard_map/ppermute | solution.py:409
  4.3 1.7 %collective-permute-start.3 = (bf16[13,2,8192]{2,1,0:T(2,128)(2,1)S(1)}, bf16[13,2,8192]{2,1,0:T(2,128)(2,1)S(1)}, u32[]{:S(2)}, u32[]{:S(2)}) collective-permute-start(bf16[13,2,8192]{2,1,0:T(2,128)(2,1)S(1)} %collective-permute-done.2.refs_1_), channel_id=1, source_target_pairs={{0,4},{1,3},{2,0},{3,7},{4,8},{5,1},{6,2},{7,11},{8,12},{9,5},{10,... | collective-permute-start | bytes 1277960 | tf_op jit(solution)/shard_map/ppermute | solution.py:421
  8.2 2.1 %collective-permute-done.refs_1_ = bf16[13,2,8192]{2,1,0:T(2,128)(2,1)S(1)} collective-permute-done((bf16[13,2,8192]{2,1,0:T(2,128)(2,1)S(1)}, bf16[13,2,8192]{2,1,0:T(2,128)(2,1)S(1)}, u32[]{:S(2)}, u32[]{:S(2)}) %collective-permute-start) | collective-permute-done | bytes 426016 | tf_op jit(solution)/shard_map/ppermute | solution.py:409
  10.3 2.2 %hold.4 = (bf16[4096,512]{1,0:T(8,128)(2,1)S(1)}, bf16[13,2,8192]{2,1,0:T(2,128)(2,1)S(1)}) custom-call(bf16[8192,512]{1,0:T(8,128)(2,1)} %refs_0_.3, bf16[13,2,8192]{2,1,0:T(2,128)(2,1)S(1)} %collective-permute-done.refs_1_, s32[16,26]{1,0:T(8,128)S(1)} %row_places.1.refs_2_.place_ref), custom_call_target="tpu_custom_call", output_to_operand_aliasing={{1}: (1, {})} | custom-call | tf_op jit(solution)/shard_map/hold/pallas_call | solution.py:129
  12.5 2.1 %collective-permute-start.5 = (bf16[13,2,8192]{2,1,0:T(2,128)(2,1)S(1)}, bf16[13,2,8192]{2,1,0:T(2,128)(2,1)S(1)}, u32[]{:S(2)}, u32[]{:S(2)}) collective-permute-start(bf16[13,2,8192]{2,1,0:T(2,128)(2,1)S(1)} %get-tuple-element.20.refs_0_), channel_id=1, source_target_pairs={{0,4},{1,3},{2,0},{3,7},{4,8},{5,1},{6,2},{7,11},{8,12},{9,5},{10,... | collective-permute-start | bytes 1277960 | tf_op jit(solution)/shard_map/ppermute | solution.py:409
  14.9 2.2 %hold.5 = (bf16[4096,512]{1,0:T(8,128)(2,1)S(1)}, bf16[13,2,8192]{2,1,0:T(2,128)(2,1)S(1)}) custom-call(bf16[8192,512]{1,0:T(8,128)(2,1)} %refs_0_.3, bf16[13,2,8192]{2,1,0:T(2,128)(2,1)S(1)} %collective-permute-done.3.refs_1_), custom_call_target="tpu_custom_call", output_to_operand_aliasing={{1}: (1, {})} | custom-call | tf_op jit(solution)/shard_map/hold/pallas_call | solution.py:129
  17.1 2.1 %collective-permute-start.7 = (bf16[13,2,8192]{2,1,0:T(2,128)(2,1)S(1)}, bf16[13,2,8192]{2,1,0:T(2,128)(2,1)S(1)}, u32[]{:S(2)}, u32[]{:S(2)}) collective-permute-start(bf16[13,2,8192]{2,1,0:T(2,128)(2,1)S(1)} %get-tuple-element.21.refs_2_), channel_id=1, source_target_pairs={{0,4},{1,3},{2,0},{3,7},{4,8},{5,1},{6,2},{7,11},{8,12},{9,5},{10,... | collective-permute-start | bytes 1277960 | tf_op jit(solution)/shard_map/ppermute | solution.py:421
  19.2 1.5 %collective-permute-done.5.refs_1_ = bf16[13,2,8192]{2,1,0:T(2,128)(2,1)S(1)} collective-permute-done((bf16[13,2,8192]{2,1,0:T(2,128)(2,1)S(1)}, bf16[13,2,8192]{2,1,0:T(2,128)(2,1)S(1)}, u32[]{:S(2)}, u32[]{:S(2)}) %collective-permute-start.5) | collective-permute-done | bytes 426016 | tf_op jit(solution)/shard_map/ppermute | solution.py:409
  20.7 2.2 %hold.6 = (bf16[256,8192]{1,0:T(8,128)(2,1)S(1)}, bf16[13,2,8192]{2,1,0:T(2,128)(2,1)S(1)}) custom-call(bf16[256,8192]{1,0:T(8,128)(2,1)} %bitcast.7, bf16[13,2,8192]{2,1,0:T(2,128)(2,1)S(1)} %collective-permute-done.5.refs_1_), custom_call_target="tpu_custom_call", output_to_operand_aliasing={{1}: (1, {})} | custom-call | tf_op jit(solution)/shard_map/hold/pallas_call | solution.py:129
  22.9 2.1 %collective-permute-start.14 = (bf16[13,2,8192]{2,1,0:T(2,128)(2,1)S(1)}, bf16[13,2,8192]{2,1,0:T(2,128)(2,1)S(1)}, u32[]{:S(2)}, u32[]{:S(2)}) collective-permute-start(bf16[13,2,8192]{2,1,0:T(2,128)(2,1)S(1)} %get-tuple-element.22.refs_4_), channel_id=1, source_target_pairs={{0,4},{1,3},{2,0},{3,7},{4,8},{5,1},{6,2},{7,11},{8,12},{9,5},{10,... | collective-permute-start | bytes 1277960 | tf_op jit(solution)/shard_map/ppermute | solution.py:409
  25.6 2.6 %hold.7 = (bf16[8192,256]{1,0:T(8,128)(2,1)S(1)}, bf16[13,2,8192]{2,1,0:T(2,128)(2,1)S(1)}) custom-call(bf16[256,8192]{1,0:T(8,128)(2,1)} %bitcast.8, bf16[13,2,8192]{2,1,0:T(2,128)(2,1)S(1)} %collective-permute-done.7.refs_1_), custom_call_target="tpu_custom_call", output_to_operand_aliasing={{1}: (1, {})} | custom-call | tf_op jit(solution)/shard_map/hold/pallas_call | solution.py:129
  28.2 1.8 %collective-permute-start.9 = (bf16[13,2,8192]{2,1,0:T(2,128)(2,1)S(1)}, bf16[13,2,8192]{2,1,0:T(2,128)(2,1)S(1)}, u32[]{:S(2)}, u32[]{:S(2)}) collective-permute-start(bf16[13,2,8192]{2,1,0:T(2,128)(2,1)S(1)} %get-tuple-element.23.refs_6_), channel_id=1, source_target_pairs={{0,4},{1,3},{2,0},{3,7},{4,8},{5,1},{6,2},{7,11},{8,12},{9,5},{10,... | collective-permute-start | bytes 1277960 | tf_op jit(solution)/shard_map/ppermute | solution.py:421
  31.1 2.1 %collective-permute-start.17 = (bf16[13,2,8192]{2,1,0:T(2,128)(2,1)S(1)}, bf16[13,2,8192]{2,1,0:T(2,128)(2,1)S(1)}, u32[]{:S(2)}, u32[]{:S(2)}) collective-permute-start(bf16[13,2,8192]{2,1,0:T(2,128)(2,1)S(1)} %collective-permute-done.14.refs_0_), channel_id=1, source_target_pairs={{0,4},{1,3},{2,0},{3,7},{4,8},{5,1},{6,2},{7,11},{8,12},{9,5},{10,... | collective-permute-start | bytes 1277960 | tf_op jit(solution)/shard_map/ppermute | solution.py:409
  33.2 3.2 %collective-permute-done.9.refs_12_.refs_2_ = bf16[13,2,8192]{2,1,0:T(2,128)(2,1)S(1)} collective-permute-done((bf16[13,2,8192]{2,1,0:T(2,128)(2,1)S(1)}, bf16[13,2,8192]{2,1,0:T(2,128)(2,1)S(1)}, u32[]{:S(2)}, u32[]{:S(2)}) %collective-permute-start.9) | collective-permute-done | bytes 426016 | tf_op jit(solution)/shard_map/ppermute | solution.py:421
  36.4 4.5 %block_products.3 = (bf16[2,29,2,512]{3,2,1,0:T(2,128)(2,1)S(1)}, bf16[2,29,2,512]{3,2,1,0:T(2,128)(2,1)S(1)}, bf16[2,29,2,512]{3,2,1,0:T(2,128)(2,1)S(1)}, bf16[2,29,2,512]{3,2,1,0:T(2,128)(2,1)S(1)}) custom-call(s32[16,26]{1,0:T(8,128)S(1)} %row_places.1.refs_2_.place_ref, bf16[13,2,8192]{2,1,0:T(2,128)(2,1)S(1)} %get-tuple-element.20.refs_0_, ...), custom_call_target="tpu_custom_call" | custom-call | flops 3221225472 | bytes 16777216 | tf_op jit(solution)/shard_map/block_products/pallas_call | solution.py:236
  41.5 1.7 %collective-permute-start.10 = (bf16[2,29,2,512]{3,2,1,0:T(2,128)(2,1)S(1)}, bf16[2,29,2,512]{3,2,1,0:T(2,128)(2,1)S(1)}, u32[]{:S(2)}, u32[]{:S(2)}) collective-permute-start(bf16[2,29,2,512]{3,2,1,0:T(2,128)(2,1)S(1)} %get-tuple-element.28.refs_1_), channel_id=1, source_target_pairs={{0,2},{1,5},{2,6},{3,1},{4,0},{5,9},{6,10},{7,3},{8,4},{9,13},{10,... | collective-permute-start | bytes 356360 | tf_op jit(solution)/shard_map/ppermute | solution.py:396
  43.5 2.7 %collective-permute-start.12 = (bf16[2,29,2,512]{3,2,1,0:T(2,128)(2,1)S(1)}, bf16[2,29,2,512]{3,2,1,0:T(2,128)(2,1)S(1)}, u32[]{:S(2)}, u32[]{:S(2)}) collective-permute-start(bf16[2,29,2,512]{3,2,1,0:T(2,128)(2,1)S(1)} %get-tuple-element.30), channel_id=1, source_target_pairs={{0,6},{1,9},{2,10},{3,5},{4,2},{5,13},{6,14},{7,1},{8,0},{9,15},{1... | collective-permute-start | bytes 356360 | tf_op jit(solution)/shard_map/ppermute | solution.py:396
  46.5 3.5 %block_products.4 = (bf16[2,29,2,512]{3,2,1,0:T(2,128)(2,1)S(1)}, bf16[2,29,2,512]{3,2,1,0:T(2,128)(2,1)S(1)}, bf16[2,29,2,512]{3,2,1,0:T(2,128)(2,1)S(1)}) custom-call(s32[16,26]{1,0:T(8,128)S(1)} %row_places.1.refs_2_.place_ref, bf16[13,2,8192]{2,1,0:T(2,128)(2,1)S(1)} %collective-permute-done.14.refs_0_, ...), custom_call_target="tpu_custom_call" | custom-call | flops 2415919104 | bytes 16777216 | tf_op jit(solution)/shard_map/block_products/pallas_call | solution.py:236
  50.0 3.8 %collective-permute-start.20 = (bf16[2,29,2,512]{3,2,1,0:T(2,128)(2,1)S(1)}, bf16[2,29,2,512]{3,2,1,0:T(2,128)(2,1)S(1)}, u32[]{:S(2)}, u32[]{:S(2)}) collective-permute-start(bf16[2,29,2,512]{3,2,1,0:T(2,128)(2,1)S(1)} %get-tuple-element.32.refs_4_.refs_6_), channel_id=1, source_target_pairs={{0,10},{1,13},{2,14},{3,9},{4,6},{5,15},{6,12},{7,5},{8,2},{9,11},... | collective-permute-start | bytes 356360 | tf_op jit(solution)/shard_map/ppermute | solution.py:396
  54.0 4.5 %collective-permute-start.22 = (bf16[2,29,2,512]{3,2,1,0:T(2,128)(2,1)S(1)}, bf16[2,29,2,512]{3,2,1,0:T(2,128)(2,1)S(1)}, u32[]{:S(2)}, u32[]{:S(2)}) collective-permute-start(bf16[2,29,2,512]{3,2,1,0:T(2,128)(2,1)S(1)} %get-tuple-element.34), channel_id=1, source_target_pairs={{0,14},{1,15},{2,12},{3,13},{4,10},{5,11},{6,8},{7,9},{8,6},{9,7},... | collective-permute-start | bytes 356360 | tf_op jit(solution)/shard_map/ppermute | solution.py:396
  59.0 3.0 %block_products.5.refs_3_.refs_8_ = bf16[2,29,2,512]{3,2,1,0:T(2,128)(2,1)S(1)} custom-call(s32[16,26]{1,0:T(8,128)S(1)} %row_places.1.refs_2_.place_ref, bf16[13,2,8192]{2,1,0:T(2,128)(2,1)S(1)} %pair_rows.1.refs_0_, bf16[13,2,8192]{2,1,0:T(2,128)(2,1)S(1)} %collective-permute-done.2.refs_1_, ...), custom_call_target="tpu_custom_call" | custom-call | flops 805306368 | bytes 16777216 | tf_op jit(solution)/shard_map/block_products/pallas_call | solution.py:236
  62.0 3.5 %collective-permute-done.21.refs_1_.refs_6_ = bf16[2,29,2,512]{3,2,1,0:T(2,128)(2,1)S(1)} collective-permute-done((bf16[2,29,2,512]{3,2,1,0:T(2,128)(2,1)S(1)}, bf16[2,29,2,512]{3,2,1,0:T(2,128)(2,1)S(1)}, u32[]{:S(2)}, u32[]{:S(2)}) %collective-permute-start.21) | collective-permute-done | bytes 118816 | tf_op jit(solution)/shard_map/ppermute | solution.py:399
  66.0 1.5 %collective-permute-done.23.refs_9_ = bf16[4,29,2,512]{3,2,1,0:T(2,128)(2,1)S(1)} collective-permute-done((bf16[4,29,2,512]{3,2,1,0:T(2,128)(2,1)S(1)}, bf16[4,29,2,512]{3,2,1,0:T(2,128)(2,1)S(1)}, u32[]{:S(2)}, u32[]{:S(2)}) %collective-permute-start.23) | collective-permute-done | bytes 237600 | tf_op jit(solution)/shard_map/ppermute | solution.py:437
  67.5 1.4 %assemble.1 = bf16[26,8192]{1,0:T(8,128)(2,1)} custom-call(s32[16,26]{1,0:T(8,128)S(1)} %row_places.1.refs_2_.place_ref, bf16[2,29,2,512]{3,2,1,0:T(2,128)(2,1)S(1)} %collective-permute-done.10.refs_0_, bf16[2,29,2,512]{3,2,1,0:T(2,128)(2,1)S(1)} %collective-permute-done.11.refs_1_, bf16[2,29,2,512]{3,2,1,0:T(2,128)(2,1)S(1)} %collective-permute-done.12.refs_2_, ...), custom_call_target="tpu_custom_call" | custom-call | tf_op jit(solution)/shard_map/assemble/pallas_call | solution.py:323
  (42 shorter events, 7.9 us)
Async XLA Ops:
  1.1 3.2 %collective-permute-start.2 = (bf16[13,2,8192]{2,1,0:T(2,128)(2,1)S(1)}, bf16[13,2,8192]{2,1,0:T(2,128)(2,1)S(1)}, u32[]{:S(2)}, u32[]{:S(2)}) collective-permute-start(bf16[13,2,8192]{2,1,0:T(2,128)(2,1)S(1)} %pair_rows.1.refs_0_), channel_id=1, source_target_pairs={{0,1},{1,0},{2,3},{3,2},{4,5},{5,4},{6,7},{7,6},{8,9},{9,8},{10,11... | collective-permute-start | bytes 1277960 | tf_op jit(solution)/shard_map/ppermute | solution.py:369
  1.6 8.7 %collective-permute-start = (bf16[13,2,8192]{2,1,0:T(2,128)(2,1)S(1)}, bf16[13,2,8192]{2,1,0:T(2,128)(2,1)S(1)}, u32[]{:S(2)}, u32[]{:S(2)}) collective-permute-start(bf16[13,2,8192]{2,1,0:T(2,128)(2,1)S(1)} %pair_rows.1.refs_0_), channel_id=1, source_target_pairs={{0,4},{1,3},{2,0},{3,7},{4,8},{5,1},{6,2},{7,11},{8,12},{9,5},{10,... | collective-permute-start | bytes 1277960 | tf_op jit(solution)/shard_map/ppermute | solution.py:409
  4.3 10.6 %collective-permute-start.3 = (bf16[13,2,8192]{2,1,0:T(2,128)(2,1)S(1)}, bf16[13,2,8192]{2,1,0:T(2,128)(2,1)S(1)}, u32[]{:S(2)}, u32[]{:S(2)}) collective-permute-start(bf16[13,2,8192]{2,1,0:T(2,128)(2,1)S(1)} %collective-permute-done.2.refs_1_), channel_id=1, source_target_pairs={{0,4},{1,3},{2,0},{3,7},{4,8},{5,1},{6,2},{7,11},{8,12},{9,5},{10,... | collective-permute-start | bytes 1277960 | tf_op jit(solution)/shard_map/ppermute | solution.py:421
  12.5 8.2 %collective-permute-start.5 = (bf16[13,2,8192]{2,1,0:T(2,128)(2,1)S(1)}, bf16[13,2,8192]{2,1,0:T(2,128)(2,1)S(1)}, u32[]{:S(2)}, u32[]{:S(2)}) collective-permute-start(bf16[13,2,8192]{2,1,0:T(2,128)(2,1)S(1)} %get-tuple-element.20.refs_0_), channel_id=1, source_target_pairs={{0,4},{1,3},{2,0},{3,7},{4,8},{5,1},{6,2},{7,11},{8,12},{9,5},{10,... | collective-permute-start | bytes 1277960 | tf_op jit(solution)/shard_map/ppermute | solution.py:409
  17.1 8.5 %collective-permute-start.7 = (bf16[13,2,8192]{2,1,0:T(2,128)(2,1)S(1)}, bf16[13,2,8192]{2,1,0:T(2,128)(2,1)S(1)}, u32[]{:S(2)}, u32[]{:S(2)}) collective-permute-start(bf16[13,2,8192]{2,1,0:T(2,128)(2,1)S(1)} %get-tuple-element.21.refs_2_), channel_id=1, source_target_pairs={{0,4},{1,3},{2,0},{3,7},{4,8},{5,1},{6,2},{7,11},{8,12},{9,5},{10,... | collective-permute-start | bytes 1277960 | tf_op jit(solution)/shard_map/ppermute | solution.py:421
  19.2 10.8 %collective-permute-start.1 = (bf16[13,2,8192]{2,1,0:T(2,128)(2,1)S(1)}, bf16[13,2,8192]{2,1,0:T(2,128)(2,1)S(1)}, u32[]{:S(2)}, u32[]{:S(2)}) collective-permute-start(bf16[13,2,8192]{2,1,0:T(2,128)(2,1)S(1)} %get-tuple-element.20.refs_0_), channel_id=1, source_target_pairs={{0,1},{1,0},{2,3},{3,2},{4,5},{5,4},{6,7},{7,6},{8,9},{9,8},{10,11... | collective-permute-start | bytes 1277960 | tf_op jit(solution)/shard_map/ppermute | solution.py:419
  22.9 8.2 %collective-permute-start.14 = (bf16[13,2,8192]{2,1,0:T(2,128)(2,1)S(1)}, bf16[13,2,8192]{2,1,0:T(2,128)(2,1)S(1)}, u32[]{:S(2)}, u32[]{:S(2)}) collective-permute-start(bf16[13,2,8192]{2,1,0:T(2,128)(2,1)S(1)} %get-tuple-element.22.refs_4_), channel_id=1, source_target_pairs={{0,4},{1,3},{2,0},{3,7},{4,8},{5,1},{6,2},{7,11},{8,12},{9,5},{10,... | collective-permute-start | bytes 1277960 | tf_op jit(solution)/shard_map/ppermute | solution.py:409
  25.1 8.1 %collective-permute-start.6 = (bf16[13,2,8192]{2,1,0:T(2,128)(2,1)S(1)}, bf16[13,2,8192]{2,1,0:T(2,128)(2,1)S(1)}, u32[]{:S(2)}, u32[]{:S(2)}) collective-permute-start(bf16[13,2,8192]{2,1,0:T(2,128)(2,1)S(1)} %get-tuple-element.22.refs_4_), channel_id=1, source_target_pairs={{0,1},{1,0},{2,3},{3,2},{4,5},{5,4},{6,7},{7,6},{8,9},{9,8},{10,11... | collective-permute-start | bytes 1277960 | tf_op jit(solution)/shard_map/ppermute | solution.py:419
  25.1 8.1 %collective-permute-start.4 = (bf16[13,2,8192]{2,1,0:T(2,128)(2,1)S(1)}, bf16[13,2,8192]{2,1,0:T(2,128)(2,1)S(1)}, u32[]{:S(2)}, u32[]{:S(2)}) collective-permute-start(bf16[13,2,8192]{2,1,0:T(2,128)(2,1)S(1)} %get-tuple-element.21.refs_2_), channel_id=1, source_target_pairs={{0,1},{1,0},{2,3},{3,2},{4,5},{5,4},{6,7},{7,6},{8,9},{9,8},{10,11... | collective-permute-start | bytes 1277960 | tf_op jit(solution)/shard_map/ppermute | solution.py:426
  28.2 8.2 %collective-permute-start.9 = (bf16[13,2,8192]{2,1,0:T(2,128)(2,1)S(1)}, bf16[13,2,8192]{2,1,0:T(2,128)(2,1)S(1)}, u32[]{:S(2)}, u32[]{:S(2)}) collective-permute-start(bf16[13,2,8192]{2,1,0:T(2,128)(2,1)S(1)} %get-tuple-element.23.refs_6_), channel_id=1, source_target_pairs={{0,4},{1,3},{2,0},{3,7},{4,8},{5,1},{6,2},{7,11},{8,12},{9,5},{10,... | collective-permute-start | bytes 1277960 | tf_op jit(solution)/shard_map/ppermute | solution.py:421
  30.1 6.4 %collective-permute-start.8 = (bf16[13,2,8192]{2,1,0:T(2,128)(2,1)S(1)}, bf16[13,2,8192]{2,1,0:T(2,128)(2,1)S(1)}, u32[]{:S(2)}, u32[]{:S(2)}) collective-permute-start(bf16[13,2,8192]{2,1,0:T(2,128)(2,1)S(1)} %get-tuple-element.23.refs_6_), channel_id=1, source_target_pairs={{0,1},{1,0},{2,3},{3,2},{4,5},{5,4},{6,7},{7,6},{8,9},{9,8},{10,11... | collective-permute-start | bytes 1277960 | tf_op jit(solution)/shard_map/ppermute | solution.py:426
  31.1 9.9 %collective-permute-start.17 = (bf16[13,2,8192]{2,1,0:T(2,128)(2,1)S(1)}, bf16[13,2,8192]{2,1,0:T(2,128)(2,1)S(1)}, u32[]{:S(2)}, u32[]{:S(2)}) collective-permute-start(bf16[13,2,8192]{2,1,0:T(2,128)(2,1)S(1)} %collective-permute-done.14.refs_0_), channel_id=1, source_target_pairs={{0,4},{1,3},{2,0},{3,7},{4,8},{5,1},{6,2},{7,11},{8,12},{9,5},{10,... | collective-permute-start | bytes 1277960 | tf_op jit(solution)/shard_map/ppermute | solution.py:409
  33.2 10.3 %collective-permute-start.15 = (bf16[13,2,8192]{2,1,0:T(2,128)(2,1)S(1)}, bf16[13,2,8192]{2,1,0:T(2,128)(2,1)S(1)}, u32[]{:S(2)}, u32[]{:S(2)}) collective-permute-start(bf16[13,2,8192]{2,1,0:T(2,128)(2,1)S(1)} %collective-permute-done.14.refs_0_), channel_id=1, source_target_pairs={{0,1},{1,0},{2,3},{3,2},{4,5},{5,4},{6,7},{7,6},{8,9},{9,8},{10,11... | collective-permute-start | bytes 1277960 | tf_op jit(solution)/shard_map/ppermute | solution.py:419
  41.0 5.3 %collective-permute-start.18 = (bf16[13,2,8192]{2,1,0:T(2,128)(2,1)S(1)}, bf16[13,2,8192]{2,1,0:T(2,128)(2,1)S(1)}, u32[]{:S(2)}, u32[]{:S(2)}) collective-permute-start(bf16[13,2,8192]{2,1,0:T(2,128)(2,1)S(1)} %after.1.refs_4_), channel_id=1, source_target_pairs={{0,1},{1,0},{2,3},{3,2},{4,5},{5,4},{6,7},{7,6},{8,9},{9,8},{10,11... | collective-permute-start | bytes 1277960 | tf_op jit(solution)/shard_map/ppermute | solution.py:419
  41.0 5.5 %collective-permute-start.16 = (bf16[13,2,8192]{2,1,0:T(2,128)(2,1)S(1)}, bf16[13,2,8192]{2,1,0:T(2,128)(2,1)S(1)}, u32[]{:S(2)}, u32[]{:S(2)}) collective-permute-start(bf16[13,2,8192]{2,1,0:T(2,128)(2,1)S(1)} %collective-permute-done.9.refs_12_.refs_2_), channel_id=1, source_target_pairs={{0,1},{1,0},{2,3},{3,2},{4,5},{5,4},{6,7},{7,6},{8,9},{9,8},{10,11... | collective-permute-start | bytes 1277960 | tf_op jit(solution)/shard_map/ppermute | solution.py:426
  41.5 12.2 %collective-permute-start.10 = (bf16[2,29,2,512]{3,2,1,0:T(2,128)(2,1)S(1)}, bf16[2,29,2,512]{3,2,1,0:T(2,128)(2,1)S(1)}, u32[]{:S(2)}, u32[]{:S(2)}) collective-permute-start(bf16[2,29,2,512]{3,2,1,0:T(2,128)(2,1)S(1)} %get-tuple-element.28.refs_1_), channel_id=1, source_target_pairs={{0,2},{1,5},{2,6},{3,1},{4,0},{5,9},{6,10},{7,3},{8,4},{9,13},{10,... | collective-permute-start | bytes 356360 | tf_op jit(solution)/shard_map/ppermute | solution.py:396
  43.2 10.8 %collective-permute-start.11 = (bf16[2,29,2,512]{3,2,1,0:T(2,128)(2,1)S(1)}, bf16[2,29,2,512]{3,2,1,0:T(2,128)(2,1)S(1)}, u32[]{:S(2)}, u32[]{:S(2)}) collective-permute-start(bf16[2,29,2,512]{3,2,1,0:T(2,128)(2,1)S(1)} %get-tuple-element.29), channel_id=1, source_target_pairs={{0,4},{1,3},{2,0},{3,7},{4,8},{5,1},{6,2},{7,11},{8,12},{9,5},{10,... | collective-permute-start | bytes 356360 | tf_op jit(solution)/shard_map/ppermute | solution.py:399
  43.5 15.0 %collective-permute-start.12 = (bf16[2,29,2,512]{3,2,1,0:T(2,128)(2,1)S(1)}, bf16[2,29,2,512]{3,2,1,0:T(2,128)(2,1)S(1)}, u32[]{:S(2)}, u32[]{:S(2)}) collective-permute-start(bf16[2,29,2,512]{3,2,1,0:T(2,128)(2,1)S(1)} %get-tuple-element.30), channel_id=1, source_target_pairs={{0,6},{1,9},{2,10},{3,5},{4,2},{5,13},{6,14},{7,1},{8,0},{9,15},{1... | collective-permute-start | bytes 356360 | tf_op jit(solution)/shard_map/ppermute | solution.py:396
  46.3 12.3 %collective-permute-start.13 = (bf16[2,29,2,512]{3,2,1,0:T(2,128)(2,1)S(1)}, bf16[2,29,2,512]{3,2,1,0:T(2,128)(2,1)S(1)}, u32[]{:S(2)}, u32[]{:S(2)}) collective-permute-start(bf16[2,29,2,512]{3,2,1,0:T(2,128)(2,1)S(1)} %get-tuple-element.31), channel_id=1, source_target_pairs={{0,8},{1,7},{2,4},{3,11},{4,12},{5,3},{6,0},{7,15},{8,14},{9,1},{1... | collective-permute-start | bytes 356360 | tf_op jit(solution)/shard_map/ppermute | solution.py:399
  50.0 12.1 %collective-permute-start.20 = (bf16[2,29,2,512]{3,2,1,0:T(2,128)(2,1)S(1)}, bf16[2,29,2,512]{3,2,1,0:T(2,128)(2,1)S(1)}, u32[]{:S(2)}, u32[]{:S(2)}) collective-permute-start(bf16[2,29,2,512]{3,2,1,0:T(2,128)(2,1)S(1)} %get-tuple-element.32.refs_4_.refs_6_), channel_id=1, source_target_pairs={{0,10},{1,13},{2,14},{3,9},{4,6},{5,15},{6,12},{7,5},{8,2},{9,11},... | collective-permute-start | bytes 356360 | tf_op jit(solution)/shard_map/ppermute | solution.py:396
  53.7 11.8 %collective-permute-start.21 = (bf16[2,29,2,512]{3,2,1,0:T(2,128)(2,1)S(1)}, bf16[2,29,2,512]{3,2,1,0:T(2,128)(2,1)S(1)}, u32[]{:S(2)}, u32[]{:S(2)}) collective-permute-start(bf16[2,29,2,512]{3,2,1,0:T(2,128)(2,1)S(1)} %get-tuple-element.33), channel_id=1, source_target_pairs={{0,12},{1,11},{2,8},{3,15},{4,14},{5,7},{6,4},{7,13},{8,10},{9,3},... | collective-permute-start | bytes 356360 | tf_op jit(solution)/shard_map/ppermute | solution.py:399
  54.0 11.5 %collective-permute-start.22 = (bf16[2,29,2,512]{3,2,1,0:T(2,128)(2,1)S(1)}, bf16[2,29,2,512]{3,2,1,0:T(2,128)(2,1)S(1)}, u32[]{:S(2)}, u32[]{:S(2)}) collective-permute-start(bf16[2,29,2,512]{3,2,1,0:T(2,128)(2,1)S(1)} %get-tuple-element.34), channel_id=1, source_target_pairs={{0,14},{1,15},{2,12},{3,13},{4,10},{5,11},{6,8},{7,9},{8,6},{9,7},... | collective-permute-start | bytes 356360 | tf_op jit(solution)/shard_map/ppermute | solution.py:396
  58.9 7.1 %collective-permute-start.19 = (bf16[4,29,2,512]{3,2,1,0:T(2,128)(2,1)S(1)}, bf16[4,29,2,512]{3,2,1,0:T(2,128)(2,1)S(1)}, u32[]{:S(2)}, u32[]{:S(2)}) collective-permute-start(bf16[4,29,2,512]{3,2,1,0:T(2,128)(2,1)S(1)} %others.2), channel_id=1, source_target_pairs={{0,1},{1,0},{2,3},{3,2},{4,5},{5,4},{6,7},{7,6},{8,9},{9,8},{10,11... | collective-permute-start | bytes 712712 | tf_op jit(solution)/shard_map/ppermute | solution.py:437
  65.9 1.6 %collective-permute-start.23 = (bf16[4,29,2,512]{3,2,1,0:T(2,128)(2,1)S(1)}, bf16[4,29,2,512]{3,2,1,0:T(2,128)(2,1)S(1)}, u32[]{:S(2)}, u32[]{:S(2)}) collective-permute-start(bf16[4,29,2,512]{3,2,1,0:T(2,128)(2,1)S(1)} %others.3), channel_id=1, source_target_pairs={{0,1},{1,0},{2,3},{3,2},{4,5},{5,4},{6,7},{7,6},{8,9},{9,8},{10,11... | collective-permute-start | bytes 712712 | tf_op jit(solution)/shard_map/ppermute | solution.py:437
  (2 other events, 1.7 us)
